TPU v7x, 32 devices: a whole 2x2x4 slice. The times are simulated.
32 devices in a mesh: batch: 4 (over y, x), seq: 8 (over z, core).
Axes of the slice: x: 2, y: 2, z: 4, core: 2. Of those that a mesh axis runs over, the one named last changes fastest.
Arguments:
- tokens: bfloat16 [4, 2048, 2048], P('batch', 'seq'), may hold values from -6 to 6
- prefix: bfloat16 [4, 400, 2048], P('batch', 'seq'), may hold values from -6 to 6
- seg_lengths: int32 [4, 2], P('batch'), may hold values from 0 to 2048, as said below
- attn_gain: bfloat16 [2048], P(('batch', 'seq')), may hold values from 0.5 to 1.5
- attn_shift: bfloat16 [2048], P(('batch', 'seq')), may hold values from -0.125 to 0.125
- query_weight: bfloat16 [2048, 2048], P(('batch', 'seq')), may hold values from -0.125 to 0.125
- key_weight: bfloat16 [2048, 2048], P(('batch', 'seq')), may hold values from -0.125 to 0.125
- value_weight: bfloat16 [2048, 2048], P(('batch', 'seq')), may hold values from -0.125 to 0.125
- query_bias: bfloat16 [2048], P(('batch', 'seq')), may hold values from -1.75 to 1.75
- value_bias: bfloat16 [2048], P(('batch', 'seq')), may hold values from -0.125 to 0.125
- output_weight: bfloat16 [2048, 2048], P(('batch', 'seq')), may hold values from -3 to 3
- output_bias: bfloat16 [2048], P(('batch', 'seq')), may hold values from -1.75 to 1.75
- mlp_gain: bfloat16 [2048], P(('batch', 'seq')), may hold values from 0.5 to 1.5
- mlp_shift: bfloat16 [2048], P(('batch', 'seq')), may hold values from -1.75 to 1.75
- up_weight: bfloat16 [2048, 8192], P(('batch', 'seq')), may hold values from -0.125 to 0.125
- up_bias: bfloat16 [8192], P(('batch', 'seq')), may hold values from -1.75 to 1.75
- down_weight: bfloat16 [8192, 2048], P(('batch', 'seq')), may hold values from -0.0625 to 0.0625
- down_bias: bfloat16 [2048], P(('batch', 'seq')), may hold values from -1.75 to 1.75
- cot_tokens: bfloat16 [4, 2048, 2048], P('batch', 'seq'), may hold values from -6 to 6
- cot_prefix: bfloat16 [4, 400, 2048], P('batch', 'seq'), may hold values from -6 to 6
Outputs:
- out_tokens: bfloat16 [4, 2048, 2048], P('batch', 'seq')
- out_prefix: bfloat16 [4, 400, 2048], P('batch', 'seq')
- grad_tokens: float32 [4, 2048, 2048], P('batch', 'seq')
- grad_prefix: float32 [4, 400, 2048], P('batch', 'seq')
- grad_attn_gain: float32 [2048], P(('batch', 'seq'))
- grad_attn_shift: float32 [2048], P(('batch', 'seq'))
- grad_query_weight: float32 [2048, 2048], P(('batch', 'seq'))
- grad_key_weight: float32 [2048, 2048], P(('batch', 'seq'))
- grad_value_weight: float32 [2048, 2048], P(('batch', 'seq'))
- grad_query_bias: float32 [2048], P(('batch', 'seq'))
- grad_value_bias: float32 [2048], P(('batch', 'seq'))
- grad_output_weight: float32 [2048, 2048], P(('batch', 'seq'))
- grad_output_bias: float32 [2048], P(('batch', 'seq'))
- grad_mlp_gain: float32 [2048], P(('batch', 'seq'))
- grad_mlp_shift: float32 [2048], P(('batch', 'seq'))
- grad_up_weight: float32 [2048, 8192], P(('batch', 'seq'))
- grad_up_bias: float32 [8192], P(('batch', 'seq'))
- grad_down_weight: float32 [8192, 2048], P(('batch', 'seq'))
- grad_down_bias: float32 [2048], P(('batch', 'seq'))
Inputs may be any that keep to these rules, and one draw needn't show every extreme that they name: `seg_lengths`: in each item the nonzero lengths come first, each between 1024 and 2048, and they sum to at most 2048; the remaining slots are padding.
All inputs are finite; a program needn't handle non-finite values.
Results may differ from a plain program's by a relative error of at most 0.04.
Values may be sent and summed in bfloat16 or wider, within the bound.
No kernel may reach another device: no remote copies, remote signals or barrier semaphores. Data moves between devices by JAX's collectives and lax.ppermute only.
A program may use at most 448 MiB of HBM per device.

v0:
```python
import math

import jax
import jax.numpy as jnp
from jax import lax
from jax.sharding import PartitionSpec as P

HEADS = 32
HEAD_DIM = 64


EPS = 1e-05
NEGATIVE = -1e30


def layer_norm(values, gain, shift):
    center = values - jnp.mean(values, axis=-1, keepdims=True)
    spread = jnp.mean(center * center, axis=-1, keepdims=True)
    return center * lax.rsqrt(spread + EPS) * gain + shift


def gelu_exact(values):
    return jax.nn.gelu(values, approximate=False)


def local_labels(lengths, first_row, count, tok_dev, pre_dev):
    rows = first_row + jnp.arange(count, dtype=jnp.int32)
    width = tok_dev + pre_dev
    device = rows // width
    inside = rows % width
    is_token = inside < tok_dev
    place = jnp.where(is_token, device * tok_dev + inside, device * pre_dev + inside - tok_dev)
    ends = jnp.cumsum(lengths)
    segment = jnp.sum((ends[None, :] <= place[:, None]).astype(jnp.int32), axis=1)
    segment = jnp.where(is_token, segment, -1)
    validity = jnp.where(is_token & (place >= ends[-1]), 0.0, 1.0).astype(jnp.float32)
    return (segment, place, validity)


def visible(query_seg, query_pos, key_seg, key_pos):
    same = (key_seg[None, :] == query_seg[:, None]) & (key_pos[None, :] <= query_pos[:, None])
    memory = (key_seg[None, :] < 0) & (query_seg[:, None] >= 0)
    return same | memory


def block_rows(count, width):
    shards = count // width
    group = 1
    for trial in range(1, shards + 1):
        if shards % trial == 0 and trial * width <= 1024:
            group = trial
    return group * width


def rows_dot(left, right):
    return lax.dot_general(
        left, right, (((0,), (0,)), ((), ())), preferred_element_type=jnp.float32
    )


def back_dot(left, right):
    return lax.dot_general(
        left, right, (((1,), (1,)), ((), ())), preferred_element_type=jnp.float32
    )


def body(
    tokens,
    prefix,
    seg_lengths,
    attn_gain,
    attn_shift,
    query_weight,
    key_weight,
    value_weight,
    query_bias,
    value_bias,
    output_weight,
    output_bias,
    mlp_gain,
    mlp_shift,
    up_weight,
    up_bias,
    down_weight,
    down_bias,
    cot_tokens,
    cot_prefix,
):
    tok_dev = tokens.shape[1]
    pre_dev = prefix.shape[1]
    width = tok_dev + pre_dev
    model = tokens.shape[2]
    heads = HEADS
    head_dim = HEAD_DIM
    scale = 1.0 / math.sqrt(HEAD_DIM)
    lengths = seg_lengths[0]
    here = lax.axis_index("seq")
    own_seg, own_pos, own_valid = local_labels(lengths, here * width, width, tok_dev, pre_dev)
    validity = own_valid[:, None]
    rows_in = jnp.concatenate([tokens[0], prefix[0]], axis=0).astype(jnp.float32)
    gain_a, shift_a, weight_q, weight_k, weight_v, bias_q, bias_v, weight_o, bias_o = (
        lax.all_gather(attn_gain, ("batch", "seq"), axis=0, tiled=True),
        lax.all_gather(attn_shift, ("batch", "seq"), axis=0, tiled=True),
        lax.all_gather(query_weight, ("batch", "seq"), axis=0, tiled=True),
        lax.all_gather(key_weight, ("batch", "seq"), axis=0, tiled=True),
        lax.all_gather(value_weight, ("batch", "seq"), axis=0, tiled=True),
        lax.all_gather(query_bias, ("batch", "seq"), axis=0, tiled=True),
        lax.all_gather(value_bias, ("batch", "seq"), axis=0, tiled=True),
        lax.all_gather(output_weight, ("batch", "seq"), axis=0, tiled=True),
        lax.all_gather(output_bias, ("batch", "seq"), axis=0, tiled=True),
    )
    normed = layer_norm(rows_in, gain_a.astype(jnp.float32), shift_a.astype(jnp.float32)).astype(
        jnp.bfloat16
    )
    queries = (
        jnp.dot(normed, weight_q, preferred_element_type=jnp.float32) + bias_q.astype(jnp.float32)
    ).astype(jnp.bfloat16)
    keys_local = jnp.dot(normed, weight_k, preferred_element_type=jnp.float32).astype(jnp.bfloat16)
    values_local = (
        jnp.dot(normed, weight_v, preferred_element_type=jnp.float32) + bias_v.astype(jnp.float32)
    ).astype(jnp.bfloat16)
    query_heads = queries.reshape(width, heads, head_dim)

    def scores_for(key_block, first):
        count = key_block.shape[0]
        key_seg, key_pos, unused = local_labels(lengths, first, count, tok_dev, pre_dev)
        mask = visible(own_seg, own_pos, key_seg, key_pos)
        raw = (
            jnp.einsum(
                "qhd,khd->hqk",
                query_heads,
                key_block.reshape(count, heads, head_dim),
                preferred_element_type=jnp.float32,
            )
            * scale
        )
        return (raw, mask)

    start_state = (
        jnp.full((heads, width), NEGATIVE, jnp.float32),
        jnp.zeros((heads, width), jnp.float32),
        jnp.zeros((heads, width, head_dim), jnp.float32),
    )
    key_piece = lax.all_gather(keys_local, "seq", axis=0, tiled=True)
    value_piece = lax.all_gather(values_local, "seq", axis=0, tiled=True)
    count = key_piece.shape[0]
    size = block_rows(count, width)

    def forward_one_block(index, inner):
        top, total, summed = inner
        first = index * size
        key_block = lax.dynamic_slice_in_dim(key_piece, first, size, 0)
        value_block = lax.dynamic_slice_in_dim(value_piece, first, size, 0)
        raw, mask = scores_for(key_block, first)
        raw = jnp.where(mask[None], raw, NEGATIVE)
        new_top = jnp.maximum(top, jnp.max(raw, axis=2))
        factor = jnp.exp(top - new_top)
        weights = jnp.where(mask[None], jnp.exp(raw - new_top[:, :, None]), 0.0)
        total = total * factor + jnp.sum(weights, axis=2)
        summed = summed * factor[:, :, None] + jnp.einsum(
            "hqk,khd->hqd",
            weights.astype(jnp.bfloat16),
            value_block.reshape(size, heads, head_dim),
            preferred_element_type=jnp.float32,
        )
        return (new_top, total, summed)

    top, total, summed = lax.fori_loop(0, count // size, forward_one_block, start_state)
    attended = summed / total[:, :, None]
    log_total = top + jnp.log(total)
    mixed_low = attended.transpose(1, 0, 2).reshape(width, model).astype(jnp.bfloat16)
    branch = jnp.dot(mixed_low, weight_o, preferred_element_type=jnp.float32) + bias_o.astype(
        jnp.float32
    )
    resid = rows_in + validity * branch
    gain_m, shift_m, weight_up, bias_up, weight_down, bias_down = (
        lax.all_gather(mlp_gain, ("batch", "seq"), axis=0, tiled=True),
        lax.all_gather(mlp_shift, ("batch", "seq"), axis=0, tiled=True),
        lax.all_gather(up_weight, ("batch", "seq"), axis=0, tiled=True),
        lax.all_gather(up_bias, ("batch", "seq"), axis=0, tiled=True),
        lax.all_gather(down_weight, ("batch", "seq"), axis=0, tiled=True),
        lax.all_gather(down_bias, ("batch", "seq"), axis=0, tiled=True),
    )
    normed_m = layer_norm(resid, gain_m.astype(jnp.float32), shift_m.astype(jnp.float32)).astype(
        jnp.bfloat16
    )
    hidden_pre = jnp.dot(normed_m, weight_up, preferred_element_type=jnp.float32) + bias_up.astype(
        jnp.float32
    )
    hidden = gelu_exact(hidden_pre).astype(jnp.bfloat16)
    final = resid + validity * (
        jnp.dot(hidden, weight_down, preferred_element_type=jnp.float32)
        + bias_down.astype(jnp.float32)
    )
    out_rows = final.astype(jnp.bfloat16)
    cot_rows = jnp.concatenate([cot_tokens[0], cot_prefix[0]], axis=0).astype(jnp.float32)
    gain_m, shift_m, weight_up, bias_up, weight_down, bias_down = (
        lax.all_gather(mlp_gain, ("batch", "seq"), axis=0, tiled=True),
        lax.all_gather(mlp_shift, ("batch", "seq"), axis=0, tiled=True),
        lax.all_gather(up_weight, ("batch", "seq"), axis=0, tiled=True),
        lax.all_gather(up_bias, ("batch", "seq"), axis=0, tiled=True),
        lax.all_gather(down_weight, ("batch", "seq"), axis=0, tiled=True),
        lax.all_gather(down_bias, ("batch", "seq"), axis=0, tiled=True),
    )
    mlp_out_grad = (validity * cot_rows).astype(jnp.bfloat16)
    grad_down = rows_dot(hidden, mlp_out_grad)
    grad_down_bias = jnp.sum(mlp_out_grad.astype(jnp.float32), axis=0)
    hidden_grad = back_dot(mlp_out_grad, weight_down)
    unused, gelu_back = jax.vjp(gelu_exact, hidden_pre)
    pre_grad = gelu_back(hidden_grad)[0].astype(jnp.bfloat16)
    grad_up = rows_dot(normed_m, pre_grad)
    grad_up_bias = jnp.sum(pre_grad.astype(jnp.float32), axis=0)
    normed_grad = back_dot(pre_grad, weight_up)
    unused, norm_back = jax.vjp(
        layer_norm, resid, gain_m.astype(jnp.float32), shift_m.astype(jnp.float32)
    )
    resid_extra, grad_gain_m, grad_shift_m = norm_back(normed_grad)
    resid_grad = cot_rows + resid_extra
    mlp_shares = (
        lax.psum_scatter(grad_gain_m, ("batch", "seq"), scatter_dimension=0, tiled=True),
        lax.psum_scatter(grad_shift_m, ("batch", "seq"), scatter_dimension=0, tiled=True),
        lax.psum_scatter(grad_up, ("batch", "seq"), scatter_dimension=0, tiled=True),
        lax.psum_scatter(grad_up_bias, ("batch", "seq"), scatter_dimension=0, tiled=True),
        lax.psum_scatter(grad_down, ("batch", "seq"), scatter_dimension=0, tiled=True),
        lax.psum_scatter(grad_down_bias, ("batch", "seq"), scatter_dimension=0, tiled=True),
    )
    gain_a, shift_a, weight_q, weight_k, weight_v, bias_q, bias_v, weight_o, bias_o = (
        lax.all_gather(attn_gain, ("batch", "seq"), axis=0, tiled=True),
        lax.all_gather(attn_shift, ("batch", "seq"), axis=0, tiled=True),
        lax.all_gather(query_weight, ("batch", "seq"), axis=0, tiled=True),
        lax.all_gather(key_weight, ("batch", "seq"), axis=0, tiled=True),
        lax.all_gather(value_weight, ("batch", "seq"), axis=0, tiled=True),
        lax.all_gather(query_bias, ("batch", "seq"), axis=0, tiled=True),
        lax.all_gather(value_bias, ("batch", "seq"), axis=0, tiled=True),
        lax.all_gather(output_weight, ("batch", "seq"), axis=0, tiled=True),
        lax.all_gather(output_bias, ("batch", "seq"), axis=0, tiled=True),
    )
    branch_grad = (validity * resid_grad).astype(jnp.bfloat16)
    grad_out = rows_dot(mixed_low, branch_grad)
    grad_out_bias = jnp.sum(branch_grad.astype(jnp.float32), axis=0)
    mixed_grad = back_dot(branch_grad, weight_o).astype(jnp.bfloat16)
    grad_heads = mixed_grad.reshape(width, heads, head_dim)
    delta = jnp.sum(grad_heads.astype(jnp.float32).transpose(1, 0, 2) * attended, axis=2)
    own_keys = keys_local.reshape(width, heads, head_dim)
    own_values = values_local.reshape(width, heads, head_dim)
    query_start = jnp.zeros((heads, width, head_dim), jnp.float32)
    backward_key_piece = lax.all_gather(keys_local, "seq", axis=0, tiled=True)
    backward_value_piece = lax.all_gather(values_local, "seq", axis=0, tiled=True)
    count = backward_key_piece.shape[0]
    backward_size = block_rows(count, width)

    def backward_one_block(index, inner):
        first = index * backward_size
        key_block = lax.dynamic_slice_in_dim(backward_key_piece, first, backward_size, 0)
        value_block = lax.dynamic_slice_in_dim(backward_value_piece, first, backward_size, 0)
        raw, mask = scores_for(key_block, first)
        probs = jnp.where(mask[None], jnp.exp(raw - log_total[:, :, None]), 0.0)
        prob_grad = jnp.einsum(
            "qhd,khd->hqk",
            grad_heads,
            value_block.reshape(backward_size, heads, head_dim),
            preferred_element_type=jnp.float32,
        )
        score_grad = (probs * (prob_grad - delta[:, :, None])).astype(jnp.bfloat16)
        step_sum = (
            jnp.einsum(
                "hqk,khd->hqd",
                score_grad,
                key_block.reshape(backward_size, heads, head_dim),
                preferred_element_type=jnp.float32,
            )
            * scale
        )
        return inner + step_sum

    back_result = lax.fori_loop(0, count // backward_size, backward_one_block, query_start)
    query_piece = lax.all_gather(
        queries.astype(jnp.float32).astype(jnp.bfloat16), "seq", axis=0, tiled=True
    ).astype(jnp.float32)
    grad_piece = lax.all_gather(
        mixed_grad.astype(jnp.float32).astype(jnp.bfloat16), "seq", axis=0, tiled=True
    ).astype(jnp.float32)
    total_piece = lax.all_gather(
        log_total.T.astype(jnp.bfloat16), "seq", axis=0, tiled=True
    ).astype(jnp.float32)
    delta_piece = lax.all_gather(delta.T.astype(jnp.bfloat16), "seq", axis=0, tiled=True).astype(
        jnp.float32
    )
    count = query_piece.shape[0]
    owner_size = block_rows(count, width)

    def owner_one_block(index, inner):
        first = index * owner_size
        query_block = lax.dynamic_slice_in_dim(query_piece, first, owner_size, 0).astype(
            jnp.bfloat16
        )
        grad_block = lax.dynamic_slice_in_dim(grad_piece, first, owner_size, 0).astype(jnp.bfloat16)
        total_block = lax.dynamic_slice_in_dim(total_piece, first, owner_size, 0)
        delta_block = lax.dynamic_slice_in_dim(delta_piece, first, owner_size, 0)
        query_block = query_block.reshape(owner_size, heads, head_dim)
        grad_block = grad_block.reshape(owner_size, heads, head_dim)
        query_seg, query_pos, unused = local_labels(lengths, first, owner_size, tok_dev, pre_dev)
        mask = visible(query_seg, query_pos, own_seg, own_pos)
        raw = (
            jnp.einsum("qhd,khd->hqk", query_block, own_keys, preferred_element_type=jnp.float32)
            * scale
        )
        probs = jnp.where(mask[None], jnp.exp(raw - total_block.T[:, :, None]), 0.0)
        value_grad = jnp.einsum(
            "hqk,qhd->khd",
            probs.astype(jnp.bfloat16),
            grad_block,
            preferred_element_type=jnp.float32,
        )
        prob_grad = jnp.einsum(
            "qhd,khd->hqk", grad_block, own_values, preferred_element_type=jnp.float32
        )
        score_grad = (probs * (prob_grad - delta_block.T[:, :, None])).astype(jnp.bfloat16)
        key_grad = (
            jnp.einsum("hqk,qhd->khd", score_grad, query_block, preferred_element_type=jnp.float32)
            * scale
        )
        return inner + jnp.concatenate(
            [key_grad.reshape(width, model), value_grad.reshape(width, model)], axis=1
        )

    key_value_grad = lax.fori_loop(
        0, count // owner_size, owner_one_block, jnp.zeros((width, 2 * model), jnp.float32)
    )
    query_grad = back_result.transpose(1, 0, 2).reshape(width, model).astype(jnp.bfloat16)
    key_grad_low = key_value_grad[:, :model].astype(jnp.bfloat16)
    value_grad_low = key_value_grad[:, model:].astype(jnp.bfloat16)
    grad_query = rows_dot(normed, query_grad)
    grad_query_bias = jnp.sum(query_grad.astype(jnp.float32), axis=0)
    grad_key = rows_dot(normed, key_grad_low)
    grad_value = rows_dot(normed, value_grad_low)
    grad_value_bias = jnp.sum(value_grad_low.astype(jnp.float32), axis=0)
    normed_back = (
        back_dot(query_grad, weight_q)
        + back_dot(key_grad_low, weight_k)
        + back_dot(value_grad_low, weight_v)
    )
    unused, first_back = jax.vjp(
        layer_norm, rows_in, gain_a.astype(jnp.float32), shift_a.astype(jnp.float32)
    )
    input_extra, grad_gain_a, grad_shift_a = first_back(normed_back)
    input_grad = resid_grad + input_extra
    attn_shares = (
        lax.psum_scatter(grad_gain_a, ("batch", "seq"), scatter_dimension=0, tiled=True),
        lax.psum_scatter(grad_shift_a, ("batch", "seq"), scatter_dimension=0, tiled=True),
        lax.psum_scatter(grad_query, ("batch", "seq"), scatter_dimension=0, tiled=True),
        lax.psum_scatter(grad_key, ("batch", "seq"), scatter_dimension=0, tiled=True),
        lax.psum_scatter(grad_value, ("batch", "seq"), scatter_dimension=0, tiled=True),
        lax.psum_scatter(grad_query_bias, ("batch", "seq"), scatter_dimension=0, tiled=True),
        lax.psum_scatter(grad_value_bias, ("batch", "seq"), scatter_dimension=0, tiled=True),
        lax.psum_scatter(grad_out, ("batch", "seq"), scatter_dimension=0, tiled=True),
        lax.psum_scatter(grad_out_bias, ("batch", "seq"), scatter_dimension=0, tiled=True),
    )
    shares = attn_shares + mlp_shares
    return (
        out_rows[:tok_dev][None],
        out_rows[tok_dev:][None],
        input_grad[:tok_dev][None],
        input_grad[tok_dev:][None],
        shares[0],
        shares[1],
        shares[2],
        shares[3],
        shares[4],
        shares[5],
        shares[6],
        shares[7],
        shares[8],
        shares[9],
        shares[10],
        shares[11],
        shares[12],
        shares[13],
        shares[14],
    )


def solution(mesh):
    placed = (
        P("batch", "seq", None),
        P("batch", "seq", None),
        P("batch", None),
        P(("batch", "seq")),
        P(("batch", "seq")),
        P(("batch", "seq"), None),
        P(("batch", "seq"), None),
        P(("batch", "seq"), None),
        P(("batch", "seq")),
        P(("batch", "seq")),
        P(("batch", "seq"), None),
        P(("batch", "seq")),
        P(("batch", "seq")),
        P(("batch", "seq")),
        P(("batch", "seq"), None),
        P(("batch", "seq")),
        P(("batch", "seq"), None),
        P(("batch", "seq")),
        P("batch", "seq", None),
        P("batch", "seq", None),
    )
    return jax.shard_map(
        body,
        mesh=mesh,
        in_specs=placed,
        out_specs=(
            P("batch", "seq", None),
            P("batch", "seq", None),
            P("batch", "seq", None),
            P("batch", "seq", None),
            P(("batch", "seq")),
            P(("batch", "seq")),
            P(("batch", "seq"), None),
            P(("batch", "seq"), None),
            P(("batch", "seq"), None),
            P(("batch", "seq")),
            P(("batch", "seq")),
            P(("batch", "seq"), None),
            P(("batch", "seq")),
            P(("batch", "seq")),
            P(("batch", "seq")),
            P(("batch", "seq"), None),
            P(("batch", "seq")),
            P(("batch", "seq"), None),
            P(("batch", "seq")),
        ),
        check_vma=False,
    )
```

profile of v0, /device:TPU:0, one launch (start us, length us, event | category | flops | bytes accessed | tf_op | source)
XLA Modules:
  0.0 3831.1 jit_solution(12423914437784234045)
XLA Ops:
  16.3 43.4 %all-reduce.18 = (bf16[2048]{0:T(1024)(128)(2,1)S(1)}, bf16[2048]{0:T(1024)(128)(2,1)S(1)}, bf16[2048]{0:T(1024)(128)(2,1)S(1)}, bf16[2048]{0:T(1024)(128)(2,1)S...) all-reduce(bf16[2048]{0:T(1024)(128)(2,1)S(1)} %dynamic-update-slic, ...), channel_id=1, replica_groups=mesh['batch'=4,'seq'=8] {'batch','seq'}, use_global_device_ids=true, to_apply=%add.1 | all-reduce | flops 16384 | bytes 65536
  63.4 28.0 all-gather.18.cloned.1.call-done
  98.9 71.4 %all-gather.22.cloned.1.call-done = bf16[2048,2048]{1,0:T(8,128)(2,1)} async-done(((bf16[64,2048]{1,0:T(8,128)(2,1)}), bf16[2048,2048]{1,0:T(8,128)(2,1)}) %all-gather.22.cloned.1.call-update) | async-done | bytes 8388624 | tf_op jit(solution)/shard_map/all_gather | solution.py:106
  177.8 71.5 %all-gather.20.cloned.1.call-done = bf16[2048,2048]{1,0:T(8,128)(2,1)} async-done(((bf16[64,2048]{1,0:T(8,128)(2,1)}), bf16[2048,2048]{1,0:T(8,128)(2,1)}) %all-gather.20.cloned.1.call-update) | async-done | bytes 8388624 | tf_op jit(solution)/shard_map/all_gather | solution.py:104
  260.6 39.9 %all-gather.2 = bf16[32,1,256]{2,1,0:T(2,128)(2,1)S(1)} all-gather(bf16[1,1,256]{2,1,0:T(2,128)(2,1)S(1)} %reshape.782), channel_id=1, replica_groups=mesh['batch'=4,'seq'=8] {'batch','seq'}, dimensions={0}, use_global_device_ids=true | all-gather | bytes 16896 | tf_op jit(solution)/shard_map/all_gather | solution.py:180
  308.7 38.8 %all-gather.30.cloned.1.call-done = bf16[8,306,2048]{2,1,0:T(8,128)(2,1)} async-done(((bf16[1,306,2048]{2,1,0:T(8,128)(2,1)}), bf16[8,306,2048]{2,1,0:T(8,128)(2,1)}) %all-gather.30.cloned.1.call-update) | async-done | bytes 10027024 | tf_op jit(solution)/shard_map/all_gather | solution.py:144
  373.8 70.7 %all-gather.32.cloned.1.call-done = bf16[8,306,2048]{2,1,0:T(8,128)(2,1)} async-done(((bf16[1,306,2048]{2,1,0:T(8,128)(2,1)}), bf16[8,306,2048]{2,1,0:T(8,128)(2,1)}) %all-gather.32.cloned.1.call-update) | async-done | bytes 10027024 | tf_op jit(solution)/shard_map/all_gather | solution.py:145
  470.9 194.1 %while.52 = (s32[]{:T(128)}, f32[32,306]{1,0:T(8,128)S(1)}, f32[32,306]{1,0:T(8,128)S(1)}, f32[32,306,64]{1,2,0:T(8,128)}, s32[1,2]{1,0:T(1,128)S(1)}, /*index=5...) while((s32[]{:T(128)}, f32[32,306]{1,0:T(8,128)S(1)}, ...), condition=%wide.region_9.10_spmd.clone, body=%wide.region_5.9_spmd.clone.sunk | while | flops 1614930688 | bytes 94619704 | solution.py:168
  681.5 20.2 reshape.793
  712.2 105.4 %all-gather.26.cloned.1.call-done = bf16[2048,8192]{1,0:T(8,128)(2,1)} async-done(((bf16[64,8192]{1,0:T(8,128)(2,1)}), bf16[2048,8192]{1,0:T(8,128)(2,1)}) %all-gather.26.cloned.1.call-update) | async-done | bytes 33554448 | tf_op jit(solution)/shard_map/all_gather | solution.py:179
  817.6 39.6 %multiply_convert_fusion.1 = (bf16[306,8192]{1,0:T(8,128)(2,1)}, f32[306,8192]{1,0:T(8,128)}, f32[306,8192]{1,0:T(8,128)}) fusion(f32[8192]{0:T(1024)S(1)} %bitcast.251, bf16[2048,8192]{1,0:T(8,128)(2,1)} %all-gather.26.cloned.1.call-done, f32[306,2048]{1,0:T(8,128)} %copy-done.6, f32[2048]{0:T(1024)S(1)} %copy-done.39, f32[2048]{0:T(1024)S(1)} %copy-done.35, ...), kind=kOutput, calls=%fused_computation.132 | convolution fusion | flops 10436235264 | bytes 61180304 | tf_op jit(solution)/shard_map/dot_general | solution.py:187
  857.2 156.5 %all-gather.28.cloned.1.call-done = bf16[8192,2048]{1,0:T(8,128)(2,1)} async-done(((bf16[256,2048]{1,0:T(8,128)(2,1)}), bf16[8192,2048]{1,0:T(8,128)(2,1)}) %all-gather.28.cloned.1.call-update) | async-done | bytes 33554448 | tf_op jit(solution)/shard_map/all_gather | solution.py:181
  1013.7 25.4 convert_reduce_fusion
  1086.5 144.2 %while.53 = (s32[]{:T(128)}, f32[32,306,64]{1,2,0:T(8,128)}, s32[1,2]{1,0:T(1,128)S(1)}, s32[306]{0:T(512)S(1)}, bf16[2448,2048]{0,1:T(8,128)(2,1)}, /*index=5*/...) while((s32[]{:T(128)}, f32[32,306,64]{1,2,0:T(8,128)}, ...), condition=%wide.region_17.18_spmd.clone, body=%wide.region_15.17_spmd.clone.sunk | while | flops 2339998976 | bytes 78499664 | solution.py:276
  1254.2 253.5 %while.54 = (s32[]{:T(128)}, f32[306,4096]{0,1:T(8,128)}, bf16[2448,2048]{1,0:T(8,128)(2,1)}, s32[306]{0:T(512)S(1)}, s32[1,2]{1,0:T(1,128)S(1)}, /*index=5*/bf1...) while((s32[]{:T(128)}, f32[306,4096]{0,1:T(8,128)}, ...), condition=%wide.region_20.21_spmd.clone, body=%wide.region_18.20_spmd.clone.sunk | while | flops 3133542656 | bytes 135715568 | solution.py:327
  1569.8 30.9 fusion.116
  1601.9 28.9 fusion.110
  1631.5 19.5 fusion.85
  1671.4 172.2 %reduce-scatter.7.cloned.1.call-done = f32[64,2048]{1,0:T(8,128)} async-done(((f32[2048,2048]{1,0:T(8,128)}), f32[64,2048]{1,0:T(8,128)}) %reduce-scatter.7.cloned.1.call-update) | async-done | bytes 524304 | tf_op jit(solution)/shard_map/reduce_scatter | solution.py:351
  1843.6 187.3 %reduce-scatter.13.cloned.1.call-done = f32[64,2048]{1,0:T(8,128)} async-done(((f32[2048,2048]{1,0:T(8,128)}), f32[64,2048]{1,0:T(8,128)}) %reduce-scatter.13.cloned.1.call-update) | async-done | bytes 524304 | tf_op jit(solution)/shard_map/reduce_scatter | solution.py:356
  2030.9 187.2 %reduce-scatter.9.cloned.1.call-done = f32[64,2048]{1,0:T(8,128)} async-done(((f32[2048,2048]{1,0:T(8,128)}), f32[64,2048]{1,0:T(8,128)}) %reduce-scatter.9.cloned.1.call-update) | async-done | bytes 524304 | tf_op jit(solution)/shard_map/reduce_scatter | solution.py:352
  2218.1 187.2 %reduce-scatter.11.cloned.1.call-done = f32[64,2048]{1,0:T(8,128)} async-done(((f32[2048,2048]{1,0:T(8,128)}), f32[64,2048]{1,0:T(8,128)}) %reduce-scatter.11.cloned.1.call-update) | async-done | bytes 524304 | tf_op jit(solution)/shard_map/reduce_scatter | solution.py:353
  2405.3 710.0 %reduce-scatter.15.cloned.1.call-done = f32[64,8192]{1,0:T(8,128)} async-done(((f32[2048,8192]{1,0:T(8,128)}), f32[64,8192]{1,0:T(8,128)}) %reduce-scatter.15.cloned.1.call-update) | async-done | bytes 2097168 | tf_op jit(solution)/shard_map/reduce_scatter | solution.py:222
  3115.3 708.8 %reduce-scatter.17.cloned.1.call-done = f32[256,2048]{1,0:T(8,128)} async-done(((f32[8192,2048]{1,0:T(8,128)}), f32[256,2048]{1,0:T(8,128)}) %reduce-scatter.17.cloned.1.call-update) | async-done | bytes 2097168 | tf_op jit(solution)/shard_map/reduce_scatter | solution.py:224
  (427 shorter events, 871.9 us)
Async XLA Ops:
  7.2 84.2 %all-gather.18.cloned.1.call-start = ((), (), s32[]{:S(2)}) async-start(), calls=%async_computation.6 | async-start | bytes 8650752 | tf_op jit(solution)/shard_map/all_gather | solution.py:105
  7.9 162.3 %all-gather.22.cloned.1.call-start = ((), (), s32[]{:S(2)}) async-start(), calls=%async_computation.8 | async-start | bytes 8650752 | tf_op jit(solution)/shard_map/all_gather | solution.py:106
  8.7 240.6 %all-gather.20.cloned.1.call-start = ((), (), s32[]{:S(2)}) async-start(), calls=%async_computation.7 | async-start | bytes 8650752 | tf_op jit(solution)/shard_map/all_gather | solution.py:104
  9.4 338.1 %all-gather.30.cloned.1.call-start = ((), (), s32[]{:S(2)}) async-start(), calls=%async_computation.18 | async-start | bytes 11501568 | tf_op jit(solution)/shard_map/all_gather | solution.py:144
  59.6 189.7 %copy-start.37 = (f32[2048]{0:T(1024)}, f32[2048]{0:T(1024)S(1)}, u32[]{:S(2)}) copy-start(f32[2048]{0:T(1024)S(1)} %convert_element_type.232) | copy-start | bytes 24580
  59.6 189.7 %copy-start.33 = (f32[2048]{0:T(1024)}, f32[2048]{0:T(1024)S(1)}, u32[]{:S(2)}) copy-start(f32[2048]{0:T(1024)S(1)} %convert_element_type.231) | copy-start | bytes 24580
  61.3 188.0 %copy-start.41 = (f32[306]{0:T(512)}, f32[306]{0:T(512)S(1)}, u32[]{:S(2)}) copy-start(f32[306]{0:T(512)S(1)} %broadcast_multiply_fusion.1) | copy-start | bytes 3676
  63.4 185.9 %copy-start.43 = (f32[306]{0:T(512)}, f32[306]{0:T(512)S(1)}, u32[]{:S(2)}) copy-start(f32[306]{0:T(512)S(1)} %fusion.107) | copy-start | bytes 3676
  98.8 345.7 %all-gather.32.cloned.1.call-start = ((), (), s32[]{:S(2)}) async-start(), calls=%async_computation.19 | async-start | bytes 11501568 | tf_op jit(solution)/shard_map/all_gather | solution.py:145
  177.7 503.8 %all-gather.34.cloned.1.call-start = ((), (), s32[]{:S(2)}) async-start(), calls=%async_computation.20 | async-start | bytes 11501568 | tf_op jit(solution)/shard_map/all_gather | solution.py:277
  256.7 447.4 %all-gather.24.cloned.1.call-start = ((), (), s32[]{:S(2)}) async-start(), calls=%async_computation.9 | async-start | bytes 8650752 | tf_op jit(solution)/shard_map/all_gather | solution.py:109
  257.5 560.1 %all-gather.26.cloned.1.call-start = ((), (), s32[]{:S(2)}) async-start(), calls=%async_computation.10 | async-start | bytes 34603008 | tf_op jit(solution)/shard_map/all_gather | solution.py:179
  258.2 755.5 %all-gather.28.cloned.1.call-start = ((), (), s32[]{:S(2)}) async-start(), calls=%async_computation.11 | async-start | bytes 34603008 | tf_op jit(solution)/shard_map/all_gather | solution.py:181
  259.0 983.2 %all-gather.36.cloned.1.call-start = ((), (), s32[]{:S(2)}) async-start(), calls=%async_computation.21 | async-start | bytes 11501568 | tf_op jit(solution)/shard_map/all_gather | solution.py:280
  710.3 346.9 %copy-start.45 = (f32[306]{0:T(512)}, f32[306]{0:T(512)S(1)}, u32[]{:S(2)}) copy-start(f32[306]{0:T(512)S(1)} %broadcast_multiply_fusion) | copy-start | bytes 3676
  712.2 345.0 %copy-start.47 = (f32[306]{0:T(512)}, f32[306]{0:T(512)S(1)}, u32[]{:S(2)}) copy-start(f32[306]{0:T(512)S(1)} %fusion.108) | copy-start | bytes 3676
  817.6 196.1 %copy-start.29 = (bf16[1,50,2048]{2,1,0:T(8,128)(2,1)S(1)}, bf16[1,50,2048]{2,1,0:T(8,128)(2,1)}, u32[]{:S(2)}) copy-start(bf16[1,50,2048]{2,1,0:T(8,128)(2,1)} %param.45) | copy-start | bytes 614404
  1071.0 588.9 %all-reduce.21.cloned.1.call-start = ((), (), s32[]{:S(2)}) async-start(), calls=%async_computation.22 | async-start | bytes 196608
  1528.9 314.7 %reduce-scatter.7.cloned.1.call-start = ((), (), s32[]{:S(2)}) async-start(), calls=%async_computation.12 | async-start | bytes 17301504 | tf_op jit(solution)/shard_map/reduce_scatter | solution.py:351
  1537.5 493.4 %reduce-scatter.13.cloned.1.call-start = ((), (), s32[]{:S(2)}) async-start(), calls=%async_computation.15 | async-start | bytes 17301504 | tf_op jit(solution)/shard_map/reduce_scatter | solution.py:356
  1548.3 669.8 %reduce-scatter.9.cloned.1.call-start = ((), (), s32[]{:S(2)}) async-start(), calls=%async_computation.13 | async-start | bytes 17301504 | tf_op jit(solution)/shard_map/reduce_scatter | solution.py:352
  1558.8 846.5 %reduce-scatter.11.cloned.1.call-start = ((), (), s32[]{:S(2)}) async-start(), calls=%async_computation.14 | async-start | bytes 17301504 | tf_op jit(solution)/shard_map/reduce_scatter | solution.py:353
  1569.1 1546.2 %reduce-scatter.15.cloned.1.call-start = ((), (), s32[]{:S(2)}) async-start(), calls=%async_computation.16 | async-start | bytes 69206016 | tf_op jit(solution)/shard_map/reduce_scatter | solution.py:222
  1600.7 2223.5 %reduce-scatter.17.cloned.1.call-start = ((), (), s32[]{:S(2)}) async-start(), calls=%async_computation.17 | async-start | bytes 69206016 | tf_op jit(solution)/shard_map/reduce_scatter | solution.py:224
  (64 other events, 1034.2 us)
Sparse Core Ops, SparseCore 0:
  11.0 80.3 all-gather.17
  94.4 75.8 all-gather.21
  173.3 75.9 all-gather.19
  251.4 96.0 all-gather.29
  349.0 95.5 all-gather.31
  446.6 95.6 all-gather.33
  545.3 75.7 all-gather.23
  624.1 193.4 all-gather.25
  820.6 193.0 all-gather.27
  1071.1 95.6 all-gather.35
  1529.0 123.9 all-reduce.20
  1655.9 187.6 reduce-scatter.6
  1846.5 184.3 reduce-scatter.12
  2033.7 184.3 reduce-scatter.8
  2220.9 184.3 reduce-scatter.10
  2408.2 707.0 reduce-scatter.14
  3118.2 705.8 reduce-scatter.16
where the time goes:
time: 3840 us; the launch traced here: 3830 us
  waiting for transfers between devices  2700 us (70%)
  matrix products  640 us (17%)
  local copies, waits for them, and re-layouts  244 us (6%)
  other arithmetic  118 us (3%)
  blocking collectives  112 us (3%)
    reduce_scatter x1, waiting for transfers between devices, body(): lax.psum_scatter(grad_up, ('batch', 'seq'), scatter_dimension=0, tiled=True)  710 us
    reduce_scatter x1, waiting for transfers between devices, body(): lax.psum_scatter(grad_down, ('batch', 'seq'), scatter_dimension=0, tiled=...  709 us
    reduce_scatter x1, waiting for transfers between devices, body(): lax.psum_scatter(grad_out, ('batch', 'seq'), scatter_dimension=0, tiled=T...  187 us
    reduce_scatter x1, waiting for transfers between devices, body(): lax.psum_scatter(grad_key, ('batch', 'seq'), scatter_dimension=0, tiled=T...  187 us
    reduce_scatter x1, waiting for transfers between devices, body(): lax.psum_scatter(grad_value, ('batch', 'seq'), scatter_dimension=0, tiled...  187 us
    reduce_scatter x1, waiting for transfers between devices, body(): lax.psum_scatter(grad_query, ('batch', 'seq'), scatter_dimension=0, tiled...  172 us
    all_gather x1, waiting for transfers between devices, body(): lax.all_gather(down_weight, ('batch', 'seq'), axis=0, tiled=True)  156 us
    all_gather x1, waiting for transfers between devices, body(): lax.all_gather(up_weight, ('batch', 'seq'), axis=0, tiled=True)  105 us
  transfers between devices with their start and end apart: 17, of which 13 were waited for; matrix products, arithmetic and copies ran while one was open for 17% of the time, Pallas kernels for 0%

commit v1 on v0

v1 whole, which is shorter than its diff:
```python
import functools
import math

import jax
import jax.numpy as jnp
from jax import lax
from jax.experimental import pallas as pl
from jax.experimental.pallas import tpu as pltpu
from jax.sharding import PartitionSpec as P

HEADS = 32
HEAD_DIM = 64
EPS = 1e-05
NEGATIVE = -1e30
FAR = 1 << 20
BLOCK = 256
BF16 = jnp.bfloat16
F32 = jnp.float32


def contract(left, right, left_dim, right_dim):
    return lax.dot_general(
        left, right, (((left_dim,), (right_dim,)), ((), ())), preferred_element_type=F32
    )


def row_pieces(devices, pre, tok):
    pieces = []
    for device in range(devices):
        first = device * (pre + tok)
        pieces.append((first, device * pre, pre))
        pieces.append((first + pre, devices * pre + device * tok, tok))
    return pieces


def block_mask(place, low, high):
    return (place <= high) & ((place >= low) | (place < 0))


def forward_kernel(
    devices, pre, tok, heads, head_dim,
    qkv_ref, place_ref, low_ref, high_ref,
    o_ref, ot_ref, lse_ref,
    q_s, k_s, vt_s, acc_s, m_s, l_s,
):
    width = heads * head_dim
    blocks = devices * (pre + tok) // BLOCK
    for src, dst, cnt in row_pieces(devices, pre, tok):
        q_s[dst : dst + cnt, :] = qkv_ref[src : src + cnt, 0:width]
        k_s[dst : dst + cnt, :] = qkv_ref[src : src + cnt, width : 2 * width]
        o_ref[dst : dst + cnt, :] = qkv_ref[src : src + cnt, 2 * width : 3 * width]
    for b in range(blocks):
        rows = slice(b * BLOCK, (b + 1) * BLOCK)
        vt_s[:, rows] = o_ref[rows, :].astype(F32).T.astype(BF16)
    lane = lax.broadcasted_iota(jnp.int32, (BLOCK, width), 1) // head_dim

    def query_block(i, carry):
        qs = pl.ds(pl.multiple_of(i * BLOCK, BLOCK), BLOCK)
        q = q_s[qs, :]
        qh = [jnp.where(lane == h, q, jnp.zeros_like(q)) for h in range(heads)]
        low = low_ref[:, qs]
        high = high_ref[:, qs]
        acc_s[...] = jnp.zeros_like(acc_s)
        m_s[...] = jnp.full_like(m_s, NEGATIVE)
        l_s[...] = jnp.zeros_like(l_s)

        def key_block(j, inner):
            ks = pl.ds(pl.multiple_of(j * BLOCK, BLOCK), BLOCK)
            k = k_s[ks, :]
            bias = jnp.where(block_mask(place_ref[ks, :], low, high), 0.0, NEGATIVE)
            for h in range(heads):
                s = contract(k, qh[h], 1, 1) + bias
                old = m_s[h : h + 1, :]
                new = jnp.maximum(old, jnp.max(s, axis=0, keepdims=True))
                p = jnp.exp(s - new)
                alpha = jnp.exp(old - new)
                m_s[h : h + 1, :] = new
                l_s[h : h + 1, :] = l_s[h : h + 1, :] * alpha + jnp.sum(p, axis=0, keepdims=True)
                hs = slice(h * head_dim, (h + 1) * head_dim)
                acc_s[hs, :] = acc_s[hs, :] * alpha + contract(vt_s[hs, ks], p.astype(BF16), 1, 0)
            return inner

        lax.fori_loop(0, i + 1, key_block, 0)
        for h in range(heads):
            hs = slice(h * head_dim, (h + 1) * head_dim)
            total = l_s[h : h + 1, :]
            acc_s[hs, :] = acc_s[hs, :] / total
            lse_ref[h : h + 1, qs] = m_s[h : h + 1, :] + jnp.log(total)
        result = acc_s[...]
        ot_ref[:, qs] = result
        q_s[qs, :] = result.T.astype(BF16)
        return carry

    lax.fori_loop(0, blocks, query_block, 0)
    for src, dst, cnt in row_pieces(devices, pre, tok):
        o_ref[src : src + cnt, :] = q_s[dst : dst + cnt, :]


def attention_forward(qkv, place, low, high, devices, pre, tok, heads, head_dim):
    width = heads * head_dim
    rows = devices * (pre + tok)
    vmem = pl.BlockSpec(memory_space=pltpu.VMEM)
    pairs = rows * rows // 2 * heads
    return pl.pallas_call(
        functools.partial(forward_kernel, devices, pre, tok, heads, head_dim),
        out_shape=(
            jax.ShapeDtypeStruct((rows, width), BF16),
            jax.ShapeDtypeStruct((width, rows), F32),
            jax.ShapeDtypeStruct((8, rows), F32),
        ),
        in_specs=[vmem] * 4,
        out_specs=(vmem,) * 3,
        scratch_shapes=[
            pltpu.VMEM((rows, width), BF16),
            pltpu.VMEM((rows, width), BF16),
            pltpu.VMEM((width, rows), BF16),
            pltpu.VMEM((width, BLOCK), F32),
            pltpu.VMEM((8, BLOCK), F32),
            pltpu.VMEM((8, BLOCK), F32),
        ],
        compiler_params=pltpu.CompilerParams(vmem_limit_bytes=48 << 20),
        cost_estimate=pl.CostEstimate(
            flops=16 * pairs * head_dim, bytes_accessed=rows * width * 12, transcendentals=pairs
        ),
    )(qkv, place, low, high)


def backward_kernel(
    devices, pre, tok, heads, head_dim,
    qkv_ref, do_ref, ot_ref, lse_ref, place_ref, low_ref, high_ref,
    out_ref,
    q_s, k_s, v_s, do_s, kt_s, dk_s, dv_s, dqt_s,
):
    width = heads * head_dim
    scale = 1.0 / math.sqrt(head_dim)
    blocks = devices * (pre + tok) // BLOCK
    for src, dst, cnt in row_pieces(devices, pre, tok):
        q_s[dst : dst + cnt, :] = qkv_ref[src : src + cnt, 0:width]
        k_s[dst : dst + cnt, :] = qkv_ref[src : src + cnt, width : 2 * width]
        v_s[dst : dst + cnt, :] = qkv_ref[src : src + cnt, 2 * width : 3 * width]
        do_s[dst : dst + cnt, :] = do_ref[src : src + cnt, :]
    for b in range(blocks):
        rows = slice(b * BLOCK, (b + 1) * BLOCK)
        kt_s[:, rows] = k_s[rows, :].astype(F32).T.astype(BF16)
    dk_s[...] = jnp.zeros_like(dk_s)
    dv_s[...] = jnp.zeros_like(dv_s)
    lane = lax.broadcasted_iota(jnp.int32, (BLOCK, width), 1) // head_dim

    def query_block(i, carry):
        qs = pl.ds(pl.multiple_of(i * BLOCK, BLOCK), BLOCK)
        q = q_s[qs, :]
        do = do_s[qs, :]
        qh = [jnp.where(lane == h, q, jnp.zeros_like(q)) for h in range(heads)]
        doh = [jnp.where(lane == h, do, jnp.zeros_like(do)) for h in range(heads)]
        low = low_ref[:, qs]
        high = high_ref[:, qs]
        prod = do.astype(F32).T * ot_ref[:, qs]
        delta = [
            jnp.sum(prod[h * head_dim : (h + 1) * head_dim, :], axis=0, keepdims=True)
            for h in range(heads)
        ]
        lse = [lse_ref[h : h + 1, qs] for h in range(heads)]
        dqt_s[...] = jnp.zeros_like(dqt_s)

        def key_block(j, inner):
            ks = pl.ds(pl.multiple_of(j * BLOCK, BLOCK), BLOCK)
            k = k_s[ks, :]
            v = v_s[ks, :]
            bias = jnp.where(block_mask(place_ref[ks, :], low, high), 0.0, NEGATIVE)
            dk = None
            dv = None
            for h in range(heads):
                s = contract(k, qh[h], 1, 1)
                dp = contract(v, doh[h], 1, 1)
                p = jnp.exp(s + bias - lse[h])
                p_low = p.astype(BF16)
                ds = (p * (dp - delta[h])).astype(BF16)
                dv_h = contract(p_low, doh[h], 1, 0)
                dk_h = contract(ds, qh[h], 1, 0)
                dv = dv_h if dv is None else dv + dv_h
                dk = dk_h if dk is None else dk + dk_h
                hs = slice(h * head_dim, (h + 1) * head_dim)
                dqt_s[hs, :] += contract(kt_s[hs, ks], ds, 1, 0)
            dk_s[ks, :] += dk
            dv_s[ks, :] += dv
            return inner

        lax.fori_loop(0, i + 1, key_block, 0)
        q_s[qs, :] = (dqt_s[...] * scale).T.astype(BF16)
        return carry

    lax.fori_loop(0, blocks, query_block, 0)
    for src, dst, cnt in row_pieces(devices, pre, tok):
        out_ref[src : src + cnt, 0:width] = q_s[dst : dst + cnt, :]
        out_ref[src : src + cnt, width : 2 * width] = dk_s[dst : dst + cnt, :].astype(BF16)
        out_ref[src : src + cnt, 2 * width : 3 * width] = dv_s[dst : dst + cnt, :].astype(BF16)


def attention_backward(qkv, do, ot, lse, place, low, high, devices, pre, tok, heads, head_dim):
    width = heads * head_dim
    rows = devices * (pre + tok)
    vmem = pl.BlockSpec(memory_space=pltpu.VMEM)
    pairs = rows * rows // 2 * heads
    low_rows = pltpu.VMEM((rows, width), BF16)
    return pl.pallas_call(
        functools.partial(backward_kernel, devices, pre, tok, heads, head_dim),
        out_shape=jax.ShapeDtypeStruct((rows, 3 * width), BF16),
        in_specs=[vmem] * 7,
        out_specs=vmem,
        scratch_shapes=[
            low_rows,
            low_rows,
            low_rows,
            low_rows,
            pltpu.VMEM((width, rows), BF16),
            pltpu.VMEM((rows, width), F32),
            pltpu.VMEM((rows, width), F32),
            pltpu.VMEM((width, BLOCK), F32),
        ],
        compiler_params=pltpu.CompilerParams(vmem_limit_bytes=56 << 20),
        cost_estimate=pl.CostEstimate(
            flops=40 * pairs * head_dim, bytes_accessed=rows * width * 20, transcendentals=pairs
        ),
    )(qkv, do, ot, lse, place, low, high)


def slot_labels(lengths, devices, pre, tok, real):
    slot = jnp.arange(devices * pre, dtype=jnp.int32)
    inside = slot % pre
    place = (slot // pre) * real + inside - devices * real
    is_real = inside < real
    t = jnp.arange(devices * tok, dtype=jnp.int32)
    ends = jnp.cumsum(lengths)
    start = jnp.max(jnp.where(ends[None, :] <= t[:, None], ends[None, :], 0), axis=1)
    places = jnp.concatenate([jnp.where(is_real, place, FAR), t])
    high = jnp.concatenate([jnp.where(is_real, place, -1), t])
    low = jnp.concatenate([jnp.full((devices * pre,), FAR, jnp.int32), start])
    return places[:, None], low[None, :], high[None, :]


def normalize(values):
    center = values - jnp.mean(values, axis=-1, keepdims=True)
    spread = jnp.mean(center * center, axis=-1, keepdims=True)
    inverse = lax.rsqrt(spread + EPS)
    return center * inverse, inverse


def norm_backward(grad, hat, inverse, gain):
    e = grad * gain
    mean_e = jnp.mean(e, axis=-1, keepdims=True)
    mean_eh = jnp.mean(e * hat, axis=-1, keepdims=True)
    return inverse * (e - mean_e - hat * mean_eh)


def gelu_parts(values):
    cdf = 0.5 * (1.0 + lax.erf(values * (1.0 / math.sqrt(2.0))))
    return cdf


def pick(array, index, axis):
    return lax.dynamic_index_in_dim(array, index, axis, keepdims=False)


def build(n_batch, n_seq):
    n_z = n_seq // 2
    n_dev = n_batch * n_seq
    groups = n_dev // 4
    size_of = {"batch": n_batch, "seq": n_seq}

    def bits_of(n):
        bits = []
        bit = 1
        while bit < n:
            bits.append(bit)
            bit *= 2
        return bits

    batch_bits = [("batch", bit) for bit in bits_of(n_batch)]
    quad_bits = [("seq", 1), ("seq", 2)]
    far_bits = [("seq", bit) for bit in bits_of(n_seq) if bit >= 4]
    group_bits = list(reversed(batch_bits)) + list(reversed(far_bits))
    all_bits = list(reversed(batch_bits)) + [("seq", bit) for bit in reversed(bits_of(n_seq))]

    def swap(array, which):
        axis, bit = which
        return lax.ppermute(array, axis, [(i, i ^ bit) for i in range(size_of[axis])])

    def side(which):
        axis, bit = which
        return (lax.axis_index(axis) // bit) % 2

    def shift(array, distance):
        pairs = [
            (z * 2 + c, ((z + distance) % n_z) * 2 + c) for z in range(n_z) for c in range(2)
        ]
        return lax.ppermute(array, "seq", pairs)

    def step_right(array, first, last):
        pairs = [(z * 2 + c, z * 2 + 2 + c) for z in range(first, last) for c in range(2)]
        return lax.ppermute(array, "seq", pairs)

    def step_left(array, first, last):
        pairs = [(z * 2 + c, z * 2 - 2 + c) for z in range(first, last) for c in range(2)]
        return lax.ppermute(array, "seq", pairs)

    def join(mine, other, which, axis):
        first = side(which) == 0
        return jnp.where(
            first, jnp.stack([mine, other], axis), jnp.stack([other, mine], axis)
        )

    def gather_bits(array, order, ranked):
        taken = []
        current = array
        shape = array.shape
        for which in order:
            other = swap(current, which)
            rank = ranked.index(which)
            place = sum(1 for t in taken if ranked.index(t) < rank)
            current = join(current, other, which, place)
            taken.append(which)
        return current.reshape((2 ** len(order),) + shape)

    def scatter_bits(array, order, ranked):
        shape = array.shape[1:]
        current = array.reshape((2,) * len(ranked) + shape)
        left = list(ranked)
        for which in order:
            place = left.index(which)
            mine = side(which)
            away = pick(current, 1 - mine, place).astype(BF16)
            keep = pick(current, mine, place).astype(F32)
            current = keep + swap(away, which).astype(F32)
            left.remove(which)
        return current

    def gather_pieces(block, order, ranked):
        pieces = [(frozenset(), block)]
        for which in order:
            pieces = pieces + [(took | {which}, swap(piece, which)) for took, piece in pieces]
        placed = []
        for took, piece in pieces:
            index = 0
            for which in ranked:
                here = side(which)
                index = index * 2 + ((1 - here) if which in took else here)
            placed.append((index, piece))
        return placed

    def assemble(placed):
        rows = placed[0][1].shape[0]
        out = jnp.zeros((rows * len(placed),) + placed[0][1].shape[1:], placed[0][1].dtype)
        for index, piece in placed:
            out = lax.dynamic_update_slice_in_dim(out, piece, index * rows, 0)
        return out

    def body(
        tokens, prefix, seg_lengths, attn_gain, attn_shift, query_weight, key_weight, value_weight,
        query_bias, value_bias, output_weight, output_bias, mlp_gain, mlp_shift, up_weight, up_bias,
        down_weight, down_bias, cot_tokens, cot_prefix,
    ):
        tok = tokens.shape[1]
        real = prefix.shape[1]
        pre = -(-real // 16) * 16
        width = pre + tok
        model = tokens.shape[2]
        heads = HEADS // n_seq
        span = heads * HEAD_DIM
        part = model // n_dev
        unit = up_bias.shape[0]
        hidden_here = groups * unit
        s_here = lax.axis_index("seq")
        z_here = s_here // 2
        c_here = s_here % 2
        core = ("seq", 1)
        near = ("seq", 2)
        lengths = seg_lengths[0]

        def rows_of(pre_part, tok_part):
            return jnp.concatenate([jnp.pad(pre_part, ((0, pre - real), (0, 0))), tok_part], axis=0)

        own = rows_of(prefix[0], tokens[0])
        cot = rows_of(cot_prefix[0], cot_tokens[0])
        row = jnp.arange(width, dtype=jnp.int32)
        position = row - pre + s_here * tok
        valid = jnp.where(row < pre, row < real, position < jnp.sum(lengths))
        validity = valid.astype(F32)[:, None]

        small = jnp.concatenate(
            [attn_gain, attn_shift, query_bias, value_bias, output_bias, mlp_gain, mlp_shift, down_bias, up_bias]
        )[None]
        small = gather_bits(small, list(reversed(all_bits)), all_bits).reshape(n_dev, -1)
        vectors = [small[:, n * part : (n + 1) * part].reshape(model).astype(F32) for n in range(8)]
        gain_a, shift_a, bias_q, bias_v, bias_o, gain_m, shift_m, bias_down = vectors
        bias_up = pick(small[:, 8 * part :].reshape(groups, 4, unit), s_here % 4, 1)
        bias_up = bias_up.reshape(hidden_here).astype(F32)

        stacked = jnp.stack([query_weight, key_weight, value_weight], axis=1)
        stacked = stacked.reshape(part, 3, n_z, 2, span).transpose(2, 3, 0, 1, 4)
        stacked = stacked.reshape(n_z, 2, part, 3 * span)
        mixed = join(pick(stacked, c_here, 1), swap(pick(stacked, 1 - c_here, 1), core), core, 1)
        mixed = mixed.reshape(n_z, 2 * part, 3 * span)
        placed = [(z_here, pick(mixed, z_here, 0))]
        for d in range(1, n_z):
            piece = shift(pick(mixed, (z_here + d) % n_z, 0), d)
            placed.append(((z_here - d) % n_z, piece))
        local = assemble(placed)
        half = local.shape[0] // 2
        ranked_batch = list(reversed(batch_bits))
        weight_qkv = jnp.stack(
            [
                gather_bits(local[:half], batch_bits, ranked_batch),
                gather_bits(local[half:], ranked_batch, ranked_batch),
            ],
            axis=1,
        ).reshape(model, 3 * span)

        gathered = [own]
        from_left = []
        from_right = []
        moving_right = own
        moving_left = own
        for k in range(1, n_z):
            moving_right = step_right(moving_right, k - 1, n_z - 1)
            moving_left = step_left(moving_left, 1, n_z - k + 1)
            from_left.append(moving_right)
            from_right.append(moving_left)
        for k in range(1, n_z):
            gathered.append(jnp.where(z_here >= k, from_left[k - 1], from_right[n_z - k - 1]))

        bias_qkv = jnp.concatenate(
            [
                lax.dynamic_slice_in_dim(bias_q, s_here * span, span, 0),
                jnp.zeros((span,), F32),
                lax.dynamic_slice_in_dim(bias_v, s_here * span, span, 0),
            ]
        )
        factor = jnp.concatenate(
            [jnp.full((span,), 1.0 / math.sqrt(HEAD_DIM), F32), jnp.ones((2 * span,), F32)]
        )
        normed = jnp.zeros((n_z * 2 * width, model), BF16)
        qkv = jnp.zeros((n_z * 2 * width, 3 * span), BF16)
        for k in range(n_z):
            chunk = join(gathered[k], swap(gathered[k], core), core, 0).reshape(2 * width, model)
            hat, unused = normalize(chunk.astype(F32))
            chunk = (hat * gain_a + shift_a).astype(BF16)
            first = ((z_here - k) % n_z) * 2 * width
            normed = lax.dynamic_update_slice_in_dim(normed, chunk, first, 0)
            result = (contract(chunk, weight_qkv, 1, 0) + bias_qkv).astype(BF16).astype(F32) * factor
            qkv = lax.dynamic_update_slice_in_dim(qkv, result.astype(BF16), first, 0)

        places, low, high = slot_labels(lengths, n_seq, pre, tok, real)
        attended, attended_t, log_total = attention_forward(
            qkv, places, low, high, n_seq, pre, tok, heads, HEAD_DIM
        )

        blocks = attended.reshape(n_z, 2, width, span)
        ours = join(pick(blocks, c_here, 1), swap(pick(blocks, 1 - c_here, 1), core), core, 2)
        ours = ours.reshape(n_z, width, 2 * span)
        mixed_low = jnp.zeros((width, model), BF16)
        mixed_low = lax.dynamic_update_slice_in_dim(
            mixed_low, pick(ours, z_here, 0), z_here * 2 * span, 1
        )
        for d in range(1, n_z):
            piece = shift(pick(ours, (z_here + d) % n_z, 0), d)
            mixed_low = lax.dynamic_update_slice_in_dim(
                mixed_low, piece, ((z_here - d) % n_z) * 2 * span, 1
            )

        order_o = [near] + far_bits
        half_model = model // 2
        weight_o = []
        for n, batch_order in enumerate((batch_bits, ranked_batch)):
            columns = output_weight[:, n * half_model : (n + 1) * half_model]
            gathered_o = gather_bits(columns, order_o + batch_order + [core], all_bits)
            weight_o.append(gathered_o.reshape(model, half_model))
        weight_o = jnp.concatenate(weight_o, axis=1)

        rows_in = own.astype(F32)
        branch = contract(mixed_low, weight_o, 1, 0) + bias_o
        resid = rows_in + validity * branch
        hat_m, inverse_m = normalize(resid)
        normed_m_own = (hat_m * gain_m + shift_m).astype(BF16)

        shaped = up_weight.reshape(part, groups, 2, 2, unit)
        shaped = join(pick(shaped, c_here, 3), swap(pick(shaped, 1 - c_here, 3), core), core, 0)
        near_here = side(near)
        shaped = join(pick(shaped, near_here, 3), swap(pick(shaped, 1 - near_here, 3), near), near, 0)
        up_block = shaped.reshape(4 * part, hidden_here)
        order_up = far_bits + batch_bits
        order_down = far_bits + list(reversed(batch_bits))
        weight_up = assemble(gather_pieces(up_block, order_up, group_bits))
        weight_down = assemble(gather_pieces(down_weight, order_down, group_bits))

        def quad_gather(array):
            other = swap(array, near)
            both = join(array, other, near, 0)
            return join(both, swap(both, core), core, 1).reshape((4 * width,) + array.shape[1:])

        def quad_scatter(array):
            shaped = array.reshape(2, 2, width, model)
            mine = pick(shaped, c_here, 1)
            both = mine + swap(pick(shaped, 1 - c_here, 1).astype(BF16), core).astype(F32)
            away = pick(both, 1 - near_here, 0).astype(BF16)
            return pick(both, near_here, 0) + swap(away, near).astype(F32)

        cot_rows = cot.astype(F32)
        mlp_out_grad = (validity * cot_rows).astype(BF16)
        mlp_out_grad_quad = quad_gather(mlp_out_grad)
        normed_m = quad_gather(normed_m_own)

        hidden_pre = contract(normed_m, weight_up, 1, 0) + bias_up
        cdf = 0.5 * (1.0 + lax.erf(hidden_pre * (1.0 / math.sqrt(2.0))))
        hidden = (hidden_pre * cdf).astype(BF16)
        slope = cdf + hidden_pre * jnp.exp(-0.5 * hidden_pre * hidden_pre) * (
            1.0 / math.sqrt(2.0 * math.pi)
        )
        hidden_grad = contract(mlp_out_grad_quad, weight_down, 1, 1)
        pre_grad = (hidden_grad * slope).astype(BF16)
        normed_grad = quad_scatter(contract(pre_grad, weight_up, 1, 1))
        final = resid + validity * (quad_scatter(contract(hidden, weight_down, 1, 0)) + bias_down)
        out_rows = final.astype(BF16)
        grad_up_bias = jnp.sum(pre_grad.astype(F32), axis=0)
        grad_down_bias = jnp.sum(mlp_out_grad.astype(F32), axis=0)

        def group_scatter(left, right, order):
            first = order[0]
            place = group_bits.index(first)
            shaped = left.reshape((left.shape[0],) + (2,) * len(group_bits) + (-1,))
            rest = [which for which in group_bits if which != first]
            halves = []
            for which_side in (1 - side(first), side(first)):
                columns = pick(shaped, which_side, 1 + place).reshape(left.shape[0], -1)
                halves.append(contract(columns, right, 0, 0))
            current = halves[1] + swap(halves[0].astype(BF16), first).astype(F32)
            current = current.reshape((2 ** len(rest), -1, right.shape[1]))
            return scatter_bits(current, order[1:], rest)

        grad_down = group_scatter(hidden, mlp_out_grad_quad, list(reversed(order_down)))
        grad_up = group_scatter(normed_m, pre_grad, list(reversed(order_up)))
        grad_up = grad_up.reshape(2, 2, part, hidden_here)
        grad_up = join(
            pick(grad_up, near_here, 0).astype(BF16),
            swap(pick(grad_up, 1 - near_here, 0).astype(BF16), near),
            near,
            0,
        )
        grad_up = join(pick(grad_up, c_here, 1), swap(pick(grad_up, 1 - c_here, 1), core), core, 1)
        grad_up = grad_up.reshape(4, part, groups, unit).transpose(1, 2, 0, 3)
        grad_up = grad_up.reshape(part, n_dev * unit).astype(F32)

        grad_gain_m = jnp.sum(normed_grad * hat_m, axis=0)
        grad_shift_m = jnp.sum(normed_grad, axis=0)
        resid_grad = cot_rows + norm_backward(normed_grad, hat_m, inverse_m, gain_m)

        branch_grad = (validity * resid_grad).astype(BF16)
        grad_out_bias = jnp.sum(branch_grad.astype(F32), axis=0)
        mixed_grad = contract(branch_grad, weight_o, 1, 1).astype(BF16)
        columns = mixed_grad.reshape(width, n_z, 2 * span)
        rows_grad = jnp.zeros((n_z, width, 2 * span), BF16)
        rows_grad = lax.dynamic_update_slice_in_dim(
            rows_grad, pick(columns, z_here, 1)[None], z_here, 0
        )
        for d in range(1, n_z):
            piece = shift(pick(columns, (z_here + d) % n_z, 1), d)
            rows_grad = lax.dynamic_update_slice_in_dim(
                rows_grad, piece[None], (z_here - d) % n_z, 0
            )
        rows_grad = rows_grad.reshape(n_z, width, 2, span)
        rows_grad = join(
            pick(rows_grad, c_here, 2), swap(pick(rows_grad, 1 - c_here, 2), core), core, 1
        )
        rows_grad = rows_grad.reshape(n_z * 2 * width, span)

        grad_out = contract(mixed_low, branch_grad, 0, 0).reshape(n_dev, part, model)
        ranked_pairs = [which for which in all_bits if which != core]
        grad_out = grad_out.reshape(n_dev // 2, 2, part, model)
        grad_out = pick(grad_out, c_here, 1) + swap(
            pick(grad_out, 1 - c_here, 1).astype(BF16), core
        ).astype(F32)
        grad_out = jnp.concatenate(
            [
                scatter_bits(
                    grad_out[:, :, n * half_model : (n + 1) * half_model],
                    batch_order + far_bits + [near],
                    ranked_pairs,
                )
                for n, batch_order in enumerate((batch_bits, ranked_batch))
            ],
            axis=1,
        )

        qkv_grad = attention_backward(
            qkv, rows_grad, attended_t, log_total, places, low, high, n_seq, pre, tok, heads, HEAD_DIM
        )
        bias_sums = jnp.sum(qkv_grad.astype(F32), axis=0)

        def rows_for(r):
            first = ((z_here + r) % n_z) * 2 * width
            rows = lax.dynamic_slice_in_dim(qkv_grad, first, 2 * width, 0)
            share = contract(rows, weight_qkv, 1, 1).reshape(2, width, model)
            away = swap(pick(share, 1 - c_here, 0).astype(BF16), core)
            return pick(share, c_here, 0) + away.astype(F32)

        chunks = [rows_for(r) for r in range(n_z)]
        right = None
        left = None
        for k in range(1, n_z):
            going = jnp.where(z_here + n_z - k < n_z, chunks[n_z - k], 0.0)
            right = going if right is None else going + right.astype(F32)
            right = step_right(right.astype(BF16), 0, k)
            going = jnp.where(z_here - (n_z - k) >= 0, chunks[k], 0.0)
            left = going if left is None else going + left.astype(F32)
            left = step_left(left.astype(BF16), n_z - k, n_z)
        normed_back = chunks[0] + right.astype(F32) + left.astype(F32)

        grad_qkv = contract(normed, qkv_grad, 0, 0).reshape(n_batch, 2, -1, 3 * span)
        grad_qkv = jnp.concatenate(
            [
                scatter_bits(grad_qkv[:, n], batch_order, ranked_batch)
                for n, batch_order in enumerate((ranked_batch, batch_bits))
            ],
            axis=0,
        ).astype(BF16)
        grad_qkv = grad_qkv.reshape(n_z, 2, part, 3 * span)
        grad_qkv = join(
            pick(grad_qkv, c_here, 1), swap(pick(grad_qkv, 1 - c_here, 1), core), core, 1
        )
        shares = jnp.zeros((n_z, 2, part, 3 * span), BF16)
        shares = lax.dynamic_update_slice_in_dim(shares, pick(grad_qkv, z_here, 0)[None], z_here, 0)
        for d in range(1, n_z):
            piece = shift(pick(grad_qkv, (z_here + d) % n_z, 0), d)
            shares = lax.dynamic_update_slice_in_dim(shares, piece[None], (z_here - d) % n_z, 0)
        shares = shares.reshape(n_seq, part, 3, span).transpose(2, 1, 0, 3)
        shares = shares.reshape(3, part, model).astype(F32)

        hat_a, inverse_a = normalize(rows_in)
        grad_gain_a = jnp.sum(normed_back * hat_a, axis=0)
        grad_shift_a = jnp.sum(normed_back, axis=0)
        input_grad = resid_grad + norm_backward(normed_back, hat_a, inverse_a, gain_a)

        zero = jnp.zeros((model,), F32)
        grad_bias_q = lax.dynamic_update_slice_in_dim(zero, bias_sums[:span], s_here * span, 0)
        grad_bias_v = lax.dynamic_update_slice_in_dim(zero, bias_sums[2 * span :], s_here * span, 0)
        full_up_bias = lax.dynamic_update_slice_in_dim(
            jnp.zeros((groups, 4, unit), F32), grad_up_bias.reshape(groups, 1, unit), s_here % 4, 1
        ).reshape(n_dev, unit)
        sums = jnp.concatenate(
            [
                vector.reshape(n_dev, part)
                for vector in (
                    grad_gain_a, grad_shift_a, grad_bias_q, grad_bias_v, grad_out_bias,
                    grad_gain_m, grad_shift_m, grad_down_bias,
                )
            ]
            + [full_up_bias],
            axis=1,
        )
        current = sums.reshape((2,) * len(all_bits) + (sums.shape[1],))
        for which in all_bits:
            mine = side(which)
            current = pick(current, mine, 0) + swap(pick(current, 1 - mine, 0), which)
        small_grads = [current[n * part : (n + 1) * part] for n in range(8)]

        return (
            out_rows[pre:][None],
            out_rows[:real][None],
            input_grad[pre:][None],
            input_grad[:real][None],
            small_grads[0],
            small_grads[1],
            shares[0],
            shares[1],
            shares[2],
            small_grads[2],
            small_grads[3],
            grad_out,
            small_grads[4],
            small_grads[5],
            small_grads[6],
            grad_up,
            current[8 * part :],
            grad_down,
            small_grads[7],
        )

    return body


def solution(mesh):
    rows = P("batch", "seq", None)
    vector = P(("batch", "seq"))
    matrix = P(("batch", "seq"), None)
    return jax.shard_map(
        build(mesh.shape["batch"], mesh.shape["seq"]),
        mesh=mesh,
        in_specs=(
            rows, rows, P("batch", None), vector, vector, matrix, matrix, matrix, vector, vector,
            matrix, vector, vector, vector, matrix, vector, matrix, vector, rows, rows,
        ),
        out_specs=(
            rows, rows, rows, rows, vector, vector, matrix, matrix, matrix, vector, vector, matrix,
            vector, vector, vector, matrix, vector, matrix, vector,
        ),
        check_vma=False,
    )
```

time: 3840 us -> 1390 us (0.36)
  waiting for transfers between devices: 2700 us -> 488 us
  matrix products: 640 us -> 159 us
  starting transfers between devices: 0.68 us -> 164 us
  Pallas kernels: 0 us -> 148 us
  blocking collectives: 112 us -> 0 us
  other arithmetic: 118 us -> 172 us
    reduce_scatter x6 -> x0, waiting for transfers between devices: 2150 us -> none  [the longest x1 710 us: body(): lax.psum_scatter(grad_up, ('batch', 'seq'), scatter_dimension=0, tiled=True)]
    all_gather x10 -> x0, waiting for transfers between devices: 542 us -> none  [the longest x1 156 us: body(): lax.all_gather(down_weight, ('batch', 'seq'), axis=0, tiled=True)]
    ppermute x0 -> x105, waiting for transfers between devices: none -> 488 us  [the longest x81 374 us: swap(): lax.ppermute(array, axis, [(i, i ^ bit) for i in range(size_of[axis])])]
    dot_general x46 -> x20, matrix products: 640 us -> 159 us  [contract(): lax.dot_general(left, right, (((left_dim,), (right_dim,)), ((), ())), pre...]
    ppermute x0 -> x105, starting transfers between devices: none -> 164 us  [the longest x81 96.7 us: swap(): lax.ppermute(array, axis, [(i, i ^ bit) for i in range(size_of[axis])])]
    pallas_call x0 -> x2, Pallas kernels: none -> 148 us  [the longest x1 83.7 us: attention_backward(): pl.pallas_call(functools.partial(backward_kernel, devices, pre, tok, head...]
    dynamic_slice x20 -> x14, local copies, waits for them, and re-layouts: 106 us -> 24.7 us  [the longest x11 23 us: pick(): return lax.dynamic_index_in_dim(array, index, axis, keepdims=False)]
    all_gather x3 -> x0, blocking collectives: 69 us -> none  [the longest x1 39.9 us: body(): lax.all_gather(up_bias, ('batch', 'seq'), axis=0, tiled=True)]
  transfers between devices with their start and end apart: 17 -> 105, of which waited for: 13 -> 42; matrix products, arithmetic and copies ran while one was open for 17% -> 34% of each run, Pallas kernels for 0% -> 11%
where the time goes in v1:
time: 1390 us; the launch traced here: 1380 us
  waiting for transfers between devices  488 us (35%)
  local copies, waits for them, and re-layouts  244 us (18%)
  other arithmetic  172 us (12%)
  starting transfers between devices  164 us (12%)
  matrix products  159 us (11%)
  Pallas kernels  148 us (11%)
    ppermute x81, waiting for transfers between devices, swap(): lax.ppermute(array, axis, [(i, i ^ bit) for i in range(size_of[axis])])  374 us
    dot_general x20, matrix products, contract(): lax.dot_general(left, right, (((left_dim,), (right_dim,)), ((), ())), pre...  159 us
    ppermute x81, starting transfers between devices, swap(): lax.ppermute(array, axis, [(i, i ^ bit) for i in range(size_of[axis])])  96.7 us
    pallas_call x1, Pallas kernels, attention_backward(): pl.pallas_call(functools.partial(backward_kernel, devices, pre, tok, head...  83.7 us
    ppermute x12, waiting for transfers between devices, shift(): return lax.ppermute(array, 'seq', pairs)  64.7 us
    pallas_call x1, Pallas kernels, attention_forward(): pl.pallas_call(functools.partial(forward_kernel, devices, pre, tok, heads...  64.7 us
    select_n x42, other arithmetic, join(): jnp.where(first, jnp.stack([mine, other], axis), jnp.stack([other, mine],...  55.1 us
    unnamed x231, local copies, waits for them, and re-layouts  37.2 us
  transfers between devices with their start and end apart: 105, of which 42 were waited for; matrix products, arithmetic and copies ran while one was open for 34% of the time, Pallas kernels for 11%

profile of v1, /device:TPU:0, one launch (start us, length us, event | category | flops | bytes accessed | tf_op | source)
XLA Modules:
  0.0 1379.1 jit_solution(7049228477437648948)
XLA Ops:
  49.1 19.4 %collective-permute-done.3 = bf16[2,2,1,768]{3,1,0,2:T(2,128)(2,1)S(1)} collective-permute-done((bf16[2,2,1,768]{3,1,0,2:T(2,128)(2,1)S(1)}, bf16[2,2,1,768]{3,1,0,2:T(2,128)(2,1)S(1)}, u32[]{:S(2)}, u32[]{:S(2)}) %collective-permute-start.3) | collective-permute-done | bytes 6176 | tf_op jit(solution)/shard_map/ppermute | solution.py:286
  148.3 12.8 collective-permute-done.12
  207.8 17.5 %collective-permute-done.13 = bf16[2,256,768]{2,1,0:T(8,128)(2,1)} collective-permute-done((bf16[2,256,768]{2,1,0:T(8,128)(2,1)}, bf16[2,256,768]{2,1,0:T(8,128)(2,1)}, u32[]{:S(2)}, u32[]{:S(2)}) %collective-permute-start.13) | collective-permute-done | bytes 786464 | tf_op jit(solution)/shard_map/ppermute | solution.py:286
  259.9 46.7 %collective-permute-done.41 = bf16[256,2048]{1,0:T(8,128)(2,1)S(1)} collective-permute-done((bf16[256,2048]{1,0:T(8,128)(2,1)S(1)}, bf16[256,2048]{1,0:T(8,128)(2,1)S(1)}, u32[]{:S(2)}, u32[]{:S(2)}) %collective-permute-start.41) | collective-permute-done | bytes 1048608 | tf_op jit(solution)/shard_map/ppermute | solution.py:286
  315.9 13.9 %collective-permute-done.44 = bf16[256,2048]{1,0:T(8,128)(2,1)S(1)} collective-permute-done((bf16[256,2048]{1,0:T(8,128)(2,1)S(1)}, bf16[256,2048]{1,0:T(8,128)(2,1)S(1)}, u32[]{:S(2)}, u32[]{:S(2)}) %collective-permute-start.44) | collective-permute-done | bytes 1048608 | tf_op jit(solution)/shard_map/ppermute | solution.py:286
  338.1 17.8 %collective-permute-done.45 = bf16[256,2048]{1,0:T(8,128)(2,1)S(1)} collective-permute-done((bf16[256,2048]{1,0:T(8,128)(2,1)S(1)}, bf16[256,2048]{1,0:T(8,128)(2,1)S(1)}, u32[]{:S(2)}, u32[]{:S(2)}) %collective-permute-start.45) | collective-permute-done | bytes 1048608 | tf_op jit(solution)/shard_map/ppermute | solution.py:286
  376.2 28.5 %collective-permute-done.17 = bf16[320,2048]{1,0:T(8,128)(2,1)S(1)} collective-permute-done((bf16[320,2048]{1,0:T(8,128)(2,1)S(1)}, bf16[320,2048]{1,0:T(8,128)(2,1)S(1)}, u32[]{:S(2)}, u32[]{:S(2)}) %collective-permute-start.17) | collective-permute-done | bytes 1310752 | tf_op jit(solution)/shard_map/ppermute | solution.py:304
  430.1 64.7 %shard_map.339 = (bf16[2560,256]{1,0:T(8,128)(2,1)S(1)}, f32[256,2560]{1,0:T(8,128)S(1)}, f32[8,2560]{1,0:T(8,128)S(1)}) custom-call(bf16[2560,768]{1,0:T(8,128)(2,1)} %copy-done.59, s32[2560,1]{1,0:T(8,128)S(1)} %broadcast_in_dim.164.place_ref, s32[1,2560]{1,0:T(1,128)S(1)} %broadcast_in_dim.145.low_ref, s32[1,2560]{1,0:T(1,128)S(1)} %broadcast_in_dim.146.high_ref), custom_call_target="tpu_custom_call" | custom-call | flops 13421772800 | bytes 7864320 | tf_op jit(solution)/shard_map/pallas_call | solution.py:104
  524.7 13.1 collective-permute-done.25
  566.0 12.0 collective-permute-done.37
  600.3 20.0 %multiply_convert_fusion = (bf16[1280,2048]{1,0:T(8,128)(2,1)}, f32[1280,2048]{1,0:T(8,128)}) fusion(f32[2048]{0:T(1024)S(1)} %bitcast.688, bf16[1280,2048]{1,0:T(8,128)(2,1)S(1)} %bitcast.559, bf16[2048,2048]{1,0:T(8,128)(2,1)} %constant_dynamic-update-slice_fusion.12), kind=kOutput, calls=%fused_computation.8 | convolution fusion | flops 10753146880 | bytes 29368320 | tf_op jit(solution)/shard_map/dot_general | solution.py:22
  620.3 20.3 %convert_reduce_fusion = (f32[2048]{0:T(1024)S(1)}, bf16[1280,2048]{1,0:T(8,128)(2,1)}) fusion(f32[1280,2048]{1,0:T(8,128)} %get-tuple-element.211, f32[2048]{0:T(1024)S(1)} %bitcast.689, bf16[1280,2048]{1,0:T(8,128)(2,1)S(1)} %bitcast.555, bf16[2048,2048]{1,0:T(8,128)(2,1)} %constant_dynamic-update-slice_fusion.4), kind=kOutput, calls=%fused_computation.7 | convolution fusion | flops 10771494912 | bytes 29376512 | tf_op jit(solution)/shard_map/dot_general | solution.py:22
  640.7 15.2 %fusion.123 = f32[1280,2048]{1,0:T(8,128)S(1)} fusion(bf16[1280,2048]{1,0:T(8,128)(2,1)} %get-tuple-element.213, bf16[2048,2048]{1,0:T(8,128)(2,1)} %constant_dynamic-update-slice_fusion.12), kind=kOutput, calls=%fused_computation.432 | convolution fusion | flops 10737418240 | bytes 24117248 | tf_op jit(solution)/shard_map/dot_general | solution.py:22
  663.1 16.2 %fusion.122 = f32[1280,2048]{1,0:T(8,128)} fusion(bf16[1280,2048]{1,0:T(8,128)(2,1)S(1)} %copy-done.45, bf16[2048,2048]{1,0:T(8,128)(2,1)} %constant_dynamic-update-slice_fusion.4), kind=kOutput, calls=%fused_computation.431 | convolution fusion | flops 10737418240 | bytes 24117248 | tf_op jit(solution)/shard_map/dot_general | solution.py:22
  780.2 23.4 %collective-permute-done.56 = bf16[320,2048]{1,0:T(8,128)(2,1)} collective-permute-done((bf16[320,2048]{1,0:T(8,128)(2,1)}, bf16[320,2048]{1,0:T(8,128)(2,1)}, u32[]{:S(2)}, u32[]{:S(2)}) %collective-permute-start.56) | collective-permute-done | bytes 1310752 | tf_op jit(solution)/shard_map/ppermute | solution.py:286
  881.5 83.7 %shard_map.340 = bf16[2560,768]{1,0:T(8,128)(2,1)} custom-call(bf16[2560,768]{1,0:T(8,128)(2,1)} %copy-done.59, bf16[2560,256]{1,0:T(8,128)(2,1)} %bitcast.651, f32[256,2560]{1,0:T(8,128)} %copy-done.3, f32[8,2560]{1,0:T(8,128)} %copy-done.4, s32[2560,1]{1,0:T(8,128)} %copy-done, s32[1,2560]{1,0:T(1,128)} %copy-done.1, s32[1,2560]{1,0:T(1,128)} %copy-done.2), custom_call_target="tpu_custom_call" | custom-call | flops 33554432000 | bytes 13107200 | tf_op jit(solution)/shard_map/pallas_call | solution.py:205
  1048.5 32.8 %collective-permute-done.103 = bf16[2,256,2048]{2,1,0:T(8,128)(2,1)S(1)} collective-permute-done((bf16[2,256,2048]{2,1,0:T(8,128)(2,1)S(1)}, bf16[2,256,2048]{2,1,0:T(8,128)(2,1)S(1)}, u32[]{:S(2)}, u32[]{:S(2)}) %collective-permute-start.103) | collective-permute-done | bytes 2097184 | tf_op jit(solution)/shard_map/ppermute | solution.py:286
  1088.2 21.0 %collective-permute-done.85 = bf16[2,64,768]{2,1,0:T(8,128)(2,1)S(1)} collective-permute-done((bf16[2,64,768]{2,1,0:T(8,128)(2,1)S(1)}, bf16[2,64,768]{2,1,0:T(8,128)(2,1)S(1)}, u32[]{:S(2)}, u32[]{:S(2)}) %collective-permute-start.85) | collective-permute-done | bytes 196640 | tf_op jit(solution)/shard_map/ppermute | solution.py:296
  1109.2 23.9 %collective-permute-start.86 = (bf16[2,64,768]{2,1,0:T(8,128)(2,1)S(1)}, bf16[2,64,768]{2,1,0:T(8,128)(2,1)S(1)}, u32[]{:S(2)}, u32[]{:S(2)}) collective-permute-start(bf16[2,64,768]{2,1,0:T(8,128)(2,1)S(1)} %get-tuple-element.158), channel_id=1, source_target_pairs={{0,4},{1,5},{2,6},{3,7},{4,0},{5,1},{6,2},{7,3},{8,12},{9,13},{10,... | collective-permute-start | bytes 589832 | tf_op jit(solution)/shard_map/ppermute | solution.py:296
  1165.2 27.9 %collective-permute-done.100 = bf16[2,64,2048]{2,1,0:T(8,128)(2,1)S(1)} collective-permute-done((bf16[2,64,2048]{2,1,0:T(8,128)(2,1)S(1)}, bf16[2,64,2048]{2,1,0:T(8,128)(2,1)S(1)}, u32[]{:S(2)}, u32[]{:S(2)}) %collective-permute-start.100) | collective-permute-done | bytes 524320 | tf_op jit(solution)/shard_map/ppermute | solution.py:286
  1208.2 17.4 %collective-permute-done.70 = bf16[320,2048]{1,0:T(8,128)(2,1)} collective-permute-done((bf16[320,2048]{1,0:T(8,128)(2,1)}, bf16[320,2048]{1,0:T(8,128)(2,1)}, u32[]{:S(2)}, u32[]{:S(2)}) %collective-permute-start.70) | collective-permute-done | bytes 1310752 | tf_op jit(solution)/shard_map/ppermute | solution.py:300
  1243.0 16.9 %collective-permute-done.89 = bf16[2,2,2,64,1024]{4,3,2,1,0:T(8,128)(2,1)S(1)} collective-permute-done((bf16[2,2,2,64,1024]{4,3,2,1,0:T(8,128)(2,1)S(1)}, bf16[2,2,2,64,1024]{4,3,2,1,0:T(8,128)(2,1)S(1)}, u32[]{:S(2)}, u32[]{:S(2)}) %collective-permute-start.89) | collective-permute-done | bytes 1048608 | tf_op jit(solution)/shard_map/ppermute | solution.py:286
  1297.5 25.8 %collective-permute-done.95 = bf16[2,64,1024]{2,1,0:T(8,128)(2,1)S(1)} collective-permute-done((bf16[2,64,1024]{2,1,0:T(8,128)(2,1)S(1)}, bf16[2,64,1024]{2,1,0:T(8,128)(2,1)S(1)}, u32[]{:S(2)}, u32[]{:S(2)}) %collective-permute-start.95) | collective-permute-done | bytes 262176 | tf_op jit(solution)/shard_map/ppermute | solution.py:286
  1334.7 17.8 %collective-permute-done.96 = bf16[64,1024]{1,0:T(8,128)(2,1)S(1)} collective-permute-done((bf16[64,1024]{1,0:T(8,128)(2,1)S(1)}, bf16[64,1024]{1,0:T(8,128)(2,1)S(1)}, u32[]{:S(2)}, u32[]{:S(2)}) %collective-permute-start.96) | collective-permute-done | bytes 131104 | tf_op jit(solution)/shard_map/ppermute | solution.py:286
  (765 shorter events, 766.6 us)
Async XLA Ops:
  9.4 174.8 %collective-permute-start = (bf16[320,2048]{1,0:T(8,128)(2,1)S(1)}, bf16[320,2048]{1,0:T(8,128)(2,1)}, u32[]{:S(2)}, u32[]{:S(2)}) collective-permute-start(bf16[320,2048]{1,0:T(8,128)(2,1)S(1)} %get-tuple-element.118), channel_id=1, source_target_pairs={{0,1},{1,0},{2,3},{3,2},{4,5},{5,4},{6,7},{7,6},{8,9},{9,8},{10,11... | collective-permute-start | bytes 3932168 | tf_op jit(solution)/shard_map/ppermute | solution.py:286
  15.3 96.6 %collective-permute-start.6 = (bf16[4,64,768]{2,1,0:T(8,128)(2,1)}, bf16[4,64,768]{2,1,0:T(8,128)(2,1)}, u32[]{:S(2)}, u32[]{:S(2)}) collective-permute-start(bf16[4,64,768]{2,1,0:T(8,128)(2,1)} %get-tuple-element.173), channel_id=1, source_target_pairs={{0,1},{1,0},{2,3},{3,2},{4,5},{5,4},{6,7},{7,6},{8,9},{9,8},{10,11... | collective-permute-start | bytes 1179656 | tf_op jit(solution)/shard_map/ppermute | solution.py:286
  16.7 69.0 %collective-permute-start.32 = (bf16[64,1024]{1,0:T(8,128)(2,1)}, bf16[64,1024]{1,0:T(8,128)(2,1)S(1)}, u32[]{:S(2)}, u32[]{:S(2)}) collective-permute-start(bf16[64,1024]{1,0:T(8,128)(2,1)} %get-tuple-element.178), channel_id=1, source_target_pairs={{0,2},{1,3},{2,0},{3,1},{4,6},{5,7},{6,4},{7,5},{8,10},{9,11},{10,... | collective-permute-start | bytes 393224 | tf_op jit(solution)/shard_map/ppermute | solution.py:286
  19.3 159.5 %collective-permute-start.48 = (bf16[256,2048]{1,0:T(8,128)(2,1)}, bf16[256,2048]{1,0:T(8,128)(2,1)}, u32[]{:S(2)}, u32[]{:S(2)}) collective-permute-start(bf16[256,2048]{1,0:T(8,128)(2,1)} %param.36), channel_id=1, source_target_pairs={{0,4},{1,5},{2,6},{3,7},{4,0},{5,1},{6,2},{7,3},{8,12},{9,13},{10,... | collective-permute-start | bytes 3145736 | tf_op jit(solution)/shard_map/ppermute | solution.py:286
  231.2 75.4 %collective-permute-start.41 = (bf16[256,2048]{1,0:T(8,128)(2,1)S(1)}, bf16[256,2048]{1,0:T(8,128)(2,1)S(1)}, u32[]{:S(2)}, u32[]{:S(2)}) collective-permute-start(bf16[256,2048]{1,0:T(8,128)(2,1)S(1)} %bitcast.610), channel_id=1, source_target_pairs={{0,4},{1,5},{2,6},{3,7},{4,0},{5,1},{6,2},{7,3},{8,12},{9,13},{10,... | collective-permute-start | bytes 3145736 | tf_op jit(solution)/shard_map/ppermute | solution.py:286
  236.6 70.5 %collective-permute-start.42 = (bf16[256,2048]{1,0:T(8,128)(2,1)S(1)}, bf16[256,2048]{1,0:T(8,128)(2,1)S(1)}, u32[]{:S(2)}, u32[]{:S(2)}) collective-permute-start(bf16[256,2048]{1,0:T(8,128)(2,1)S(1)} %bitcast.611), channel_id=1, source_target_pairs={{0,8},{8,0},{16,24},{24,16},{1,9},{9,1},{17,25},{25,17},{2,10},{10... | collective-permute-start | bytes 3145736 | tf_op jit(solution)/shard_map/ppermute | solution.py:286
  254.7 75.6 %collective-permute-start.19 = (bf16[320,2048]{1,0:T(8,128)(2,1)S(1)}, bf16[320,2048]{1,0:T(8,128)(2,1)S(1)}, u32[]{:S(2)}, u32[]{:S(2)}) collective-permute-start(bf16[320,2048]{1,0:T(8,128)(2,1)S(1)} %collective-permute-done.14), channel_id=1, source_target_pairs={{2,4},{3,5},{4,6},{5,7},{10,12},{11,13},{12,14},{13,15},{18,20},{1... | collective-permute-start | bytes 3932168 | tf_op jit(solution)/shard_map/ppermute | solution.py:300
  255.4 76.4 %collective-permute-start.16 = (bf16[320,2048]{1,0:T(8,128)(2,1)S(1)}, bf16[320,2048]{1,0:T(8,128)(2,1)S(1)}, u32[]{:S(2)}, u32[]{:S(2)}) collective-permute-start(bf16[320,2048]{1,0:T(8,128)(2,1)S(1)} %collective-permute-done.15), channel_id=1, source_target_pairs={{2,0},{3,1},{4,2},{5,3},{10,8},{11,9},{12,10},{13,11},{18,16},{19,... | collective-permute-start | bytes 3932168 | tf_op jit(solution)/shard_map/ppermute | solution.py:304
  356.9 140.0 %collective-permute-start.58 = (bf16[2,320,2048]{2,1,0:T(8,128)(2,1)}, bf16[2,320,2048]{2,1,0:T(8,128)(2,1)}, u32[]{:S(2)}, u32[]{:S(2)}) collective-permute-start(bf16[2,320,2048]{2,1,0:T(8,128)(2,1)} %maximum_select_fusion.10), channel_id=1, source_target_pairs={{0,1},{1,0},{2,3},{3,2},{4,5},{5,4},{6,7},{7,6},{8,9},{9,8},{10,11... | collective-permute-start | bytes 7864328 | tf_op jit(solution)/shard_map/ppermute | solution.py:286
  369.1 139.8 %collective-permute-start.36 = (bf16[2,2,2,2,64,1024]{5,4,3,2,0,1:T(8,128)(2,1)}, bf16[2,2,2,2,64,1024]{5,4,3,2,0,1:T(8,128)(2,1)}, u32[]{:S(2)}, u32[]{:S(2)}) collective-permute-start(bf16[2,2,2,2,64,1024]{5,4,3,2,0,1:T(8,128)(2,1)} %maximum_select_fusion.13), channel_id=1, source_target_pairs={{0,1},{1,0},{2,3},{3,2},{4,5},{5,4},{6,7},{7,6},{8,9},{9,8},{10,11... | collective-permute-start | bytes 6291464 | tf_op jit(solution)/shard_map/ppermute | solution.py:286
  370.7 141.7 %collective-permute-start.31 = (bf16[2,2,2,2,64,1024]{5,4,3,2,1,0:T(8,128)(2,1)}, bf16[2,2,2,2,64,1024]{5,4,3,2,1,0:T(8,128)(2,1)}, u32[]{:S(2)}, u32[]{:S(2)}) collective-permute-start(bf16[2,2,2,2,64,1024]{5,4,3,2,1,0:T(8,128)(2,1)} %maximum_select_fusion.11), channel_id=1, source_target_pairs={{0,1},{1,0},{2,3},{3,2},{4,5},{5,4},{6,7},{7,6},{8,9},{9,8},{10,11... | collective-permute-start | bytes 6291464 | tf_op jit(solution)/shard_map/ppermute | solution.py:286
  413.0 167.0 %collective-permute-start.47 = (bf16[256,2048]{1,0:T(8,128)(2,1)}, bf16[256,2048]{1,0:T(8,128)(2,1)}, u32[]{:S(2)}, u32[]{:S(2)}) collective-permute-start(bf16[256,2048]{1,0:T(8,128)(2,1)} %collective-permute-done.43), channel_id=1, source_target_pairs={{0,16},{8,24},{16,0},{24,8},{1,17},{9,25},{17,1},{25,9},{2,18},{10... | collective-permute-start | bytes 3145736 | tf_op jit(solution)/shard_map/ppermute | solution.py:286
  661.6 75.3 %collective-permute-start.59 = (bf16[2,320,2048]{2,1,0:T(8,128)(2,1)}, bf16[2,320,2048]{2,1,0:T(8,128)(2,1)}, u32[]{:S(2)}, u32[]{:S(2)}) collective-permute-start(bf16[2,320,2048]{2,1,0:T(8,128)(2,1)} %fusion.40), channel_id=1, source_target_pairs={{0,1},{1,0},{2,3},{3,2},{4,5},{5,4},{6,7},{7,6},{8,9},{9,8},{10,11... | collective-permute-start | bytes 7864328 | tf_op jit(solution)/shard_map/ppermute | solution.py:286
  724.7 121.2 %collective-permute-start.97 = (bf16[1024,2048]{1,0:T(8,128)(2,1)}, bf16[1024,2048]{1,0:T(8,128)(2,1)}, u32[]{:S(2)}, u32[]{:S(2)}) collective-permute-start(bf16[1024,2048]{1,0:T(8,128)(2,1)} %convolution_convert_fusion.1), channel_id=1, source_target_pairs={{0,16},{8,24},{16,0},{24,8},{1,17},{9,25},{17,1},{25,9},{2,18},{10... | collective-permute-start | bytes 12582920 | tf_op jit(solution)/shard_map/ppermute | solution.py:286
  766.9 99.7 %collective-permute-start.102 = (bf16[1024,2048]{1,0:T(8,128)(2,1)}, bf16[1024,2048]{1,0:T(8,128)(2,1)}, u32[]{:S(2)}, u32[]{:S(2)}) collective-permute-start(bf16[1024,2048]{1,0:T(8,128)(2,1)} %convolution_convert_fusion), channel_id=1, source_target_pairs={{0,8},{8,0},{16,24},{24,16},{1,9},{9,1},{17,25},{25,17},{2,10},{10... | collective-permute-start | bytes 12582920 | tf_op jit(solution)/shard_map/ppermute | solution.py:286
  846.0 353.9 %collective-permute-start.88 = (bf16[16,64,2048]{2,1,0:T(8,128)(2,1)}, bf16[16,64,2048]{2,1,0:T(8,128)(2,1)}, u32[]{:S(2)}, u32[]{:S(2)}) collective-permute-start(bf16[16,64,2048]{2,1,0:T(8,128)(2,1)} %fusion.24), channel_id=1, source_target_pairs={{0,1},{1,0},{2,3},{3,2},{4,5},{5,4},{6,7},{7,6},{8,9},{9,8},{10,11... | collective-permute-start | bytes 12582920 | tf_op jit(solution)/shard_map/ppermute | solution.py:286
  858.7 182.4 %collective-permute-start.98 = (bf16[2,256,2048]{2,1,0:T(8,128)(2,1)}, bf16[2,256,2048]{2,1,0:T(8,128)(2,1)}, u32[]{:S(2)}, u32[]{:S(2)}) collective-permute-start(bf16[2,256,2048]{2,1,0:T(8,128)(2,1)} %fusion.50), channel_id=1, source_target_pairs={{0,8},{8,0},{16,24},{24,16},{1,9},{9,1},{17,25},{25,17},{2,10},{10... | collective-permute-start | bytes 6291464 | tf_op jit(solution)/shard_map/ppermute | solution.py:286
  974.0 63.5 %collective-permute-start.68 = (bf16[320,2048]{1,0:T(8,128)(2,1)}, bf16[320,2048]{1,0:T(8,128)(2,1)}, u32[]{:S(2)}, u32[]{:S(2)}) collective-permute-start(bf16[320,2048]{1,0:T(8,128)(2,1)} %fusion.63), channel_id=1, source_target_pairs={{0,1},{1,0},{2,3},{3,2},{4,5},{5,4},{6,7},{7,6},{8,9},{9,8},{10,11... | collective-permute-start | bytes 3932168 | tf_op jit(solution)/shard_map/ppermute | solution.py:286
  1037.3 121.4 %collective-permute-start.67 = (bf16[320,2048]{1,0:T(8,128)(2,1)}, bf16[320,2048]{1,0:T(8,128)(2,1)S(1)}, u32[]{:S(2)}, u32[]{:S(2)}) collective-permute-start(bf16[320,2048]{1,0:T(8,128)(2,1)} %fusion.62), channel_id=1, source_target_pairs={{0,1},{1,0},{2,3},{3,2},{4,5},{5,4},{6,7},{7,6},{8,9},{9,8},{10,11... | collective-permute-start | bytes 3932168 | tf_op jit(solution)/shard_map/ppermute | solution.py:286
  1041.1 117.7 %collective-permute-start.69 = (bf16[320,2048]{1,0:T(8,128)(2,1)}, bf16[320,2048]{1,0:T(8,128)(2,1)}, u32[]{:S(2)}, u32[]{:S(2)}) collective-permute-start(bf16[320,2048]{1,0:T(8,128)(2,1)} %select_convert_fusion.1), channel_id=1, source_target_pairs={{0,2},{1,3},{8,10},{9,11},{16,18},{17,19},{24,26},{25,27}} | collective-permute-start | bytes 3932168 | tf_op jit(solution)/shard_map/ppermute | solution.py:300
  1081.3 75.2 %collective-permute-start.99 = (bf16[256,2048]{1,0:T(8,128)(2,1)}, bf16[256,2048]{1,0:T(8,128)(2,1)}, u32[]{:S(2)}, u32[]{:S(2)}) collective-permute-start(bf16[256,2048]{1,0:T(8,128)(2,1)} %fusion.67), channel_id=1, source_target_pairs={{0,4},{1,5},{2,6},{3,7},{4,0},{5,1},{6,2},{7,3},{8,12},{9,13},{10,... | collective-permute-start | bytes 3145736 | tf_op jit(solution)/shard_map/ppermute | solution.py:286
  1156.5 198.3 %collective-permute-start.65 = (bf16[320,2048]{1,0:T(8,128)(2,1)}, bf16[320,2048]{1,0:T(8,128)(2,1)}, u32[]{:S(2)}, u32[]{:S(2)}) collective-permute-start(bf16[320,2048]{1,0:T(8,128)(2,1)} %fusion.60), channel_id=1, source_target_pairs={{0,1},{1,0},{2,3},{3,2},{4,5},{5,4},{6,7},{7,6},{8,9},{9,8},{10,11... | collective-permute-start | bytes 3932168 | tf_op jit(solution)/shard_map/ppermute | solution.py:286
  1158.7 71.9 %collective-permute-start.104 = (bf16[256,2048]{1,0:T(8,128)(2,1)}, bf16[256,2048]{1,0:T(8,128)(2,1)}, u32[]{:S(2)}, u32[]{:S(2)}) collective-permute-start(bf16[256,2048]{1,0:T(8,128)(2,1)} %fusion.68), channel_id=1, source_target_pairs={{0,4},{1,5},{2,6},{3,7},{4,0},{5,1},{6,2},{7,3},{8,12},{9,13},{10,... | collective-permute-start | bytes 3145736 | tf_op jit(solution)/shard_map/ppermute | solution.py:286
  1265.5 89.3 %collective-permute-start.71 = (bf16[320,2048]{1,0:T(8,128)(2,1)S(1)}, bf16[320,2048]{1,0:T(8,128)(2,1)S(1)}, u32[]{:S(2)}, u32[]{:S(2)}) collective-permute-start(bf16[320,2048]{1,0:T(8,128)(2,1)S(1)} %copy-done.68), channel_id=1, source_target_pairs={{0,2},{1,3},{2,4},{3,5},{4,6},{5,7},{8,10},{9,11},{10,12},{11,13},... | collective-permute-start | bytes 3932168 | tf_op jit(solution)/shard_map/ppermute | solution.py:300
  (191 other events, 6389.8 us)

commit v2 on v1

v2 whole, which is shorter than its diff:
```python
import functools
import math

import jax
import jax.numpy as jnp
from jax import lax
from jax.experimental import pallas as pl
from jax.experimental.pallas import tpu as pltpu
from jax.sharding import PartitionSpec as P

HEADS = 32
HEAD_DIM = 64
EPS = 1e-05
NEGATIVE = -1e30
FAR = 1 << 20
BLOCK = 256
BF16 = jnp.bfloat16
F32 = jnp.float32


def contract(left, right, left_dim, right_dim):
    return lax.dot_general(
        left, right, (((left_dim,), (right_dim,)), ((), ())), preferred_element_type=F32
    )


def slot_pieces(devices, pre, tok, device):
    if isinstance(device, int):
        return [(0, device * pre, pre), (pre, devices * pre + device * tok, tok)]
    return [
        (0, pl.multiple_of(device * pre, 16), pre),
        (pre, pl.multiple_of(devices * pre + device * tok, 16), tok),
    ]


def block_pieces(devices, pre, tok, place_ref, first, blocks):
    pieces = []
    for n in range(blocks):
        for i in range(2):
            core = place_ref[0] if i == 0 else 1 - place_ref[0]
            device = place_ref[first + n] * 2 + core
            for row, slot, count in slot_pieces(devices, pre, tok, device):
                pieces.append((n, i * (pre + tok) + row, slot, count))
    return pieces


def result_pieces(devices, pre, tok, place_ref):
    pieces = []
    for z in range(devices // 2):
        for i in range(2):
            core = place_ref[0] if i == 0 else 1 - place_ref[0]
            for row, slot, count in slot_pieces(devices, pre, tok, z * 2 + core):
                pieces.append(((z * 2 + i) * (pre + tok) + row, slot, count))
    return pieces


def block_mask(place, low, high):
    return (place <= high) & ((place >= low) | (place < 0))


def forward_kernel(devices, pre, tok, heads, head_dim, *refs):
    chips = devices // 2
    spot_ref, place_ref, low_ref, high_ref = refs[:4]
    chunks = refs[4 : 4 + chips]
    o_ref, ot_ref, lse_ref, q_s, k_s, v_s, vt_s, acc_s = refs[4 + chips :]
    width = heads * head_dim
    blocks = devices * (pre + tok) // BLOCK
    for n, row, slot, cnt in block_pieces(devices, pre, tok, spot_ref, 1, chips):
        q_s[pl.ds(slot, cnt), :] = chunks[n][row : row + cnt, 0:width]
        k_s[pl.ds(slot, cnt), :] = chunks[n][row : row + cnt, width : 2 * width]
        v_s[pl.ds(slot, cnt), :] = chunks[n][row : row + cnt, 2 * width : 3 * width]
    for b in range(blocks):
        rows = slice(b * BLOCK, (b + 1) * BLOCK)
        vt_s[:, rows] = v_s[rows, :].astype(F32).T.astype(BF16)
    lane = lax.broadcasted_iota(jnp.int32, (BLOCK, width), 1) // head_dim

    def query_block(i, carry):
        qs = pl.ds(pl.multiple_of(i * BLOCK, BLOCK), BLOCK)
        q = q_s[qs, :]
        qh = [jnp.where(lane == h, q, jnp.zeros_like(q)) for h in range(heads)]
        low = low_ref[:, qs]
        high = high_ref[:, qs]
        acc_s[...] = jnp.zeros_like(acc_s)
        span = [slice(h * head_dim, (h + 1) * head_dim) for h in range(heads)]

        def key_block(j, inner):
            tops, totals = inner
            ks = pl.ds(pl.multiple_of(j * BLOCK, BLOCK), BLOCK)
            k = k_s[ks, :]
            bias = jnp.where(block_mask(place_ref[ks, :], low, high), 0.0, NEGATIVE)
            s = [contract(k, qh[h], 1, 1) + bias for h in range(heads)]
            new = [
                jnp.maximum(tops[h], jnp.max(s[h], axis=0, keepdims=True)) for h in range(heads)
            ]
            p = [jnp.exp(s[h] - new[h]) for h in range(heads)]
            alpha = [jnp.exp(tops[h] - new[h]) for h in range(heads)]
            sums = [
                totals[h] * alpha[h] + jnp.sum(p[h], axis=0, keepdims=True) for h in range(heads)
            ]
            for h in range(heads):
                share = contract(vt_s[span[h], ks], p[h].astype(BF16), 1, 0)
                acc_s[span[h], :] = acc_s[span[h], :] * alpha[h] + share
            return tuple(new), tuple(sums)

        start = (
            tuple(jnp.full((1, BLOCK), NEGATIVE, F32) for h in range(heads)),
            tuple(jnp.zeros((1, BLOCK), F32) for h in range(heads)),
        )
        tops, totals = lax.fori_loop(0, i + 1, key_block, start)
        for h in range(heads):
            acc_s[span[h], :] = acc_s[span[h], :] / totals[h]
            lse_ref[h : h + 1, qs] = tops[h] + jnp.log(totals[h])
        result = acc_s[...]
        ot_ref[:, qs] = result
        q_s[qs, :] = result.T.astype(BF16)
        return carry

    lax.fori_loop(0, blocks, query_block, 0)
    for row, slot, cnt in result_pieces(devices, pre, tok, spot_ref):
        o_ref[row : row + cnt, :] = q_s[pl.ds(slot, cnt), :]


def attention_forward(chunks, spots, place, low, high, devices, pre, tok, heads, head_dim):
    width = heads * head_dim
    rows = devices * (pre + tok)
    vmem = pl.BlockSpec(memory_space=pltpu.VMEM)
    pairs = rows * rows // 2 * heads
    return pl.pallas_call(
        functools.partial(forward_kernel, devices, pre, tok, heads, head_dim),
        out_shape=(
            jax.ShapeDtypeStruct((rows, width), BF16),
            jax.ShapeDtypeStruct((width, rows), F32),
            jax.ShapeDtypeStruct((8, rows), F32),
        ),
        in_specs=[pl.BlockSpec(memory_space=pltpu.SMEM)] + [vmem] * (3 + len(chunks)),
        out_specs=(vmem,) * 3,
        scratch_shapes=[
            pltpu.VMEM((rows, width), BF16),
            pltpu.VMEM((rows, width), BF16),
            pltpu.VMEM((rows, width), BF16),
            pltpu.VMEM((width, rows), BF16),
            pltpu.VMEM((width, BLOCK), F32),
        ],
        compiler_params=pltpu.CompilerParams(vmem_limit_bytes=48 << 20),
        cost_estimate=pl.CostEstimate(
            flops=16 * pairs * head_dim, bytes_accessed=rows * width * 12, transcendentals=pairs
        ),
    )(spots, place, low, high, *chunks)


def backward_kernel(
    devices, pre, tok, heads, head_dim, first, last, carried, final, *refs
):
    chips = devices // 2
    spot_ref, ot_ref, lse_ref, place_ref, low_ref, high_ref = refs[:6]
    chunks = refs[6 : 6 + chips]
    grads = refs[6 + chips : 6 + 2 * chips]
    refs = refs[6 + 2 * chips :]
    if carried:
        dq_in, dk_in, dv_in = refs[:3]
        refs = refs[3:]
    if final:
        out_ref, near_ref = refs[:2]
        q_s, k_s, v_s, do_s, kt_s, dqt_s, dq_s, dk_s, dv_s = refs[2:]
    else:
        dq_s, dk_s, dv_s, q_s, k_s, v_s, do_s, kt_s, dqt_s = refs
    width = heads * head_dim
    scale = 1.0 / math.sqrt(head_dim)
    for n, row, slot, cnt in block_pieces(devices, pre, tok, spot_ref, 1, chips):
        q_s[pl.ds(slot, cnt), :] = chunks[n][row : row + cnt, 0:width]
        k_s[pl.ds(slot, cnt), :] = chunks[n][row : row + cnt, width : 2 * width]
        v_s[pl.ds(slot, cnt), :] = chunks[n][row : row + cnt, 2 * width : 3 * width]
    for n, row, slot, cnt in block_pieces(devices, pre, tok, spot_ref, 1 + chips, chips):
        do_s[pl.ds(slot, cnt), :] = grads[n][row : row + cnt, :]
    for b in range(last):
        rows = slice(b * BLOCK, (b + 1) * BLOCK)
        kt_s[:, rows] = k_s[rows, :].astype(F32).T.astype(BF16)
    if carried:
        dq_s[...] = dq_in[...]
        dk_s[...] = dk_in[...]
        dv_s[...] = dv_in[...]
    else:
        dk_s[...] = jnp.zeros_like(dk_s)
        dv_s[...] = jnp.zeros_like(dv_s)
    lane = lax.broadcasted_iota(jnp.int32, (BLOCK, width), 1) // head_dim

    def query_block(i, carry):
        qs = pl.ds(pl.multiple_of(i * BLOCK, BLOCK), BLOCK)
        q = q_s[qs, :]
        do = do_s[qs, :]
        qh = [jnp.where(lane == h, q, jnp.zeros_like(q)) for h in range(heads)]
        doh = [jnp.where(lane == h, do, jnp.zeros_like(do)) for h in range(heads)]
        low = low_ref[:, qs]
        high = high_ref[:, qs]
        prod = do.astype(F32).T * ot_ref[:, qs]
        delta = [
            jnp.sum(prod[h * head_dim : (h + 1) * head_dim, :], axis=0, keepdims=True)
            for h in range(heads)
        ]
        lse = [lse_ref[h : h + 1, qs] for h in range(heads)]
        dqt_s[...] = jnp.zeros_like(dqt_s)

        def key_block(j, inner):
            ks = pl.ds(pl.multiple_of(j * BLOCK, BLOCK), BLOCK)
            k = k_s[ks, :]
            v = v_s[ks, :]
            bias = jnp.where(block_mask(place_ref[ks, :], low, high), 0.0, NEGATIVE)
            s = [contract(k, qh[h], 1, 1) for h in range(heads)]
            dp = [contract(v, doh[h], 1, 1) for h in range(heads)]
            p = [jnp.exp(s[h] + bias - lse[h]) for h in range(heads)]
            ds = [(p[h] * (dp[h] - delta[h])).astype(BF16) for h in range(heads)]
            dv = sum(contract(p[h].astype(BF16), doh[h], 1, 0) for h in range(heads))
            dk = sum(contract(ds[h], qh[h], 1, 0) for h in range(heads))
            for h in range(heads):
                hs = slice(h * head_dim, (h + 1) * head_dim)
                dqt_s[hs, :] += contract(kt_s[hs, ks], ds[h], 1, 0)
            dk_s[ks, :] += dk
            dv_s[ks, :] += dv
            return inner

        lax.fori_loop(0, i + 1, key_block, 0)
        dq_s[qs, :] = (dqt_s[...] * scale).T.astype(BF16)
        return carry

    lax.fori_loop(first, last, query_block, 0)
    if final:
        for row, slot, cnt in result_pieces(devices, pre, tok, spot_ref):
            out_ref[row : row + cnt, 0:width] = dq_s[pl.ds(slot, cnt), :]
            out_ref[row : row + cnt, width : 2 * width] = dk_s[pl.ds(slot, cnt), :].astype(BF16)
            out_ref[row : row + cnt, 2 * width : 3 * width] = dv_s[pl.ds(slot, cnt), :].astype(BF16)
        both = 2 * (pre + tok)
        for n in range(chips):
            chip = pl.multiple_of(spot_ref[1 + n] * both, 16)
            near_ref[n * both : (n + 1) * both, :] = out_ref[pl.ds(chip, both), :]


def attention_backward(
    chunks, grads, spots, ot, lse, place, low, high, devices, pre, tok, heads, head_dim, first, last, carry, final
):
    width = heads * head_dim
    rows = devices * (pre + tok)
    vmem = pl.BlockSpec(memory_space=pltpu.VMEM)
    pairs = (last - first) * (last + first + 1) // 2 * BLOCK * BLOCK * heads
    low_rows = pltpu.VMEM((rows, width), BF16)
    sums = [((rows, width), BF16), ((rows, width), F32), ((rows, width), F32)]
    scratch = [
        low_rows,
        low_rows,
        low_rows,
        low_rows,
        pltpu.VMEM((width, rows), BF16),
        pltpu.VMEM((width, BLOCK), F32),
    ]
    if final:
        out_shape = (jax.ShapeDtypeStruct((rows, 3 * width), BF16),) * 2
        scratch += [pltpu.VMEM(shape, dtype) for shape, dtype in sums]
    else:
        out_shape = tuple(jax.ShapeDtypeStruct(shape, dtype) for shape, dtype in sums)
    return pl.pallas_call(
        functools.partial(
            backward_kernel, devices, pre, tok, heads, head_dim, first, last, bool(carry), final
        ),
        out_shape=out_shape,
        in_specs=[pl.BlockSpec(memory_space=pltpu.SMEM)]
        + [vmem] * (5 + len(chunks) + len(grads) + len(carry)),
        out_specs=(vmem,) * len(out_shape),
        scratch_shapes=scratch,
        compiler_params=pltpu.CompilerParams(vmem_limit_bytes=58 << 20),
        cost_estimate=pl.CostEstimate(
            flops=20 * pairs * head_dim, bytes_accessed=rows * width * 20, transcendentals=pairs
        ),
    )(spots, ot, lse, place, low, high, *chunks, *grads, *carry)


def matmul_kernel(flipped, left_ref, right_ref, out_ref):
    out_ref[...] = contract(left_ref[...], right_ref[...], 1, 1 if flipped else 0).astype(BF16)


def matmul_low(left, right, flipped):
    rows, depth = left.shape
    columns = right.shape[0] if flipped else right.shape[1]
    step = 512
    block = (step, depth) if flipped else (depth, step)
    return pl.pallas_call(
        functools.partial(matmul_kernel, flipped),
        grid=(columns // step,),
        out_shape=jax.ShapeDtypeStruct((rows, columns), BF16),
        in_specs=[
            pl.BlockSpec((rows, depth), lambda n: (0, 0)),
            pl.BlockSpec(block, (lambda n: (n, 0)) if flipped else (lambda n: (0, n))),
        ],
        out_specs=pl.BlockSpec((rows, step), lambda n: (0, n)),
        compiler_params=pltpu.CompilerParams(vmem_limit_bytes=48 << 20),
        cost_estimate=pl.CostEstimate(flops=1 << 20, bytes_accessed=1 << 16, transcendentals=0),
    )(left, right)


def transposed_kernel(left_ref, right_ref, out_ref):
    out_ref[...] = contract(left_ref[...], right_ref[...], 0, 0).astype(BF16)


def matmul_transposed(left, right):
    depth, rows = left.shape
    columns = right.shape[1]
    step = 512
    return pl.pallas_call(
        transposed_kernel,
        grid=(rows // step,),
        out_shape=jax.ShapeDtypeStruct((rows, columns), BF16),
        in_specs=[
            pl.BlockSpec((depth, step), lambda n: (0, n)),
            pl.BlockSpec((depth, columns), lambda n: (0, 0)),
        ],
        out_specs=pl.BlockSpec((step, columns), lambda n: (n, 0)),
        compiler_params=pltpu.CompilerParams(vmem_limit_bytes=56 << 20),
        cost_estimate=pl.CostEstimate(flops=1 << 20, bytes_accessed=1 << 16, transcendentals=0),
    )(left, right)


def rows_product_kernel(*refs):
    chunks, right_ref, out_ref = refs[:-2], refs[-2], refs[-1]
    rows = chunks[0].shape[0]
    total = contract(chunks[0][...], right_ref[0:rows, :], 0, 0)
    for n in range(1, len(chunks)):
        total += contract(chunks[n][...], right_ref[n * rows : (n + 1) * rows, :], 0, 0)
    out_ref[...] = total.astype(BF16)


def rows_product(chunks, right):
    rows, columns = chunks[0].shape
    step = 512
    return pl.pallas_call(
        rows_product_kernel,
        grid=(columns // step,),
        out_shape=jax.ShapeDtypeStruct((columns, right.shape[1]), BF16),
        in_specs=[pl.BlockSpec((rows, step), lambda n: (0, n))] * len(chunks)
        + [pl.BlockSpec(right.shape, lambda n: (0, 0))],
        out_specs=pl.BlockSpec((step, right.shape[1]), lambda n: (n, 0)),
        compiler_params=pltpu.CompilerParams(vmem_limit_bytes=56 << 20),
        cost_estimate=pl.CostEstimate(
            flops=right.shape[0] * columns * right.shape[1] // 2, bytes_accessed=1 << 16, transcendentals=0
        ),
    )(*chunks, right)


def slot_labels(lengths, devices, pre, tok, real):
    slot = jnp.arange(devices * pre, dtype=jnp.int32)
    inside = slot % pre
    place = (slot // pre) * real + inside - devices * real
    is_real = inside < real
    t = jnp.arange(devices * tok, dtype=jnp.int32)
    ends = jnp.cumsum(lengths)
    start = jnp.max(jnp.where(ends[None, :] <= t[:, None], ends[None, :], 0), axis=1)
    places = jnp.concatenate([jnp.where(is_real, place, FAR), t])
    high = jnp.concatenate([jnp.where(is_real, place, -1), t])
    low = jnp.concatenate([jnp.full((devices * pre,), FAR, jnp.int32), start])
    return places[:, None], low[None, :], high[None, :]


def normalize(values):
    center = values - jnp.mean(values, axis=-1, keepdims=True)
    spread = jnp.mean(center * center, axis=-1, keepdims=True)
    inverse = lax.rsqrt(spread + EPS)
    return center * inverse, inverse


def norm_backward(grad, hat, inverse, gain):
    e = grad * gain
    mean_e = jnp.mean(e, axis=-1, keepdims=True)
    mean_eh = jnp.mean(e * hat, axis=-1, keepdims=True)
    return inverse * (e - mean_e - hat * mean_eh)


def gelu_parts(values):
    cdf = 0.5 * (1.0 + lax.erf(values * (1.0 / math.sqrt(2.0))))
    return cdf


def pick(array, index, axis):
    return lax.dynamic_index_in_dim(array, index, axis, keepdims=False)


def build(n_batch, n_seq):
    n_z = n_seq // 2
    n_dev = n_batch * n_seq
    groups = n_dev // 4
    size_of = {"batch": n_batch, "seq": n_seq}

    def bits_of(n):
        bits = []
        bit = 1
        while bit < n:
            bits.append(bit)
            bit *= 2
        return bits

    core = ("seq", 1)
    near = ("seq", 2)
    up_batch = [("batch", bit) for bit in bits_of(n_batch)]
    down_batch = list(reversed(up_batch))
    far_bits = [("seq", bit) for bit in bits_of(n_seq) if bit >= 4]
    chip_bits = [near] + far_bits
    group_bits = down_batch + list(reversed(far_bits))
    all_bits = down_batch + [("seq", bit) for bit in reversed(bits_of(n_seq))]

    def swap_pairs(which):
        axis, bit = which
        return axis, [(i, i ^ bit) for i in range(size_of[axis])]

    def shift_pairs(distance):
        return "seq", [
            (z * 2 + c, ((z + distance) % n_z) * 2 + c) for z in range(n_z) for c in range(2)
        ]

    def right_pairs(first, last):
        return "seq", [(z * 2 + c, z * 2 + 2 + c) for z in range(first, last) for c in range(2)]

    def left_pairs(first, last):
        return "seq", [(z * 2 + c, z * 2 - 2 + c) for z in range(first, last) for c in range(2)]

    def side(which):
        axis, bit = which
        return (lax.axis_index(axis) // bit) % 2

    def permute(array, pairs):
        return lax.ppermute(array, pairs[0], pairs[1])

    class Clock:
        def __init__(self):
            self.gate = ()

        def hold(self, *arrays):
            if self.gate:
                arrays = lax.optimization_barrier(tuple(arrays) + tuple(self.gate))[: len(arrays)]
            return arrays[0] if len(arrays) == 1 else arrays

        def tick(self, *arrays):
            self.gate = arrays

    def join(mine, other, which, axis):
        first = side(which) == 0
        return jnp.where(first, jnp.stack([mine, other], axis), jnp.stack([other, mine], axis))

    def body(
        tokens, prefix, seg_lengths, attn_gain, attn_shift, query_weight, key_weight, value_weight,
        query_bias, value_bias, output_weight, output_bias, mlp_gain, mlp_shift, up_weight, up_bias,
        down_weight, down_bias, cot_tokens, cot_prefix,
    ):
        clock = Clock()

        def swap(array, which):
            return permute(array, swap_pairs(which))

        def gather_bits(array, order, ranked):
            taken = []
            current = array
            for which in order:
                other = swap(current, which)
                rank = ranked.index(which)
                place = sum(1 for t in taken if ranked.index(t) < rank)
                current = join(current, other, which, place)
                taken.append(which)
            return current.reshape((2 ** len(order),) + array.shape)

        def part_of(current, left, which, mine):
            return pick(current, side(which) if mine else 1 - side(which), left.index(which))

        def hop_scatter(current, left, which, last):
            other = swap(part_of(current, left, which, False).astype(BF16), which)
            total = part_of(current, left, which, True).astype(F32) + other.astype(F32)
            rest = [b for b in left if b != which]
            return (total if last else total.astype(BF16)), rest

        tok = tokens.shape[1]
        real = prefix.shape[1]
        pre = -(-real // 16) * 16
        width = pre + tok
        model = tokens.shape[2]
        heads = HEADS // n_seq
        span = heads * HEAD_DIM
        part = model // n_dev
        unit = up_bias.shape[0]
        hidden_here = groups * unit
        s_here = lax.axis_index("seq")
        z_here = s_here // 2
        c_here = s_here % 2
        near_here = side(near)
        lengths = seg_lengths[0]

        def rows_of(pre_part, tok_part):
            return jnp.concatenate([jnp.pad(pre_part, ((0, pre - real), (0, 0))), tok_part], axis=0)

        def device_rows(array, z, c):
            return lax.dynamic_slice_in_dim(array, (z * 2 + c) * width, width, 0)

        own = rows_of(prefix[0], tokens[0])
        row = jnp.arange(width, dtype=jnp.int32)
        position = row - pre + s_here * tok
        valid = jnp.where(row < pre, row < real, position < jnp.sum(lengths))
        validity = valid.astype(F32)[:, None]

        far_group = list(reversed(far_bits))
        n_far = groups // n_batch
        far_here = s_here // 4

        def afar(array, mask):
            return permute(array, ("seq", [(i, i ^ (mask * 4)) for i in range(n_seq)]))

        def batch_gather(array):
            return lax.all_gather(array, "batch", axis=0, tiled=True)

        def batch_sum(array):
            return lax.psum_scatter(array, "batch", scatter_dimension=0, tiled=True)

        def set_far(whole, blocks, index):
            blocks = blocks.reshape((n_batch, 1, -1) + blocks.shape[1:])
            return lax.dynamic_update_slice_in_dim(whole, blocks, index, 1)

        steps = [(permute(own, right_pairs(0, n_z - 1)), permute(own, left_pairs(1, n_z)))]
        small = jnp.concatenate(
            [attn_gain, attn_shift, query_bias, value_bias, output_bias, mlp_gain, mlp_shift, down_bias, up_bias]
        )
        small_bits = down_batch + [core]
        small = gather_bits(small, list(reversed(small_bits)), small_bits)
        down_gate, unused = lax.optimization_barrier((down_weight, small))
        down_own = batch_gather(down_gate)

        stacked = jnp.stack([query_weight, key_weight, value_weight], axis=1)
        stacked = stacked.reshape(part, 3, heads, n_z, 2, HEAD_DIM).transpose(3, 4, 0, 1, 2, 5)
        stacked = stacked.reshape(n_z, 2, part, 3 * span)
        mixed = join(pick(stacked, c_here, 1), swap(pick(stacked, 1 - c_here, 1), core), core, 1)
        mixed = mixed.reshape(n_z, 2 * part, 3 * span)
        flat = small.reshape(-1)
        small_rows = -(-flat.shape[0] // (3 * span * 16)) * 16
        flat = jnp.pad(flat, (0, small_rows * 3 * span - flat.shape[0]))
        flat = jnp.broadcast_to(flat.reshape(1, small_rows, 3 * span), (n_z, small_rows, 3 * span))
        mixed = jnp.concatenate([mixed, flat], axis=1)

        up_near = up_weight.reshape(part, groups, 2, 2, unit)
        up_near = join(pick(up_near, c_here, 3), swap(pick(up_near, 1 - c_here, 3), core), core, 0)

        clock.tick(*steps[0], up_near)

        def shift_out(choose):
            pieces = [choose((z_here + d) % n_z) for d in range(1, n_z)]
            pieces = clock.hold(*pieces) if len(pieces) > 1 else [clock.hold(*pieces)]
            got = [permute(piece, shift_pairs(d + 1)) for d, piece in enumerate(pieces)]
            return [(z_here, choose(z_here))] + [
                ((z_here - d - 1) % n_z, piece) for d, piece in enumerate(got)
            ]

        placed = shift_out(lambda z: pick(mixed, z, 0))
        ranked_o = far_group + [near]
        up_other = swap(clock.hold(pick(up_near, 1 - near_here, 3)), near)
        gathered_o = gather_bits(clock.hold(output_weight), far_bits, far_group)
        clock.tick(up_other, gathered_o, *[piece for unused, piece in placed[1:]])
        up_block = join(pick(up_near, near_here, 3), up_other, near, 0)
        up_block = up_block.reshape(4 * part, hidden_here)
        local = jnp.zeros((n_z, 2 * part, 3 * span), BF16)
        small_z = jnp.zeros((n_z, small_rows, 3 * span), BF16)
        for z, piece in placed:
            local = lax.dynamic_update_slice_in_dim(local, piece[None, : 2 * part], z, 0)
            small_z = lax.dynamic_update_slice_in_dim(small_z, piece[None, 2 * part :], z, 0)
        local, unused = lax.optimization_barrier((local, down_own))
        weight_qkv = batch_gather(local.reshape(n_z * 2 * part, 3 * span))
        small = small_z.reshape(n_z, -1)[:, : n_batch * 2 * (8 * part + unit)]
        small = small.reshape(n_z, n_batch, 2, 8 * part + unit).transpose(1, 0, 2, 3)
        small = small.reshape(n_dev, 8 * part + unit)
        vectors = [small[:, n * part : (n + 1) * part].reshape(model).astype(F32) for n in range(8)]
        gain_a, shift_a, bias_q, bias_v, bias_o, gain_m, shift_m, bias_down = vectors
        bias_up = pick(small[:, 8 * part :].reshape(groups, 4, unit), s_here % 4, 1)
        bias_up = bias_up.reshape(hidden_here).astype(F32)

        bias_qkv = jnp.concatenate(
            [
                pick(bias_q.reshape(heads, n_seq, HEAD_DIM), s_here, 1).reshape(span),
                jnp.zeros((span,), F32),
                pick(bias_v.reshape(heads, n_seq, HEAD_DIM), s_here, 1).reshape(span),
            ]
        )
        factor = jnp.concatenate(
            [jnp.full((span,), 1.0 / math.sqrt(HEAD_DIM), F32), jnp.ones((2 * span,), F32)]
        )

        def source(n):
            if n == 0:
                return z_here
            short = jnp.minimum(z_here, n_z - 1 - z_here)
            both = n <= 2 * short
            distance = jnp.where(both, (n + 1) // 2, n - short)
            left = jnp.where(both, n % 2 == 1, 2 * z_here >= n_z)
            return jnp.where(left, z_here - distance, z_here + distance)

        def rows_from(n):
            rows = own
            for d in range((n + 1) // 2, n + 1) if n else ():
                right, left = steps[d - 1]
                rows = jnp.where(source(n) == z_here - d, right, rows)
                rows = jnp.where(source(n) == z_here + d, left, rows)
            rows = jnp.concatenate([rows, swap(rows, core)], axis=0)
            hat, unused = normalize(rows.astype(F32))
            return (hat * gain_a + shift_a).astype(BF16)

        def qkv_of(rows):
            result = (contract(rows, weight_qkv, 1, 0) + bias_qkv).astype(BF16).astype(F32) * factor
            return result.astype(BF16)

        exact = part == HEAD_DIM and heads == n_batch
        normed = []
        for k in range(2, n_z):
            right, left = clock.hold(*steps[-1])
            steps.append(
                (permute(right, right_pairs(k - 1, n_z - 1)), permute(left, left_pairs(1, n_z - k + 1)))
            )
            normed.append(rows_from(k - 2))
            clock.tick(*steps[-1], normed[-1])
        up_gate, unused = lax.optimization_barrier((up_block, weight_qkv))
        up_own = batch_gather(up_gate)

        other = swap(clock.hold(gathered_o), near)
        gathered_o = join(gathered_o, other, near, 1)
        gathered_o, unused = lax.optimization_barrier((gathered_o, up_own))
        gathered_o = batch_gather(gathered_o.reshape(n_z * part, model))

        weight_o = gathered_o.reshape(n_batch, n_z, part, model)
        if exact:
            weight_o = weight_o.transpose(1, 0, 2, 3).reshape(n_z * span, model)
        else:
            weight_o = join(weight_o, swap(weight_o, core), core, 2)
            weight_o = weight_o.reshape(heads, n_z, 2, HEAD_DIM, model)
            weight_o = pick(weight_o, c_here, 2).transpose(1, 0, 2, 3).reshape(n_z * span, model)

        qkv = []
        for n in range(n_z):
            if n >= n_z - 2:
                normed.append(rows_from(n))
            qkv.append(qkv_of(normed[n]))
        shifted = [z_here] + [(z_here - d) % n_z for d in range(1, n_z)]
        spots = jnp.stack([c_here] + [source(n) for n in range(n_z)] + shifted).astype(jnp.int32)

        cot_rows = rows_of(cot_prefix[0], cot_tokens[0]).astype(F32)
        mlp_out_grad = (validity * cot_rows).astype(BF16)
        places, low, high = slot_labels(lengths, n_seq, pre, tok, real)
        clock.tick(other)
        *qkv, up_gate, grad_gate = clock.hold(*qkv, up_block, mlp_out_grad)
        up_far = [afar(up_gate, mask) for mask in range(1, n_far)]
        grad_far = swap(grad_gate, near)
        attended, attended_t, log_total = attention_forward(
            qkv, spots, places, low, high, n_seq, pre, tok, heads, HEAD_DIM
        )
        clock.tick(attended, grad_far, *up_far)
        up_blocks = [batch_gather(clock.hold(piece)) for piece in up_far]

        blocks = attended.reshape(n_z, 2 * width, span)
        placed = shift_out(lambda z: pick(blocks, z, 0))
        *normed, up_own, down_own, unused = lax.optimization_barrier(
            tuple(normed) + (up_own, down_own, attended)
        )
        weight_up = set_far(
            jnp.zeros((n_batch, n_far, 4 * part, hidden_here), BF16), up_own, far_here
        )
        weight_down = set_far(
            jnp.zeros((n_batch, n_far, unit, model), BF16), down_own, far_here
        )
        grad_rows = jnp.concatenate(
            [mlp_out_grad, swap(mlp_out_grad, core), grad_far, swap(grad_far, core)], axis=0
        )
        mixed_low = jnp.zeros((2 * width, n_z * span), BF16)
        for z, piece in placed:
            mixed_low = lax.dynamic_update_slice_in_dim(mixed_low, piece, z * span, 1)
        clock.tick(mixed_low, weight_up, weight_down)
        down_far = [afar(clock.hold(down_weight), mask) for mask in range(1, n_far)]
        mixed_held = clock.hold(mixed_low)
        branch_away = contract(mixed_held[width:], weight_o, 1, 0).astype(BF16)
        branch_away = swap(branch_away, core)
        branch = contract(mixed_held[:width], weight_o, 1, 0) + branch_away.astype(F32) + bias_o
        rows_in = own.astype(F32)
        resid = rows_in + validity * branch
        hat_m, inverse_m = normalize(resid)
        normed_own = (hat_m * gain_m + shift_m).astype(BF16)

        normed_near = swap(normed_own, core)
        normed_far = swap(normed_own, near)
        normed_rows = jnp.concatenate(
            [normed_own, normed_near, normed_far, swap(normed_far, core)], axis=0
        )
        *down_far, unused = lax.optimization_barrier(tuple(down_far) + (normed_own,))
        down_blocks = [batch_gather(piece) for piece in down_far]
        *up_blocks, unused = lax.optimization_barrier(tuple(up_blocks) + (normed_own,))
        for mask, piece in enumerate(up_blocks):
            weight_up = set_far(weight_up, piece, far_here ^ (mask + 1))
        weight_up = weight_up.reshape(model, hidden_here)

        before = contract(normed_rows, weight_up, 1, 0) + bias_up
        cdf = 0.5 * (1.0 + lax.erf(before * (1.0 / math.sqrt(2.0))))
        hidden = (before * cdf).astype(BF16)
        slope = cdf + before * jnp.exp(-0.5 * before * before) * (1.0 / math.sqrt(2.0 * math.pi))
        *down_blocks, unused = lax.optimization_barrier(tuple(down_blocks) + (hidden,))
        for mask, piece in enumerate(down_blocks):
            weight_down = set_far(weight_down, piece, far_here ^ (mask + 1))
        weight_down = weight_down.reshape(hidden_here, model)
        grad_down = contract(hidden, grad_rows, 0, 0).astype(BF16)
        grad_down, grad_held = lax.optimization_barrier((grad_down, grad_rows))
        grad_down = batch_sum(grad_down)
        hidden_grad = contract(grad_held, weight_down, 1, 1)
        pre_grad = (hidden_grad * slope).astype(BF16)

        share_f = contract(pre_grad[2 * width :], weight_up, 1, 1).astype(BF16)
        back = swap(share_f[width:], core)
        back = (share_f[:width].astype(F32) + back.astype(F32)).astype(BF16)
        pre_held, hidden_held, back_held = lax.optimization_barrier((pre_grad, hidden, back))
        back = swap(back_held, near)
        share_n = matmul_low(pre_held[: 2 * width], weight_up, True)
        out_share = matmul_low(hidden_held, weight_down, False)
        here = swap(share_n[width:], core)
        back, out_share, here = lax.optimization_barrier((back, out_share, here))
        normed_grad = share_n[:width].astype(F32) + here.astype(F32) + back.astype(F32)

        grad_up_bias = jnp.sum(pre_grad.astype(F32), axis=0)
        grad_down_bias = jnp.sum(mlp_out_grad.astype(F32), axis=0)
        grad_gain_m = jnp.sum(normed_grad * hat_m, axis=0)
        grad_shift_m = jnp.sum(normed_grad, axis=0)
        resid_grad = cot_rows + norm_backward(normed_grad, hat_m, inverse_m, gain_m)

        branch_grad = (validity * resid_grad).astype(BF16)
        grad_out_bias = jnp.sum(branch_grad.astype(F32), axis=0)
        branch_grad = jnp.concatenate([branch_grad, swap(branch_grad, core)], axis=0)
        mixed_grad = contract(branch_grad, weight_o, 1, 1).astype(BF16)
        clock.tick(mixed_grad)
        placed = shift_out(lambda z: lax.dynamic_slice_in_dim(mixed_grad, z * span, span, 1))
        grad_gate, branch_gate, mixed_gate, unused = lax.optimization_barrier(
            (pre_grad, branch_grad, mixed_low, mixed_grad)
        )
        grad_up = matmul_transposed(normed_rows, grad_gate)
        grad_out = matmul_transposed(mixed_gate, branch_gate)
        if exact:
            grad_out = grad_out.reshape(n_z, n_batch, part, model).transpose(1, 0, 2, 3)
        else:
            full = jnp.zeros((heads, n_z, 2, HEAD_DIM, model), BF16)
            grad_out = grad_out.reshape(n_z, heads, 1, HEAD_DIM, model).transpose(1, 0, 2, 3, 4)
            grad_out = lax.dynamic_update_slice_in_dim(full, grad_out, c_here, 2)
            grad_out = grad_out.reshape(n_batch, n_z, 2, part, model)
            grad_out = pick(grad_out, c_here, 2).astype(F32) + swap(
                pick(grad_out, 1 - c_here, 2), core
            ).astype(F32)
            grad_out = grad_out.astype(BF16)
        rows_grad = [piece for unused, piece in placed]
        grad_up, grad_out, *rows_grad = lax.optimization_barrier((grad_up, grad_out, *rows_grad))
        grad_up = batch_sum(grad_up)
        grad_out = batch_sum(grad_out.reshape(n_batch * n_z * part, model))

        out_back = swap(out_share[3 * width :], core)
        out_back = (out_share[2 * width : 3 * width].astype(F32) + out_back.astype(F32)).astype(BF16)
        out_here = swap(out_share[width : 2 * width], core)
        clock.tick(*rows_grad, grad_down, out_share)
        down_gate, out_away, *rows_grad = clock.hold(grad_down, out_back, *rows_grad)
        down_sum = down_gate.reshape((2,) * len(far_bits) + (unit, model))
        rest_down = list(far_group)
        for n, which in enumerate(far_bits):
            down_sum, rest_down = hop_scatter(
                down_sum, rest_down, which, n == len(far_bits) - 1
            )
        grad_down = down_sum
        out_back = swap(out_away, near)
        blocks = n_seq * width // BLOCK
        qkv_grad, relative = attention_backward(
            qkv, rows_grad, spots, attended_t, log_total, places, low, high,
            n_seq, pre, tok, heads, HEAD_DIM, 0, blocks, (), True,
        )
        qkv_grad, relative, grad_down, out_back = lax.optimization_barrier(
            (qkv_grad, relative, grad_down, out_back)
        )
        bias_sums = jnp.sum(qkv_grad.astype(F32), axis=0)
        clock.tick(qkv_grad, grad_down, out_back)

        chunks = [None] * n_z
        order = []
        for k in range(1, n_z):
            for r in (n_z - k, k):
                if r not in order:
                    order.append(r)
        for r in order + [0]:
            z = (z_here + r) % n_z
            away = contract(device_rows(qkv_grad, z, 1), weight_qkv, 1, 1).astype(BF16)
            away = swap(away, core)
            keep = contract(device_rows(qkv_grad, z, 0), weight_qkv, 1, 1)
            chunks[r] = keep + away.astype(F32)
        right = None
        left = None
        for k in range(1, n_z):
            going_r = jnp.where(z_here + n_z - k < n_z, chunks[n_z - k], 0.0)
            going_l = jnp.where(z_here - (n_z - k) >= 0, chunks[k], 0.0)
            if k > 1:
                going_r = going_r + right.astype(F32)
                going_l = going_l + left.astype(F32)
            going_r, going_l = clock.hold(going_r.astype(BF16), going_l.astype(BF16))
            right = permute(going_r, right_pairs(0, k))
            left = permute(going_l, left_pairs(n_z - k, n_z))
            started = [right, left]
            if k == 1:
                up_sum = clock.hold(grad_up).reshape((2,) * len(far_bits) + (4 * part, hidden_here))
                rest_up = list(far_group)
                for which in far_bits:
                    up_sum, rest_up = hop_scatter(up_sum, rest_up, which, False)
                relative, unused = lax.optimization_barrier((relative, going_r))
                grad_qkv = rows_product(normed, relative)
                grad_qkv, right, left, up_sum, grad_out = lax.optimization_barrier(
                    (grad_qkv, right, left, up_sum, grad_out)
                )
                grad_qkv = batch_sum(grad_qkv)
                started = [right, left, up_sum]
            if k == 2:
                grad_up = up_sum.reshape(2, 2, part, hidden_here)
                up_other = swap(clock.hold(pick(grad_up, 1 - near_here, 0)), near)
                grad_up = join(pick(grad_up, near_here, 0), up_other, near, 0)
                rest_o = list(ranked_o)
                grad_out = clock.hold(grad_out).reshape((2,) * len(ranked_o) + (part, model))
                grad_out, rest_o = hop_scatter(grad_out, rest_o, near, False)
                started += [up_other, grad_out]
            if k == n_z - 1:
                grad_qkv = grad_qkv.reshape(n_z, 2, part, 3 * span)
                grad_qkv = join(
                    pick(grad_qkv, c_here, 1), swap(pick(grad_qkv, 1 - c_here, 1), core), core, 1
                )
                placed = shift_out(lambda z: pick(grad_qkv, z, 0))
                grad_out = clock.hold(grad_out)
                for n, which in enumerate(far_bits):
                    grad_out, rest_o = hop_scatter(grad_out, rest_o, which, n == len(far_bits) - 1)
            clock.tick(*started)
        right, left, unused = lax.optimization_barrier(
            (right, left, tuple(piece for unused, piece in placed[1:]))
        )
        normed_back = chunks[0] + right.astype(F32) + left.astype(F32)

        grad_up = join(pick(grad_up, c_here, 1), swap(pick(grad_up, 1 - c_here, 1), core), core, 1)
        grad_up = grad_up.reshape(4, part, groups, unit).transpose(1, 2, 0, 3)
        grad_up = grad_up.reshape(part, n_dev * unit).astype(F32)

        final = out_share[:width].astype(F32) + out_here.astype(F32) + out_back.astype(F32)
        final = resid + validity * (final + bias_down)
        out_rows = final.astype(BF16)

        shares = jnp.zeros((n_z, 2, part, 3 * span), BF16)
        for z, piece in placed:
            shares = lax.dynamic_update_slice_in_dim(shares, piece[None], z, 0)
        shares = shares.reshape(n_seq, part, 3, heads, HEAD_DIM)
        shares = [
            shares[:, :, n].transpose(1, 2, 0, 3).reshape(part, model).astype(F32) for n in range(3)
        ]

        hat_a, inverse_a = normalize(rows_in)
        grad_gain_a = jnp.sum(normed_back * hat_a, axis=0)
        grad_shift_a = jnp.sum(normed_back, axis=0)
        input_grad = resid_grad + norm_backward(normed_back, hat_a, inverse_a, gain_a)

        zero = jnp.zeros((heads, n_seq, HEAD_DIM), F32)

        def spread(sums):
            sums = sums.reshape(heads, 1, HEAD_DIM)
            return lax.dynamic_update_slice_in_dim(zero, sums, s_here, 1).reshape(model)

        full_up_bias = lax.dynamic_update_slice_in_dim(
            jnp.zeros((groups, 4, unit), F32), grad_up_bias.reshape(groups, 1, unit), s_here % 4, 1
        ).reshape(n_dev, unit)
        sums = jnp.concatenate(
            [
                vector.reshape(n_dev, part)
                for vector in (
                    grad_gain_a, grad_shift_a, spread(bias_sums[:span]), spread(bias_sums[2 * span :]),
                    grad_out_bias, grad_gain_m, grad_shift_m, grad_down_bias,
                )
            ]
            + [full_up_bias],
            axis=1,
        )
        sums, unused = lax.optimization_barrier((sums, tuple(shares)))
        current = jnp.sum(lax.all_to_all(sums, ("batch", "seq"), 0, 0, tiled=True), axis=0)
        small_grads = [current[n * part : (n + 1) * part] for n in range(8)]

        return (
            out_rows[pre:][None],
            out_rows[:real][None],
            input_grad[pre:][None],
            input_grad[:real][None],
            small_grads[0],
            small_grads[1],
            shares[0],
            shares[1],
            shares[2],
            small_grads[2],
            small_grads[3],
            grad_out,
            small_grads[4],
            small_grads[5],
            small_grads[6],
            grad_up,
            current[8 * part :],
            grad_down,
            small_grads[7],
        )

    return body


def solution(mesh):
    rows = P("batch", "seq", None)
    vector = P(("batch", "seq"))
    matrix = P(("batch", "seq"), None)
    return jax.shard_map(
        build(mesh.shape["batch"], mesh.shape["seq"]),
        mesh=mesh,
        in_specs=(
            rows, rows, P("batch", None), vector, vector, matrix, matrix, matrix, vector, vector,
            matrix, vector, vector, vector, matrix, vector, matrix, vector, rows, rows,
        ),
        out_specs=(
            rows, rows, rows, rows, vector, vector, matrix, matrix, matrix, vector, vector, matrix,
            vector, vector, vector, matrix, vector, matrix, vector,
        ),
        check_vma=False,
    )
```

time: 1390 us -> 893 us (0.64)
  waiting for transfers between devices: 488 us -> 282 us
  local copies, waits for them, and re-layouts: 244 us -> 95.5 us
  other arithmetic: 172 us -> 91.4 us
  starting transfers between devices: 164 us -> 111 us
  matrix products: 159 us -> 126 us
  Pallas kernels: 148 us -> 166 us
    ppermute x105 -> x63, waiting for transfers between devices: 488 us -> 280 us  [permute(): return lax.ppermute(array, pairs[0], pairs[1])]
    ppermute x105 -> x63, starting transfers between devices: 164 us -> 93.1 us  [permute(): return lax.ppermute(array, pairs[0], pairs[1])]
    pallas_call x0 -> x5, Pallas kernels: none -> 61.2 us  [the longest x2 23.3 us: matmul_low(): pl.pallas_call(functools.partial(matmul_kernel, flipped), grid=(columns /...]
    select_n x42 -> x13, other arithmetic: 55.1 us -> 7.47 us  [join(): jnp.where(first, jnp.stack([mine, other], axis), jnp.stack([other, mine],...]
    dot_general x20 -> x19, matrix products: 159 us -> 126 us  [contract(): lax.dot_general(left, right, (((left_dim,), (right_dim,)), ((), ())), pre...]
    convert_element_type x27 -> x6, local copies, waits for them, and re-layouts: 39 us -> 6.52 us  [body(): shares[:, :, n].transpose(1, 2, 0, 3).reshape(part, model).astype(F32)]
    reshape x8 -> x16, local copies, waits for them, and re-layouts: 37.5 us -> 9.08 us  [the longest x1 4.71 us: body(): grad_out = grad_out.reshape(n_z, n_batch, part, model).transpose(1, 0, 2, 3)]
    add x22 -> x2, other arithmetic: 29 us -> 3.91 us  [hop_scatter(): total = part_of(current, left, which, True).astype(F32) + other.astype(F32)]
  transfers between devices with their start and end apart: 105 -> 74, of which waited for: 42 -> 27; matrix products, arithmetic and copies ran while one was open for 34% -> 33% of each run, Pallas kernels for 11% -> 19%
where the time goes in v2:
time: 893 us; the launch traced here: 889 us
  waiting for transfers between devices  282 us (32%)
  Pallas kernels  166 us (19%)
  matrix products  126 us (14%)
  starting transfers between devices  111 us (12%)
  local copies, waits for them, and re-layouts  95.5 us (11%)
  other arithmetic  91.4 us (10%)
  between operations  16.5 us (2%)
    ppermute x63, waiting for transfers between devices, permute(): return lax.ppermute(array, pairs[0], pairs[1])  280 us
    dot_general x19, matrix products, contract(): lax.dot_general(left, right, (((left_dim,), (right_dim,)), ((), ())), pre...  126 us
    ppermute x63, starting transfers between devices, permute(): return lax.ppermute(array, pairs[0], pairs[1])  93.1 us
    pallas_call x1, Pallas kernels, attention_backward(): pl.pallas_call(functools.partial(backward_kernel, devices, pre, tok, head...  62.4 us
    pallas_call x1, Pallas kernels, attention_forward(): pl.pallas_call(functools.partial(forward_kernel, devices, pre, tok, heads...  42.6 us
    pallas_call x2, Pallas kernels, matmul_low(): pl.pallas_call(functools.partial(matmul_kernel, flipped), grid=(columns /...  23.3 us
    pallas_call x2, Pallas kernels, matmul_transposed(): pl.pallas_call(transposed_kernel, grid=(rows // step,), out_shape=jax.Sha...  22.9 us
  transfers between devices with their start and end apart: 74, of which 27 were waited for; matrix products, arithmetic and copies ran while one was open for 33% of the time, Pallas kernels for 19%

profile of v2, /device:TPU:0, one launch (start us, length us, event | category | flops | bytes accessed | tf_op | source)
XLA Modules:
  0.0 888.7 jit_solution(3422831633870005407)
XLA Ops:
  78.4 14.5 %collective-permute-done.13 = bf16[64,2048]{1,0:T(8,128)(2,1)S(1)} collective-permute-done((bf16[64,2048]{1,0:T(8,128)(2,1)}, bf16[64,2048]{1,0:T(8,128)(2,1)S(1)}, u32[]{:S(2)}, u32[]{:S(2)}) %collective-permute-start.13) | collective-permute-done | bytes 262176 | tf_op jit(solution)/shard_map/ppermute | solution.py:426
  104.8 22.4 %collective-permute-done.14 = bf16[320,2048]{1,0:T(8,128)(2,1)} collective-permute-done((bf16[320,2048]{1,0:T(8,128)(2,1)}, bf16[320,2048]{1,0:T(8,128)(2,1)}, u32[]{:S(2)}, u32[]{:S(2)}) %collective-permute-start.14) | collective-permute-done | bytes 1310752 | tf_op jit(solution)/shard_map/ppermute | solution.py:426
  135.2 25.2 %collective-permute-done.17 = bf16[320,2048]{1,0:T(8,128)(2,1)} collective-permute-done((bf16[320,2048]{1,0:T(8,128)(2,1)}, bf16[320,2048]{1,0:T(8,128)(2,1)}, u32[]{:S(2)}, u32[]{:S(2)}) %collective-permute-start.17) | collective-permute-done | bytes 1310752 | tf_op jit(solution)/shard_map/ppermute | solution.py:426
  179.0 13.9 %collective-permute-done.20 = bf16[2,64,2048]{2,1,0:T(8,128)(2,1)S(1)} collective-permute-done((bf16[2,64,2048]{2,1,0:T(8,128)(2,1)S(1)}, bf16[2,64,2048]{2,1,0:T(8,128)(2,1)S(1)}, u32[]{:S(2)}, u32[]{:S(2)}) %collective-permute-start.20) | collective-permute-done | bytes 524320 | tf_op jit(solution)/shard_map/ppermute | solution.py:426
  194.1 11.9 %all-gather.15.cloned.1.call-start = ((), (), s32[]{:S(2)}) async-start(), calls=%async_computation.9 | async-start | bytes 5242880 | tf_op jit(solution)/shard_map/all_gather | solution.py:510
  235.4 42.6 %shard_map.339 = (bf16[2560,256]{1,0:T(8,128)(2,1)S(1)}, f32[256,2560]{1,0:T(8,128)}, f32[8,2560]{1,0:T(8,128)S(1)}) custom-call(s32[9]{0:T(128)S(1)} %stack.212.refs_0_, s32[2560,1]{1,0:T(8,128)} %broadcast_in_dim.171.refs_1_.refs_3_, s32[1,2560]{1,0:T(1,128)S(1)} %broadcast_in_dim.78.refs_2_.refs_4_, s32[1,2560]{1,0:T(1,128)S(1)} %broadcast_in_dim.79.refs_3_.refs_5_, ...), custom_call_target="tpu_custom_call" | custom-call | flops 13421772800 | bytes 7864320 | tf_op jit(solution)/shard_map/pallas_call | solution.py:128
  285.7 7.3 collective-permute-done.23
  293.0 11.6 %collective-permute-done.24 = bf16[640,256]{1,0:T(8,128)(2,1)S(1)} collective-permute-done((bf16[640,256]{1,0:T(8,128)(2,1)}, bf16[640,256]{1,0:T(8,128)(2,1)S(1)}, u32[]{:S(2)}, u32[]{:S(2)}) %collective-permute-start.24) | collective-permute-done | bytes 327712 | tf_op jit(solution)/shard_map/ppermute | solution.py:426
  339.8 36.2 %collective-permute-done.32 = bf16[256,2048]{1,0:T(8,128)(2,1)} collective-permute-done((bf16[256,2048]{1,0:T(8,128)(2,1)}, bf16[256,2048]{1,0:T(8,128)(2,1)}, u32[]{:S(2)}, u32[]{:S(2)}) %collective-permute-start.32) | collective-permute-done | bytes 1048608 | tf_op jit(solution)/shard_map/ppermute | solution.py:426
  376.6 11.3 %collective-permute-done.28 = bf16[320,2048]{1,0:T(8,128)(2,1)S(1)} collective-permute-done((bf16[320,2048]{1,0:T(8,128)(2,1)S(1)}, bf16[320,2048]{1,0:T(8,128)(2,1)S(1)}, u32[]{:S(2)}, u32[]{:S(2)}) %collective-permute-start.28) | collective-permute-done | bytes 1310752 | tf_op jit(solution)/shard_map/ppermute | solution.py:426
  398.5 20.0 %multiply_convert_fusion = (bf16[1280,2048]{1,0:T(8,128)(2,1)S(1)}, f32[1280,2048]{1,0:T(8,128)}) fusion(f32[2048]{0:T(1024)S(1)} %bitcast.295, bf16[2048,2048]{1,0:T(8,128)(2,1)} %bitcast.59.right_ref, bf16[320,2048]{1,0:T(8,128)(2,1)} %collective-permute-done.29, bf16[320,2048]{1,0:T(8,128)(2,1)S(1)} %collective-permute-done.28, ...), kind=kOutput, calls=%fused_computation.8 | convolution fusion | flops 10774118400 | bytes 29368320 | tf_op jit(solution)/shard_map/dot_general | solution.py:22
  420.9 15.3 %convolution_convert_fusion = bf16[2048,2048]{1,0:T(8,128)(2,1)} fusion(bf16[1280,2048]{1,0:T(8,128)(2,1)S(1)} %get-tuple-element.143.left_ref, bf16[320,2048]{1,0:T(8,128)(2,1)} %collective-permute-done.31, bf16[320,2048]{1,0:T(8,128)(2,1)} %collective-permute-done.21, bf16[320,2048]{1,0:T(8,128)(2,1)} %collective-permute-done.30, ...), kind=kOutput, calls=%fused_computation.11 | convolution fusion | flops 10762584064 | bytes 18874368 | tf_op jit(solution)/shard_map/dot_general | solution.py:22
  441.2 19.7 %convert_reduce_fusion = (f32[2048]{0:T(1024)S(1)}, bf16[1280,2048]{1,0:T(8,128)(2,1)S(1)}) fusion(f32[1280,2048]{1,0:T(8,128)} %get-tuple-element.371, f32[2048]{0:T(1024)S(1)} %bitcast.296, bf16[1280,2048]{1,0:T(8,128)(2,1)} %pad_maximum_fusion.1, bf16[2048,2048]{1,0:T(8,128)(2,1)} %bitcast.246), kind=kOutput, calls=%fused_computation.7 | convolution fusion | flops 10771494912 | bytes 29376512 | tf_op jit(solution)/shard_map/dot_general | solution.py:22
  460.9 10.2 %convolution_convert_fusion.1 = bf16[640,2048]{1,0:T(8,128)(2,1)S(1)} fusion(bf16[2048,2048]{1,0:T(8,128)(2,1)} %bitcast.59.right_ref, bf16[1280,2048]{1,0:T(8,128)(2,1)S(1)} %get-tuple-element.151.right_ref), kind=kOutput, calls=%fused_computation.52 | convolution fusion | flops 5370019840 | bytes 13631488 | tf_op jit(solution)/shard_map/dot_general | solution.py:22
  476.3 8.0 shard_map.341
  484.7 15.3 %shard_map.340 = bf16[1280,2048]{1,0:T(8,128)(2,1)S(1)} custom-call(bf16[1280,2048]{1,0:T(8,128)(2,1)} %copy-done.27, bf16[2048,2048]{1,0:T(8,128)(2,1)} %bitcast.247), custom_call_target="tpu_custom_call" | custom-call | flops 1048576 | bytes 65536 | tf_op jit(solution)/shard_map/pallas_call | solution.py:284
  500.0 15.8 %collective-permute-done.34 = bf16[320,2048]{1,0:T(8,128)(2,1)S(1)} collective-permute-done((bf16[320,2048]{1,0:T(8,128)(2,1)}, bf16[320,2048]{1,0:T(8,128)(2,1)S(1)}, u32[]{:S(2)}, u32[]{:S(2)}) %collective-permute-start.34) | collective-permute-done | bytes 1310752 | tf_op jit(solution)/shard_map/ppermute | solution.py:426
  558.2 15.9 %shard_map.342 = bf16[2048,2048]{1,0:T(8,128)(2,1)} custom-call(bf16[1280,2048]{1,0:T(8,128)(2,1)} %pad_maximum_fusion.left_ref, bf16[1280,2048]{1,0:T(8,128)(2,1)} %copy-done.22), custom_call_target="tpu_custom_call" | custom-call | flops 1048576 | bytes 65536 | tf_op jit(solution)/shard_map/pallas_call | solution.py:306
  586.5 62.4 %shard_map.344 = (bf16[2560,768]{1,0:T(8,128)(2,1)}, bf16[2560,768]{1,0:T(8,128)(2,1)}) custom-call(s32[9]{0:T(128)} %copy-done.3, f32[256,2560]{1,0:T(8,128)} %get-tuple-element.146.refs_1_, f32[8,2560]{1,0:T(8,128)} %copy-done.8, s32[2560,1]{1,0:T(8,128)} %broadcast_in_dim.171.refs_1_.refs_3_, s32[1,2560]{1,0:T(1,128)} %copy-done.2, s32[1,2560]{1,0:T(1,128)} %copy-done.1, ...), custom_call_target="tpu_custom_call" | custom-call | flops 18454937600 | bytes 13107200 | tf_op jit(solution)/shard_map/pallas_call | solution.py:259
  680.4 15.0 %shard_map.345 = bf16[2048,768]{1,0:T(8,128)(2,1)} custom-call(bf16[640,2048]{1,0:T(8,128)(2,1)} %fusion.29.refs_0_, bf16[640,2048]{1,0:T(8,128)(2,1)} %get-tuple-element.172.refs_1_, bf16[640,2048]{1,0:T(8,128)(2,1)} %get-tuple-element.173.refs_2_, bf16[640,2048]{1,0:T(8,128)(2,1)} %get-tuple-element.174.refs_3_, bf16[2560,768]{1,0:T(8,128)(2,1)} %get-tuple-element.178.refs_4_), custom_call_target="tpu_custom_call" | custom-call | flops 2013265920 | bytes 65536 | tf_op jit(solution)/shard_map/pallas_call | solution.py:332
  695.4 18.5 %collective-permute-done.50 = bf16[256,2048]{1,0:T(8,128)(2,1)S(1)} collective-permute-done((bf16[256,2048]{1,0:T(8,128)(2,1)S(1)}, bf16[256,2048]{1,0:T(8,128)(2,1)S(1)}, u32[]{:S(2)}, u32[]{:S(2)}) %collective-permute-start.50) | collective-permute-done | bytes 1048608 | tf_op jit(solution)/shard_map/ppermute | solution.py:426
  748.7 9.7 %collective-permute-done.54 = bf16[2,64,2048]{2,1,0:T(8,128)(2,1)S(1)} collective-permute-done((bf16[2,64,2048]{2,1,0:T(8,128)(2,1)}, bf16[2,64,2048]{2,1,0:T(8,128)(2,1)S(1)}, u32[]{:S(2)}, u32[]{:S(2)}) %collective-permute-start.54) | collective-permute-done | bytes 524320 | tf_op jit(solution)/shard_map/ppermute | solution.py:426
  765.1 20.8 %collective-permute-done.51 = bf16[320,2048]{1,0:T(8,128)(2,1)} collective-permute-done((bf16[320,2048]{1,0:T(8,128)(2,1)}, bf16[320,2048]{1,0:T(8,128)(2,1)}, u32[]{:S(2)}, u32[]{:S(2)}) %collective-permute-start.51) | collective-permute-done | bytes 1310752 | tf_op jit(solution)/shard_map/ppermute | solution.py:426
  809.7 29.9 %collective-permute-done.58 = bf16[2,64,768]{2,1,0:T(8,128)(2,1)S(1)} collective-permute-done((bf16[2,64,768]{2,1,0:T(8,128)(2,1)S(1)}, bf16[2,64,768]{2,1,0:T(8,128)(2,1)S(1)}, u32[]{:S(2)}, u32[]{:S(2)}) %collective-permute-start.58) | collective-permute-done | bytes 196640 | tf_op jit(solution)/shard_map/ppermute | solution.py:426
  (499 shorter events, 398.6 us)
Async XLA Ops:
  7.2 60.3 %all-gather.7.cloned.1.call-start = ((), (), s32[]{:S(2)}) async-start(), calls=%async_computation.5 | async-start | bytes 5242880 | tf_op jit(solution)/shard_map/all_gather | solution.py:510
  7.9 125.0 %all-gather.9.cloned.1.call-start = ((), (), s32[]{:S(2)}) async-start(), calls=%async_computation.6 | async-start | bytes 3932160 | tf_op jit(solution)/shard_map/all_gather | solution.py:510
  68.4 125.6 %all-gather.11.cloned.1.call-start = ((), (), s32[]{:S(2)}) async-start(), calls=%async_computation.7 | async-start | bytes 5242880 | tf_op jit(solution)/shard_map/all_gather | solution.py:510
  133.0 184.4 %all-gather.13.cloned.1.call-start = ((), (), s32[]{:S(2)}) async-start(), calls=%async_computation.8 | async-start | bytes 5242880 | tf_op jit(solution)/shard_map/all_gather | solution.py:510
  194.1 199.6 %all-gather.15.cloned.1.call-start = ((), (), s32[]{:S(2)}) async-start(), calls=%async_computation.9 | async-start | bytes 5242880 | tf_op jit(solution)/shard_map/all_gather | solution.py:510
  224.2 54.4 %collective-permute-start.21 = (bf16[320,2048]{1,0:T(8,128)(2,1)}, bf16[320,2048]{1,0:T(8,128)(2,1)}, u32[]{:S(2)}, u32[]{:S(2)}) collective-permute-start(bf16[320,2048]{1,0:T(8,128)(2,1)} %get-tuple-element.126), channel_id=1, source_target_pairs={{0,2},{1,3},{2,0},{3,1},{4,6},{5,7},{6,4},{7,5},{8,10},{9,11},{10,... | collective-permute-start | bytes 3932168 | tf_op jit(solution)/shard_map/ppermute | solution.py:426
  226.7 52.0 %collective-permute-start.22 = (bf16[256,2048]{1,0:T(8,128)(2,1)}, bf16[256,2048]{1,0:T(8,128)(2,1)}, u32[]{:S(2)}, u32[]{:S(2)}) collective-permute-start(bf16[256,2048]{1,0:T(8,128)(2,1)} %bitcast.122), channel_id=1, source_target_pairs={{0,4},{1,5},{2,6},{3,7},{4,0},{5,1},{6,2},{7,3},{8,12},{9,13},{10,... | collective-permute-start | bytes 3145736 | tf_op jit(solution)/shard_map/ppermute | solution.py:426
  278.7 157.7 %all-gather.17.cloned.1.call-start = ((), (), s32[]{:S(2)}) async-start(), calls=%async_computation.10 | async-start | bytes 5242880 | tf_op jit(solution)/shard_map/all_gather | solution.py:510
  322.7 53.3 %collective-permute-start.32 = (bf16[256,2048]{1,0:T(8,128)(2,1)}, bf16[256,2048]{1,0:T(8,128)(2,1)}, u32[]{:S(2)}, u32[]{:S(2)}) collective-permute-start(bf16[256,2048]{1,0:T(8,128)(2,1)} %param.36), channel_id=1, source_target_pairs={{0,4},{1,5},{2,6},{3,7},{4,0},{5,1},{6,2},{7,3},{8,12},{9,13},{10,... | collective-permute-start | bytes 3145736 | tf_op jit(solution)/shard_map/ppermute | solution.py:426
  335.4 52.4 %collective-permute-start.28 = (bf16[320,2048]{1,0:T(8,128)(2,1)S(1)}, bf16[320,2048]{1,0:T(8,128)(2,1)S(1)}, u32[]{:S(2)}, u32[]{:S(2)}) collective-permute-start(bf16[320,2048]{1,0:T(8,128)(2,1)S(1)} %add_convert_fusion.7), channel_id=1, source_target_pairs={{0,2},{1,3},{2,0},{3,1},{4,6},{5,7},{6,4},{7,5},{8,10},{9,11},{10,... | collective-permute-start | bytes 3932168 | tf_op jit(solution)/shard_map/ppermute | solution.py:426
  339.3 48.6 %collective-permute-start.30 = (bf16[320,2048]{1,0:T(8,128)(2,1)}, bf16[320,2048]{1,0:T(8,128)(2,1)}, u32[]{:S(2)}, u32[]{:S(2)}) collective-permute-start(bf16[320,2048]{1,0:T(8,128)(2,1)} %get-tuple-element.126), channel_id=1, source_target_pairs={{0,1},{1,0},{2,3},{3,2},{4,5},{5,4},{6,7},{7,6},{8,9},{9,8},{10,11... | collective-permute-start | bytes 3932168 | tf_op jit(solution)/shard_map/ppermute | solution.py:426
  339.3 48.6 %collective-permute-start.31 = (bf16[320,2048]{1,0:T(8,128)(2,1)}, bf16[320,2048]{1,0:T(8,128)(2,1)}, u32[]{:S(2)}, u32[]{:S(2)}) collective-permute-start(bf16[320,2048]{1,0:T(8,128)(2,1)} %collective-permute-done.21), channel_id=1, source_target_pairs={{0,1},{1,0},{2,3},{3,2},{4,5},{5,4},{6,7},{7,6},{8,9},{9,8},{10,11... | collective-permute-start | bytes 3932168 | tf_op jit(solution)/shard_map/ppermute | solution.py:426
  376.0 207.1 %reduce-scatter.5.cloned.1.call-start = ((), (), s32[]{:S(2)}) async-start(), calls=%async_computation.11 | async-start | bytes 10485760 | tf_op jit(solution)/shard_map/reduce_scatter | solution.py:513
  436.3 227.5 %reduce-scatter.7.cloned.1.call-start = ((), (), s32[]{:S(2)}) async-start(), calls=%async_computation.12 | async-start | bytes 10485760 | tf_op jit(solution)/shard_map/reduce_scatter | solution.py:513
  574.1 141.4 %reduce-scatter.9.cloned.1.call-start = ((), (), s32[]{:S(2)}) async-start(), calls=%async_computation.13 | async-start | bytes 5242880 | tf_op jit(solution)/shard_map/reduce_scatter | solution.py:513
  577.2 214.3 %reduce-scatter.11.cloned.1.call-start = ((), (), s32[]{:S(2)}) async-start(), calls=%async_computation.14 | async-start | bytes 3932160 | tf_op jit(solution)/shard_map/reduce_scatter | solution.py:513
  585.4 63.5 %collective-permute-start.42 = (bf16[256,2048]{1,0:T(8,128)(2,1)}, bf16[256,2048]{1,0:T(8,128)(2,1)}, u32[]{:S(2)}, u32[]{:S(2)}) collective-permute-start(bf16[256,2048]{1,0:T(8,128)(2,1)} %dynamic-slice_bitcast_fusion.1), channel_id=1, source_target_pairs={{0,4},{1,5},{2,6},{3,7},{4,0},{5,1},{6,2},{7,3},{8,12},{9,13},{10,... | collective-permute-start | bytes 3145736 | tf_op jit(solution)/shard_map/ppermute | solution.py:426
  585.7 66.3 %collective-permute-start.43 = (bf16[320,2048]{1,0:T(8,128)(2,1)}, bf16[320,2048]{1,0:T(8,128)(2,1)}, u32[]{:S(2)}, u32[]{:S(2)}) collective-permute-start(bf16[320,2048]{1,0:T(8,128)(2,1)} %add_convert_fusion.5), channel_id=1, source_target_pairs={{0,2},{1,3},{2,0},{3,1},{4,6},{5,7},{6,4},{7,5},{8,10},{9,11},{10,... | collective-permute-start | bytes 3932168 | tf_op jit(solution)/shard_map/ppermute | solution.py:426
  665.1 48.8 %collective-permute-start.50 = (bf16[256,2048]{1,0:T(8,128)(2,1)S(1)}, bf16[256,2048]{1,0:T(8,128)(2,1)S(1)}, u32[]{:S(2)}, u32[]{:S(2)}) collective-permute-start(bf16[256,2048]{1,0:T(8,128)(2,1)S(1)} %dynamic-slice_bitcast_fusion), channel_id=1, source_target_pairs={{0,4},{1,5},{2,6},{3,7},{4,0},{5,1},{6,2},{7,3},{8,12},{9,13},{10,... | collective-permute-start | bytes 3145736 | tf_op jit(solution)/shard_map/ppermute | solution.py:426
  680.4 46.1 %collective-permute-start.36 = (bf16[320,2048]{1,0:T(8,128)(2,1)}, bf16[320,2048]{1,0:T(8,128)(2,1)}, u32[]{:S(2)}, u32[]{:S(2)}) collective-permute-start(bf16[320,2048]{1,0:T(8,128)(2,1)} %get-tuple-element.309), channel_id=1, source_target_pairs={{0,1},{1,0},{2,3},{3,2},{4,5},{5,4},{6,7},{7,6},{8,9},{9,8},{10,11... | collective-permute-start | bytes 3932168 | tf_op jit(solution)/shard_map/ppermute | solution.py:426
  726.5 133.4 %collective-permute-start.44 = (bf16[320,2048]{1,0:T(8,128)(2,1)}, bf16[320,2048]{1,0:T(8,128)(2,1)}, u32[]{:S(2)}, u32[]{:S(2)}) collective-permute-start(bf16[320,2048]{1,0:T(8,128)(2,1)} %convolution_convert_fusion.5), channel_id=1, source_target_pairs={{0,1},{1,0},{2,3},{3,2},{4,5},{5,4},{6,7},{7,6},{8,9},{9,8},{10,11... | collective-permute-start | bytes 3932168 | tf_op jit(solution)/shard_map/ppermute | solution.py:426
  740.5 45.4 %collective-permute-start.51 = (bf16[320,2048]{1,0:T(8,128)(2,1)}, bf16[320,2048]{1,0:T(8,128)(2,1)}, u32[]{:S(2)}, u32[]{:S(2)}) collective-permute-start(bf16[320,2048]{1,0:T(8,128)(2,1)} %get-tuple-element.186), channel_id=1, source_target_pairs={{0,2},{1,3},{2,4},{3,5},{8,10},{9,11},{10,12},{11,13},{16,18},{17,... | collective-permute-start | bytes 3932168 | tf_op jit(solution)/shard_map/ppermute | solution.py:426
  796.4 63.5 %collective-permute-start.55 = (bf16[320,2048]{1,0:T(8,128)(2,1)}, bf16[320,2048]{1,0:T(8,128)(2,1)}, u32[]{:S(2)}, u32[]{:S(2)}) collective-permute-start(bf16[320,2048]{1,0:T(8,128)(2,1)} %add_convert_fusion.1), channel_id=1, source_target_pairs={{0,2},{1,3},{2,4},{3,5},{4,6},{5,7},{8,10},{9,11},{10,12},{11,13},... | collective-permute-start | bytes 3932168 | tf_op jit(solution)/shard_map/ppermute | solution.py:426
  801.0 58.8 %collective-permute-start.56 = (bf16[320,2048]{1,0:T(8,128)(2,1)}, bf16[320,2048]{1,0:T(8,128)(2,1)}, u32[]{:S(2)}, u32[]{:S(2)}) collective-permute-start(bf16[320,2048]{1,0:T(8,128)(2,1)} %add_convert_fusion), channel_id=1, source_target_pairs={{2,0},{3,1},{4,2},{5,3},{6,4},{7,5},{10,8},{11,9},{12,10},{13,11},... | collective-permute-start | bytes 3932168 | tf_op jit(solution)/shard_map/ppermute | solution.py:426
  (120 other events, 2015.4 us)
Sparse Core Ops, SparseCore 0:
  9.9 55.3 all-gather.6
  68.5 46.8 all-gather.8
  133.1 58.2 all-gather.10
  194.2 56.2 all-gather.12
  278.8 54.6 all-gather.14
  376.1 53.8 all-gather.16
  436.4 89.9 reduce-scatter.4
  574.3 85.1 reduce-scatter.6
  662.4 52.6 reduce-scatter.8
  719.1 44.2 reduce-scatter.10

commit v3 on v2

--- a/solution.py
+++ b/solution.py
@@ -619,7 +619,12 @@
 
         other = swap(clock.hold(gathered_o), near)
         gathered_o = join(gathered_o, other, near, 1)
-        gathered_o, unused = lax.optimization_barrier((gathered_o, up_own))
+        qkv = []
+        for n in range(n_z):
+            if n >= n_z - 2:
+                normed.append(rows_from(n))
+            qkv.append(qkv_of(normed[n]))
+        gathered_o, unused = lax.optimization_barrier((gathered_o, (up_own, *qkv)))
         gathered_o = batch_gather(gathered_o.reshape(n_z * part, model))
 
         weight_o = gathered_o.reshape(n_batch, n_z, part, model)
@@ -630,11 +635,6 @@
             weight_o = weight_o.reshape(heads, n_z, 2, HEAD_DIM, model)
             weight_o = pick(weight_o, c_here, 2).transpose(1, 0, 2, 3).reshape(n_z * span, model)
 
-        qkv = []
-        for n in range(n_z):
-            if n >= n_z - 2:
-                normed.append(rows_from(n))
-            qkv.append(qkv_of(normed[n]))
         shifted = [z_here] + [(z_here - d) % n_z for d in range(1, n_z)]
         spots = jnp.stack([c_here] + [source(n) for n in range(n_z)] + shifted).astype(jnp.int32)
 
@@ -665,6 +665,11 @@
         grad_rows = jnp.concatenate(
             [mlp_out_grad, swap(mlp_out_grad, core), grad_far, swap(grad_far, core)], axis=0
         )
+        spread_o = [piece for unused, piece in placed[1:]]
+        *spread_o, weight_up, weight_down, weight_o = lax.optimization_barrier(
+            (*spread_o, weight_up, weight_down, weight_o)
+        )
+        placed = [placed[0]] + [(z, piece) for (z, unused), piece in zip(placed[1:], spread_o)]
         mixed_low = jnp.zeros((2 * width, n_z * span), BF16)
         for z, piece in placed:
             mixed_low = lax.dynamic_update_slice_in_dim(mixed_low, piece, z * span, 1)
@@ -681,15 +686,15 @@
 
         normed_near = swap(normed_own, core)
         normed_far = swap(normed_own, near)
-        normed_rows = jnp.concatenate(
-            [normed_own, normed_near, normed_far, swap(normed_far, core)], axis=0
-        )
         *down_far, unused = lax.optimization_barrier(tuple(down_far) + (normed_own,))
         down_blocks = [batch_gather(piece) for piece in down_far]
         *up_blocks, unused = lax.optimization_barrier(tuple(up_blocks) + (normed_own,))
         for mask, piece in enumerate(up_blocks):
             weight_up = set_far(weight_up, piece, far_here ^ (mask + 1))
         weight_up = weight_up.reshape(model, hidden_here)
+        normed_far, weight_up = lax.optimization_barrier((normed_far, weight_up))
+        normed_parts = [normed_own, normed_near, normed_far, swap(normed_far, core)]
+        normed_rows = jnp.concatenate(normed_parts, axis=0)
 
         before = contract(normed_rows, weight_up, 1, 0) + bias_up
         cdf = 0.5 * (1.0 + lax.erf(before * (1.0 / math.sqrt(2.0))))
@@ -712,8 +717,8 @@
         back = swap(back_held, near)
         share_n = matmul_low(pre_held[: 2 * width], weight_up, True)
         out_share = matmul_low(hidden_held, weight_down, False)
+        back, out_share, share_n = lax.optimization_barrier((back, out_share, share_n))
         here = swap(share_n[width:], core)
-        back, out_share, here = lax.optimization_barrier((back, out_share, here))
         normed_grad = share_n[:width].astype(F32) + here.astype(F32) + back.astype(F32)
 
         grad_up_bias = jnp.sum(pre_grad.astype(F32), axis=0)
@@ -731,7 +736,7 @@
         grad_gate, branch_gate, mixed_gate, unused = lax.optimization_barrier(
             (pre_grad, branch_grad, mixed_low, mixed_grad)
         )
-        grad_up = matmul_transposed(normed_rows, grad_gate)
+        grad_up = rows_product(normed_parts, grad_gate)
         grad_out = matmul_transposed(mixed_gate, branch_gate)
         if exact:
             grad_out = grad_out.reshape(n_z, n_batch, part, model).transpose(1, 0, 2, 3)
@@ -745,13 +750,15 @@
             ).astype(F32)
             grad_out = grad_out.astype(BF16)
         rows_grad = [piece for unused, piece in placed]
-        grad_up, grad_out, *rows_grad = lax.optimization_barrier((grad_up, grad_out, *rows_grad))
-        grad_up = batch_sum(grad_up)
-        grad_out = batch_sum(grad_out.reshape(n_batch * n_z * part, model))
-
         out_back = swap(out_share[3 * width :], core)
         out_back = (out_share[2 * width : 3 * width].astype(F32) + out_back.astype(F32)).astype(BF16)
         out_here = swap(out_share[width : 2 * width], core)
+        grad_up, grad_out, out_back, *rows_grad = lax.optimization_barrier(
+            (grad_up, grad_out, out_back, *rows_grad)
+        )
+        grad_up = batch_sum(grad_up)
+        grad_out = batch_sum(grad_out.reshape(n_batch * n_z * part, model))
+
         clock.tick(*rows_grad, grad_down, out_share)
         down_gate, out_away, *rows_grad = clock.hold(grad_down, out_back, *rows_grad)
         down_sum = down_gate.reshape((2,) * len(far_bits) + (unit, model))
@@ -774,6 +781,7 @@
         clock.tick(qkv_grad, grad_down, out_back)
 
         chunks = [None] * n_z
+        aways = []
         order = []
         for k in range(1, n_z):
             for r in (n_z - k, k):
@@ -783,6 +791,7 @@
             z = (z_here + r) % n_z
             away = contract(device_rows(qkv_grad, z, 1), weight_qkv, 1, 1).astype(BF16)
             away = swap(away, core)
+            aways.append(away)
             keep = contract(device_rows(qkv_grad, z, 0), weight_qkv, 1, 1)
             chunks[r] = keep + away.astype(F32)
         right = None
@@ -804,8 +813,8 @@
                     up_sum, rest_up = hop_scatter(up_sum, rest_up, which, False)
                 relative, unused = lax.optimization_barrier((relative, going_r))
                 grad_qkv = rows_product(normed, relative)
-                grad_qkv, right, left, up_sum, grad_out = lax.optimization_barrier(
-                    (grad_qkv, right, left, up_sum, grad_out)
+                grad_qkv, right, left, up_sum, grad_out, unused = lax.optimization_barrier(
+                    (grad_qkv, right, left, up_sum, grad_out, tuple(aways[2:]))
                 )
                 grad_qkv = batch_sum(grad_qkv)
                 started = [right, left, up_sum]

time: 893 us -> 877 us (0.982)
  waiting for transfers between devices: 282 us -> 254 us
  starting transfers between devices: 111 us -> 93.3 us
  other arithmetic: 91.4 us -> 101 us
    ppermute x63, waiting for transfers between devices: 280 us -> 242 us  [permute(): return lax.ppermute(array, pairs[0], pairs[1])]
    pallas_call x1 -> x2, Pallas kernels: 15 us -> 37.8 us  [rows_product(): pl.pallas_call(rows_product_kernel, grid=(columns // step,), out_shape=ja...]
    pallas_call x2 -> x1, Pallas kernels: 22.9 us -> 6.95 us  [matmul_transposed(): pl.pallas_call(transposed_kernel, grid=(rows // step,), out_shape=jax.Sha...]
    all_gather x6, starting transfers between devices: 12.1 us -> 0.23 us  [batch_gather(): return lax.all_gather(array, 'batch', axis=0, tiled=True)]
  transfers between devices with their start and end apart: 74 -> 74, of which waited for: 27 -> 25; matrix products, arithmetic and copies ran while one was open for 33% -> 36% of each run, Pallas kernels for 19% -> 20%
where the time goes in v3:
time: 877 us; the launch traced here: 867 us
  waiting for transfers between devices  254 us (29%)
  Pallas kernels  173 us (20%)
  matrix products  126 us (14%)
  local copies, waits for them, and re-layouts  104 us (12%)
  other arithmetic  101 us (12%)
  starting transfers between devices  93.3 us (11%)
  between operations  16.3 us (2%)
    ppermute x63, waiting for transfers between devices, permute(): return lax.ppermute(array, pairs[0], pairs[1])  242 us
    dot_general x19, matrix products, contract(): lax.dot_general(left, right, (((left_dim,), (right_dim,)), ((), ())), pre...  126 us
    ppermute x63, starting transfers between devices, permute(): return lax.ppermute(array, pairs[0], pairs[1])  88.2 us
    pallas_call x1, Pallas kernels, attention_backward(): pl.pallas_call(functools.partial(backward_kernel, devices, pre, tok, head...  61.8 us
    pallas_call x1, Pallas kernels, attention_forward(): pl.pallas_call(functools.partial(forward_kernel, devices, pre, tok, heads...  42.6 us
    pallas_call x2, Pallas kernels, rows_product(): pl.pallas_call(rows_product_kernel, grid=(columns // step,), out_shape=ja...  37.8 us
    pallas_call x2, Pallas kernels, matmul_low(): pl.pallas_call(functools.partial(matmul_kernel, flipped), grid=(columns /...  23.5 us
  transfers between devices with their start and end apart: 74, of which 25 were waited for; matrix products, arithmetic and copies ran while one was open for 36% of the time, Pallas kernels for 20%

profile of v3, /device:TPU:0, one launch (start us, length us, event | category | flops | bytes accessed | tf_op | source)
XLA Modules:
  0.0 866.6 jit_solution(1015592846574331039)
XLA Ops:
  60.7 24.3 %collective-permute-done.8 = bf16[144,768]{1,0:T(8,128)(2,1)S(1)} collective-permute-done((bf16[144,768]{1,0:T(8,128)(2,1)S(1)}, bf16[144,768]{1,0:T(8,128)(2,1)S(1)}, u32[]{:S(2)}, u32[]{:S(2)}) %collective-permute-start.8) | collective-permute-done | bytes 221216 | tf_op jit(solution)/shard_map/ppermute | solution.py:426
  101.8 22.7 %collective-permute-done.14 = bf16[320,2048]{1,0:T(8,128)(2,1)} collective-permute-done((bf16[320,2048]{1,0:T(8,128)(2,1)}, bf16[320,2048]{1,0:T(8,128)(2,1)}, u32[]{:S(2)}, u32[]{:S(2)}) %collective-permute-start.14) | collective-permute-done | bytes 1310752 | tf_op jit(solution)/shard_map/ppermute | solution.py:426
  129.7 27.5 %collective-permute-done.17 = bf16[320,2048]{1,0:T(8,128)(2,1)} collective-permute-done((bf16[320,2048]{1,0:T(8,128)(2,1)}, bf16[320,2048]{1,0:T(8,128)(2,1)}, u32[]{:S(2)}, u32[]{:S(2)}) %collective-permute-start.17) | collective-permute-done | bytes 1310752 | tf_op jit(solution)/shard_map/ppermute | solution.py:426
  178.7 9.5 %fusion.17 = (bf16[640,2048]{1,0:T(8,128)(2,1)}, bf16[640,2048]{1,0:T(8,128)(2,1)}, bf16[640,2048]{1,0:T(8,128)(2,1)}) fusion(f32[640]{0:T(1024)S(1)} %add_rsqrt_fusion, f32[640]{0:T(1024)S(1)} %broadcast_multiply_fusion, f32[2048]{0:T(1024)S(1)} %reshape.699, f32[2048]{0:T(1024)S(1)} %reshape.698, bf16[320,2048]{1,0:T(8,128)(2,1)} %collective-permute-done.19, ...), kind=kLoop, calls=%fused_computation.31 | loop fusion | flops 35389440 | bytes 15760384 | tf_op jit(solution)/shard_map/convert_element_type | solution.py:602
  190.0 12.2 %collective-permute-done.20 = bf16[2,64,2048]{2,1,0:T(8,128)(2,1)S(1)} collective-permute-done((bf16[2,64,2048]{2,1,0:T(8,128)(2,1)S(1)}, bf16[2,64,2048]{2,1,0:T(8,128)(2,1)S(1)}, u32[]{:S(2)}, u32[]{:S(2)}) %collective-permute-start.20) | collective-permute-done | bytes 524320 | tf_op jit(solution)/shard_map/ppermute | solution.py:426
  216.3 8.3 all-gather.11.cloned.1.call-done
  237.2 42.6 %shard_map.339 = (bf16[2560,256]{1,0:T(8,128)(2,1)S(1)}, f32[256,2560]{1,0:T(8,128)}, f32[8,2560]{1,0:T(8,128)S(1)}) custom-call(s32[9]{0:T(128)S(1)} %stack.212.refs_0_, s32[2560,1]{1,0:T(8,128)} %broadcast_in_dim.171.refs_1_.refs_3_, s32[1,2560]{1,0:T(1,128)S(1)} %broadcast_in_dim.78.refs_2_.refs_4_, s32[1,2560]{1,0:T(1,128)S(1)} %broadcast_in_dim.79.refs_3_.refs_5_, ...), custom_call_target="tpu_custom_call" | custom-call | flops 13421772800 | bytes 7864320 | tf_op jit(solution)/shard_map/pallas_call | solution.py:128
  331.5 36.3 %collective-permute-done.32 = bf16[256,2048]{1,0:T(8,128)(2,1)} collective-permute-done((bf16[256,2048]{1,0:T(8,128)(2,1)}, bf16[256,2048]{1,0:T(8,128)(2,1)}, u32[]{:S(2)}, u32[]{:S(2)}) %collective-permute-start.32) | collective-permute-done | bytes 1048608 | tf_op jit(solution)/shard_map/ppermute | solution.py:426
  385.2 20.0 %multiply_convert_fusion = (bf16[1280,2048]{1,0:T(8,128)(2,1)S(1)}, f32[1280,2048]{1,0:T(8,128)}) fusion(f32[2048]{0:T(1024)S(1)} %bitcast.292, bf16[2048,2048]{1,0:T(8,128)(2,1)} %bitcast.59.right_ref, bf16[320,2048]{1,0:T(8,128)(2,1)} %collective-permute-done.29.refs_3_, bf16[320,2048]{1,0:T(8,128)(2,1)S(1)} %collective-permute-done.28.refs_2_, ...), kind=kOutput, calls=%fused_computation.8 | convolution fusion | flops 10774118400 | bytes 29368320 | tf_op jit(solution)/shard_map/dot_general | solution.py:22
  407.6 15.4 %convolution_convert_fusion = bf16[2048,2048]{1,0:T(8,128)(2,1)} fusion(bf16[1280,2048]{1,0:T(8,128)(2,1)S(1)} %get-tuple-element.160.left_ref, bf16[320,2048]{1,0:T(8,128)(2,1)} %collective-permute-done.31, bf16[320,2048]{1,0:T(8,128)(2,1)} %collective-permute-done.21, bf16[320,2048]{1,0:T(8,128)(2,1)} %collective-permute-done.30, ...), kind=kOutput, calls=%fused_computation.11 | convolution fusion | flops 10762584064 | bytes 18874368 | tf_op jit(solution)/shard_map/dot_general | solution.py:22
  428.0 19.2 %convert_reduce_fusion = (f32[2048]{0:T(1024)S(1)}, bf16[1280,2048]{1,0:T(8,128)(2,1)S(1)}) fusion(f32[1280,2048]{1,0:T(8,128)} %get-tuple-element.389, f32[2048]{0:T(1024)S(1)} %bitcast.293, bf16[1280,2048]{1,0:T(8,128)(2,1)S(1)} %bitcast.254, bf16[2048,2048]{1,0:T(8,128)(2,1)} %bitcast.246), kind=kOutput, calls=%fused_computation.7 | convolution fusion | flops 10771494912 | bytes 29376512 | tf_op jit(solution)/shard_map/dot_general | solution.py:22
  447.2 10.0 %convolution_convert_fusion.1 = bf16[640,2048]{1,0:T(8,128)(2,1)S(1)} fusion(bf16[2048,2048]{1,0:T(8,128)(2,1)} %bitcast.59.right_ref, bf16[1280,2048]{1,0:T(8,128)(2,1)S(1)} %get-tuple-element.168.refs_4_), kind=kOutput, calls=%fused_computation.59 | convolution fusion | flops 5370019840 | bytes 13631488 | tf_op jit(solution)/shard_map/dot_general | solution.py:22
  461.4 8.2 shard_map.341
  469.5 15.3 %shard_map.340 = bf16[1280,2048]{1,0:T(8,128)(2,1)S(1)} custom-call(bf16[1280,2048]{1,0:T(8,128)(2,1)} %copy-done.28, bf16[2048,2048]{1,0:T(8,128)(2,1)} %bitcast.247), custom_call_target="tpu_custom_call" | custom-call | flops 1048576 | bytes 65536 | tf_op jit(solution)/shard_map/pallas_call | solution.py:284
  484.9 7.1 collective-permute-done.34
  521.1 6.9 shard_map.343
  532.8 22.8 %shard_map.342 = bf16[2048,2048]{1,0:T(8,128)(2,1)} custom-call(bf16[320,2048]{1,0:T(8,128)(2,1)} %copy-done.27, bf16[320,2048]{1,0:T(8,128)(2,1)} %collective-permute-done.27.refs_1_, bf16[320,2048]{1,0:T(8,128)(2,1)} %copy-done.40, bf16[320,2048]{1,0:T(8,128)(2,1)} %collective-permute-done.29.refs_3_, bf16[1280,2048]{1,0:T(8,128)(2,1)} %copy-done.22), custom_call_target="tpu_custom_call" | custom-call | flops 2684354560 | bytes 65536 | tf_op jit(solution)/shard_map/pallas_call | solution.py:332
  560.5 61.8 %shard_map.344 = (bf16[2560,768]{1,0:T(8,128)(2,1)}, bf16[2560,768]{1,0:T(8,128)(2,1)}) custom-call(s32[9]{0:T(128)} %copy-done.3, f32[256,2560]{1,0:T(8,128)} %get-tuple-element.163.refs_1_, f32[8,2560]{1,0:T(8,128)} %copy-done.8, s32[2560,1]{1,0:T(8,128)} %broadcast_in_dim.171.refs_1_.refs_3_, s32[1,2560]{1,0:T(1,128)} %copy-done.2, s32[1,2560]{1,0:T(1,128)} %copy-done.1, ...), custom_call_target="tpu_custom_call" | custom-call | flops 18454937600 | bytes 13107200 | tf_op jit(solution)/shard_map/pallas_call | solution.py:259
  660.5 15.0 %shard_map.345 = bf16[2048,768]{1,0:T(8,128)(2,1)} custom-call(bf16[640,2048]{1,0:T(8,128)(2,1)} %fusion.29.refs_0_, bf16[640,2048]{1,0:T(8,128)(2,1)} %get-tuple-element.190.refs_1_, bf16[640,2048]{1,0:T(8,128)(2,1)} %get-tuple-element.191.refs_2_, bf16[640,2048]{1,0:T(8,128)(2,1)} %get-tuple-element.192.refs_3_, bf16[2560,768]{1,0:T(8,128)(2,1)} %get-tuple-element.196.refs_4_), custom_call_target="tpu_custom_call" | custom-call | flops 2013265920 | bytes 65536 | tf_op jit(solution)/shard_map/pallas_call | solution.py:332
  675.5 20.3 %collective-permute-done.50 = bf16[256,2048]{1,0:T(8,128)(2,1)} collective-permute-done((bf16[256,2048]{1,0:T(8,128)(2,1)}, bf16[256,2048]{1,0:T(8,128)(2,1)}, u32[]{:S(2)}, u32[]{:S(2)}) %collective-permute-start.50) | collective-permute-done | bytes 1048608 | tf_op jit(solution)/shard_map/ppermute | solution.py:426
  727.9 9.5 %collective-permute-done.54 = bf16[2,64,2048]{2,1,0:T(8,128)(2,1)S(1)} collective-permute-done((bf16[2,64,2048]{2,1,0:T(8,128)(2,1)}, bf16[2,64,2048]{2,1,0:T(8,128)(2,1)S(1)}, u32[]{:S(2)}, u32[]{:S(2)}) %collective-permute-start.54) | collective-permute-done | bytes 524320 | tf_op jit(solution)/shard_map/ppermute | solution.py:426
  744.1 20.8 %collective-permute-done.51 = bf16[320,2048]{1,0:T(8,128)(2,1)} collective-permute-done((bf16[320,2048]{1,0:T(8,128)(2,1)}, bf16[320,2048]{1,0:T(8,128)(2,1)}, u32[]{:S(2)}, u32[]{:S(2)}) %collective-permute-start.51) | collective-permute-done | bytes 1310752 | tf_op jit(solution)/shard_map/ppermute | solution.py:426
  789.2 29.4 %collective-permute-done.58 = bf16[2,64,768]{2,1,0:T(8,128)(2,1)S(1)} collective-permute-done((bf16[2,64,768]{2,1,0:T(8,128)(2,1)S(1)}, bf16[2,64,768]{2,1,0:T(8,128)(2,1)S(1)}, u32[]{:S(2)}, u32[]{:S(2)}) %collective-permute-start.58) | collective-permute-done | bytes 196640 | tf_op jit(solution)/shard_map/ppermute | solution.py:426
  838.2 6.7 fusion.51
  (508 shorter events, 378.6 us)
Async XLA Ops:
  7.2 80.4 %all-gather.7.cloned.1.call-start = ((), (), s32[]{:S(2)}) async-start(), calls=%async_computation.5 | async-start | bytes 5242880 | tf_op jit(solution)/shard_map/all_gather | solution.py:510
  8.0 159.9 %all-gather.9.cloned.1.call-start = ((), (), s32[]{:S(2)}) async-start(), calls=%async_computation.6 | async-start | bytes 3932160 | tf_op jit(solution)/shard_map/all_gather | solution.py:510
  88.5 136.0 %all-gather.11.cloned.1.call-start = ((), (), s32[]{:S(2)}) async-start(), calls=%async_computation.7 | async-start | bytes 5242880 | tf_op jit(solution)/shard_map/all_gather | solution.py:510
  167.9 133.7 %all-gather.13.cloned.1.call-start = ((), (), s32[]{:S(2)}) async-start(), calls=%async_computation.8 | async-start | bytes 5242880 | tf_op jit(solution)/shard_map/all_gather | solution.py:510
  224.6 143.5 %all-gather.15.cloned.1.call-start = ((), (), s32[]{:S(2)}) async-start(), calls=%async_computation.9 | async-start | bytes 5242880 | tf_op jit(solution)/shard_map/all_gather | solution.py:510
  228.3 53.3 %collective-permute-start.21 = (bf16[320,2048]{1,0:T(8,128)(2,1)}, bf16[320,2048]{1,0:T(8,128)(2,1)}, u32[]{:S(2)}, u32[]{:S(2)}) collective-permute-start(bf16[320,2048]{1,0:T(8,128)(2,1)} %get-tuple-element.135), channel_id=1, source_target_pairs={{0,2},{1,3},{2,0},{3,1},{4,6},{5,7},{6,4},{7,5},{8,10},{9,11},{10,... | collective-permute-start | bytes 3932168 | tf_op jit(solution)/shard_map/ppermute | solution.py:426
  232.1 48.5 %collective-permute-start.22 = (bf16[256,2048]{1,0:T(8,128)(2,1)}, bf16[256,2048]{1,0:T(8,128)(2,1)}, u32[]{:S(2)}, u32[]{:S(2)}) collective-permute-start(bf16[256,2048]{1,0:T(8,128)(2,1)} %bitcast.122), channel_id=1, source_target_pairs={{0,4},{1,5},{2,6},{3,7},{4,0},{5,1},{6,2},{7,3},{8,12},{9,13},{10,... | collective-permute-start | bytes 3145736 | tf_op jit(solution)/shard_map/ppermute | solution.py:426
  281.6 141.4 %all-gather.17.cloned.1.call-start = ((), (), s32[]{:S(2)}) async-start(), calls=%async_computation.10 | async-start | bytes 5242880 | tf_op jit(solution)/shard_map/all_gather | solution.py:510
  314.7 53.2 %collective-permute-start.32 = (bf16[256,2048]{1,0:T(8,128)(2,1)}, bf16[256,2048]{1,0:T(8,128)(2,1)}, u32[]{:S(2)}, u32[]{:S(2)}) collective-permute-start(bf16[256,2048]{1,0:T(8,128)(2,1)} %param.36), channel_id=1, source_target_pairs={{0,4},{1,5},{2,6},{3,7},{4,0},{5,1},{6,2},{7,3},{8,12},{9,13},{10,... | collective-permute-start | bytes 3145736 | tf_op jit(solution)/shard_map/ppermute | solution.py:426
  327.0 52.4 %collective-permute-start.28 = (bf16[320,2048]{1,0:T(8,128)(2,1)S(1)}, bf16[320,2048]{1,0:T(8,128)(2,1)S(1)}, u32[]{:S(2)}, u32[]{:S(2)}) collective-permute-start(bf16[320,2048]{1,0:T(8,128)(2,1)S(1)} %add_convert_fusion.7.refs_0_), channel_id=1, source_target_pairs={{0,2},{1,3},{2,0},{3,1},{4,6},{5,7},{6,4},{7,5},{8,10},{9,11},{10,... | collective-permute-start | bytes 3932168 | tf_op jit(solution)/shard_map/ppermute | solution.py:426
  331.0 48.4 %collective-permute-start.30 = (bf16[320,2048]{1,0:T(8,128)(2,1)}, bf16[320,2048]{1,0:T(8,128)(2,1)}, u32[]{:S(2)}, u32[]{:S(2)}) collective-permute-start(bf16[320,2048]{1,0:T(8,128)(2,1)} %get-tuple-element.135), channel_id=1, source_target_pairs={{0,1},{1,0},{2,3},{3,2},{4,5},{5,4},{6,7},{7,6},{8,9},{9,8},{10,11... | collective-permute-start | bytes 3932168 | tf_op jit(solution)/shard_map/ppermute | solution.py:426
  331.0 48.4 %collective-permute-start.31 = (bf16[320,2048]{1,0:T(8,128)(2,1)}, bf16[320,2048]{1,0:T(8,128)(2,1)}, u32[]{:S(2)}, u32[]{:S(2)}) collective-permute-start(bf16[320,2048]{1,0:T(8,128)(2,1)} %collective-permute-done.21), channel_id=1, source_target_pairs={{0,1},{1,0},{2,3},{3,2},{4,5},{5,4},{6,7},{7,6},{8,9},{9,8},{10,11... | collective-permute-start | bytes 3932168 | tf_op jit(solution)/shard_map/ppermute | solution.py:426
  367.9 189.5 %reduce-scatter.5.cloned.1.call-start = ((), (), s32[]{:S(2)}) async-start(), calls=%async_computation.11 | async-start | bytes 10485760 | tf_op jit(solution)/shard_map/reduce_scatter | solution.py:513
  423.0 221.6 %reduce-scatter.7.cloned.1.call-start = ((), (), s32[]{:S(2)}) async-start(), calls=%async_computation.12 | async-start | bytes 10485760 | tf_op jit(solution)/shard_map/reduce_scatter | solution.py:513
  556.6 141.2 %reduce-scatter.9.cloned.1.call-start = ((), (), s32[]{:S(2)}) async-start(), calls=%async_computation.13 | async-start | bytes 5242880 | tf_op jit(solution)/shard_map/reduce_scatter | solution.py:513
  557.3 213.8 %reduce-scatter.11.cloned.1.call-start = ((), (), s32[]{:S(2)}) async-start(), calls=%async_computation.14 | async-start | bytes 3932160 | tf_op jit(solution)/shard_map/reduce_scatter | solution.py:513
  559.7 62.6 %collective-permute-start.42 = (bf16[256,2048]{1,0:T(8,128)(2,1)}, bf16[256,2048]{1,0:T(8,128)(2,1)}, u32[]{:S(2)}, u32[]{:S(2)}) collective-permute-start(bf16[256,2048]{1,0:T(8,128)(2,1)} %dynamic-slice_bitcast_fusion.1), channel_id=1, source_target_pairs={{0,4},{1,5},{2,6},{3,7},{4,0},{5,1},{6,2},{7,3},{8,12},{9,13},{10,... | collective-permute-start | bytes 3145736 | tf_op jit(solution)/shard_map/ppermute | solution.py:426
  559.9 65.6 %collective-permute-start.43 = (bf16[320,2048]{1,0:T(8,128)(2,1)}, bf16[320,2048]{1,0:T(8,128)(2,1)}, u32[]{:S(2)}, u32[]{:S(2)}) collective-permute-start(bf16[320,2048]{1,0:T(8,128)(2,1)} %add_convert_fusion.5), channel_id=1, source_target_pairs={{0,2},{1,3},{2,0},{3,1},{4,6},{5,7},{6,4},{7,5},{8,10},{9,11},{10,... | collective-permute-start | bytes 3932168 | tf_op jit(solution)/shard_map/ppermute | solution.py:426
  636.1 61.7 %collective-permute-start.44 = (bf16[320,2048]{1,0:T(8,128)(2,1)}, bf16[320,2048]{1,0:T(8,128)(2,1)}, u32[]{:S(2)}, u32[]{:S(2)}) collective-permute-start(bf16[320,2048]{1,0:T(8,128)(2,1)} %convolution_convert_fusion.5), channel_id=1, source_target_pairs={{0,1},{1,0},{2,3},{3,2},{4,5},{5,4},{6,7},{7,6},{8,9},{9,8},{10,11... | collective-permute-start | bytes 3932168 | tf_op jit(solution)/shard_map/ppermute | solution.py:426
  639.4 58.3 %collective-permute-start.46 = (bf16[320,2048]{1,0:T(8,128)(2,1)}, bf16[320,2048]{1,0:T(8,128)(2,1)}, u32[]{:S(2)}, u32[]{:S(2)}) collective-permute-start(bf16[320,2048]{1,0:T(8,128)(2,1)} %convolution_convert_fusion.3), channel_id=1, source_target_pairs={{0,1},{1,0},{2,3},{3,2},{4,5},{5,4},{6,7},{7,6},{8,9},{9,8},{10,11... | collective-permute-start | bytes 3932168 | tf_op jit(solution)/shard_map/ppermute | solution.py:426
  646.9 48.9 %collective-permute-start.50 = (bf16[256,2048]{1,0:T(8,128)(2,1)}, bf16[256,2048]{1,0:T(8,128)(2,1)}, u32[]{:S(2)}, u32[]{:S(2)}) collective-permute-start(bf16[256,2048]{1,0:T(8,128)(2,1)} %dynamic-slice_bitcast_fusion), channel_id=1, source_target_pairs={{0,4},{1,5},{2,6},{3,7},{4,0},{5,1},{6,2},{7,3},{8,12},{9,13},{10,... | collective-permute-start | bytes 3145736 | tf_op jit(solution)/shard_map/ppermute | solution.py:426
  654.3 46.4 %collective-permute-start.48 = (bf16[320,2048]{1,0:T(8,128)(2,1)}, bf16[320,2048]{1,0:T(8,128)(2,1)}, u32[]{:S(2)}, u32[]{:S(2)}) collective-permute-start(bf16[320,2048]{1,0:T(8,128)(2,1)} %get-tuple-element.195), channel_id=1, source_target_pairs={{0,2},{1,3},{8,10},{9,11},{16,18},{17,19},{24,26},{25,27}} | collective-permute-start | bytes 3932168 | tf_op jit(solution)/shard_map/ppermute | solution.py:426
  776.0 62.2 %collective-permute-start.55 = (bf16[320,2048]{1,0:T(8,128)(2,1)}, bf16[320,2048]{1,0:T(8,128)(2,1)}, u32[]{:S(2)}, u32[]{:S(2)}) collective-permute-start(bf16[320,2048]{1,0:T(8,128)(2,1)} %add_convert_fusion.1), channel_id=1, source_target_pairs={{0,2},{1,3},{2,4},{3,5},{4,6},{5,7},{8,10},{9,11},{10,12},{11,13},... | collective-permute-start | bytes 3932168 | tf_op jit(solution)/shard_map/ppermute | solution.py:426
  780.1 58.1 %collective-permute-start.56 = (bf16[320,2048]{1,0:T(8,128)(2,1)}, bf16[320,2048]{1,0:T(8,128)(2,1)}, u32[]{:S(2)}, u32[]{:S(2)}) collective-permute-start(bf16[320,2048]{1,0:T(8,128)(2,1)} %add_convert_fusion), channel_id=1, source_target_pairs={{2,0},{3,1},{4,2},{5,3},{6,4},{7,5},{10,8},{11,9},{12,10},{13,11},... | collective-permute-start | bytes 3932168 | tf_op jit(solution)/shard_map/ppermute | solution.py:426
  (125 other events, 2139.9 us)
Sparse Core Ops, SparseCore 0:
  9.9 55.5 all-gather.6
  88.6 46.1 all-gather.8
  168.1 56.4 all-gather.10
  226.8 52.8 all-gather.12
  281.8 52.6 all-gather.14
  368.0 52.9 all-gather.16
  424.0 87.8 reduce-scatter.4
  555.8 83.8 reduce-scatter.6
  642.7 52.6 reduce-scatter.8
  700.8 43.1 reduce-scatter.10

commit v4 on v3

--- a/solution.py
+++ b/solution.py
@@ -619,12 +619,7 @@
 
         other = swap(clock.hold(gathered_o), near)
         gathered_o = join(gathered_o, other, near, 1)
-        qkv = []
-        for n in range(n_z):
-            if n >= n_z - 2:
-                normed.append(rows_from(n))
-            qkv.append(qkv_of(normed[n]))
-        gathered_o, unused = lax.optimization_barrier((gathered_o, (up_own, *qkv)))
+        gathered_o, unused = lax.optimization_barrier((gathered_o, up_own))
         gathered_o = batch_gather(gathered_o.reshape(n_z * part, model))
 
         weight_o = gathered_o.reshape(n_batch, n_z, part, model)
@@ -635,6 +630,11 @@
             weight_o = weight_o.reshape(heads, n_z, 2, HEAD_DIM, model)
             weight_o = pick(weight_o, c_here, 2).transpose(1, 0, 2, 3).reshape(n_z * span, model)
 
+        qkv = []
+        for n in range(n_z):
+            if n >= n_z - 2:
+                normed.append(rows_from(n))
+            qkv.append(qkv_of(normed[n]))
         shifted = [z_here] + [(z_here - d) % n_z for d in range(1, n_z)]
         spots = jnp.stack([c_here] + [source(n) for n in range(n_z)] + shifted).astype(jnp.int32)
 
@@ -717,7 +717,11 @@
         back = swap(back_held, near)
         share_n = matmul_low(pre_held[: 2 * width], weight_up, True)
         out_share = matmul_low(hidden_held, weight_down, False)
-        back, out_share, share_n = lax.optimization_barrier((back, out_share, share_n))
+        *normed_late, unused = lax.optimization_barrier((*normed_parts, back_held))
+        normed_late = jnp.concatenate(normed_late, axis=0)
+        back, out_share, share_n, normed_late = lax.optimization_barrier(
+            (back, out_share, share_n, normed_late)
+        )
         here = swap(share_n[width:], core)
         normed_grad = share_n[:width].astype(F32) + here.astype(F32) + back.astype(F32)
 
@@ -736,7 +740,7 @@
         grad_gate, branch_gate, mixed_gate, unused = lax.optimization_barrier(
             (pre_grad, branch_grad, mixed_low, mixed_grad)
         )
-        grad_up = rows_product(normed_parts, grad_gate)
+        grad_up = matmul_transposed(normed_late, grad_gate)
         grad_out = matmul_transposed(mixed_gate, branch_gate)
         if exact:
             grad_out = grad_out.reshape(n_z, n_batch, part, model).transpose(1, 0, 2, 3)
@@ -752,7 +756,6 @@
         rows_grad = [piece for unused, piece in placed]
         out_back = swap(out_share[3 * width :], core)
         out_back = (out_share[2 * width : 3 * width].astype(F32) + out_back.astype(F32)).astype(BF16)
-        out_here = swap(out_share[width : 2 * width], core)
         grad_up, grad_out, out_back, *rows_grad = lax.optimization_barrier(
             (grad_up, grad_out, out_back, *rows_grad)
         )
@@ -777,7 +780,6 @@
         qkv_grad, relative, grad_down, out_back = lax.optimization_barrier(
             (qkv_grad, relative, grad_down, out_back)
         )
-        bias_sums = jnp.sum(qkv_grad.astype(F32), axis=0)
         clock.tick(qkv_grad, grad_down, out_back)
 
         chunks = [None] * n_z
@@ -832,12 +834,18 @@
                     pick(grad_qkv, c_here, 1), swap(pick(grad_qkv, 1 - c_here, 1), core), core, 1
                 )
                 placed = shift_out(lambda z: pick(grad_qkv, z, 0))
+                out_share, out_back, grads_late = clock.hold(out_share, out_back, qkv_grad)
+                out_here = swap(out_share[width : 2 * width], core)
+                final = out_share[:width].astype(F32) + out_here.astype(F32) + out_back.astype(F32)
+                final = resid + validity * (final + bias_down)
+                out_rows = final.astype(BF16)
+                bias_sums = jnp.sum(grads_late.astype(F32), axis=0)
                 grad_out = clock.hold(grad_out)
                 for n, which in enumerate(far_bits):
                     grad_out, rest_o = hop_scatter(grad_out, rest_o, which, n == len(far_bits) - 1)
             clock.tick(*started)
         right, left, unused = lax.optimization_barrier(
-            (right, left, tuple(piece for unused, piece in placed[1:]))
+            (right, left, (out_rows, bias_sums, *[piece for unused, piece in placed[1:]]))
         )
         normed_back = chunks[0] + right.astype(F32) + left.astype(F32)
 
@@ -845,9 +853,6 @@
         grad_up = grad_up.reshape(4, part, groups, unit).transpose(1, 2, 0, 3)
         grad_up = grad_up.reshape(part, n_dev * unit).astype(F32)
 
-        final = out_share[:width].astype(F32) + out_here.astype(F32) + out_back.astype(F32)
-        final = resid + validity * (final + bias_down)
-        out_rows = final.astype(BF16)
 
         shares = jnp.zeros((n_z, 2, part, 3 * span), BF16)
         for z, piece in placed:

time: 877 us -> 849 us (0.968)
  waiting for transfers between devices: 254 us -> 238 us
  starting transfers between devices: 93.3 us -> 109 us
  other arithmetic: 101 us -> 92.1 us
    pallas_call x2 -> x1, Pallas kernels: 37.8 us -> 15.2 us  [rows_product(): pl.pallas_call(rows_product_kernel, grid=(columns // step,), out_shape=ja...]
    pallas_call x1 -> x2, Pallas kernels: 6.95 us -> 22.9 us  [matmul_transposed(): pl.pallas_call(transposed_kernel, grid=(rows // step,), out_shape=jax.Sha...]
    all_gather x6, starting transfers between devices: 0.23 us -> 12.1 us  [batch_gather(): return lax.all_gather(array, 'batch', axis=0, tiled=True)]
  transfers between devices with their start and end apart: 74 -> 74, of which waited for: 25 -> 26; matrix products, arithmetic and copies ran while one was open for 36% -> 35% of each run, Pallas kernels for 20% -> 20%
where the time goes in v4:
time: 849 us; the launch traced here: 845 us
  waiting for transfers between devices  238 us (28%)
  Pallas kernels  167 us (20%)
  matrix products  126 us (15%)
  starting transfers between devices  109 us (13%)
  local copies, waits for them, and re-layouts  95.9 us (11%)
  other arithmetic  92.1 us (11%)
  between operations  16.6 us (2%)
    ppermute x63, waiting for transfers between devices, permute(): return lax.ppermute(array, pairs[0], pairs[1])  234 us
    dot_general x19, matrix products, contract(): lax.dot_general(left, right, (((left_dim,), (right_dim,)), ((), ())), pre...  126 us
    ppermute x63, starting transfers between devices, permute(): return lax.ppermute(array, pairs[0], pairs[1])  90.6 us
    pallas_call x1, Pallas kernels, attention_backward(): pl.pallas_call(functools.partial(backward_kernel, devices, pre, tok, head...  62.8 us
    pallas_call x1, Pallas kernels, attention_forward(): pl.pallas_call(functools.partial(forward_kernel, devices, pre, tok, heads...  42.6 us
    pallas_call x2, Pallas kernels, matmul_low(): pl.pallas_call(functools.partial(matmul_kernel, flipped), grid=(columns /...  23.5 us
    pallas_call x2, Pallas kernels, matmul_transposed(): pl.pallas_call(transposed_kernel, grid=(rows // step,), out_shape=jax.Sha...  22.9 us
  transfers between devices with their start and end apart: 74, of which 26 were waited for; matrix products, arithmetic and copies ran while one was open for 35% of the time, Pallas kernels for 20%

profile of v4, /device:TPU:0, one launch (start us, length us, event | category | flops | bytes accessed | tf_op | source)
XLA Modules:
  0.0 844.6 jit_solution(3252350266392255874)
XLA Ops:
  60.1 11.4 %collective-permute-done.9 = bf16[144,768]{1,0:T(8,128)(2,1)S(1)} collective-permute-done((bf16[144,768]{1,0:T(8,128)(2,1)S(1)}, bf16[144,768]{1,0:T(8,128)(2,1)S(1)}, u32[]{:S(2)}, u32[]{:S(2)}) %collective-permute-start.9) | collective-permute-done | bytes 221216 | tf_op jit(solution)/shard_map/ppermute | solution.py:426
  78.4 10.4 %collective-permute-done.13 = bf16[64,2048]{1,0:T(8,128)(2,1)S(1)} collective-permute-done((bf16[64,2048]{1,0:T(8,128)(2,1)}, bf16[64,2048]{1,0:T(8,128)(2,1)S(1)}, u32[]{:S(2)}, u32[]{:S(2)}) %collective-permute-start.13) | collective-permute-done | bytes 262176 | tf_op jit(solution)/shard_map/ppermute | solution.py:426
  105.3 22.2 %collective-permute-done.14 = bf16[320,2048]{1,0:T(8,128)(2,1)} collective-permute-done((bf16[320,2048]{1,0:T(8,128)(2,1)}, bf16[320,2048]{1,0:T(8,128)(2,1)}, u32[]{:S(2)}, u32[]{:S(2)}) %collective-permute-start.14) | collective-permute-done | bytes 1310752 | tf_op jit(solution)/shard_map/ppermute | solution.py:426
  135.4 24.2 %collective-permute-done.17 = bf16[320,2048]{1,0:T(8,128)(2,1)} collective-permute-done((bf16[320,2048]{1,0:T(8,128)(2,1)}, bf16[320,2048]{1,0:T(8,128)(2,1)}, u32[]{:S(2)}, u32[]{:S(2)}) %collective-permute-start.17) | collective-permute-done | bytes 1310752 | tf_op jit(solution)/shard_map/ppermute | solution.py:426
  170.9 7.0 fusion.17
  178.2 13.9 %collective-permute-done.20 = bf16[2,64,2048]{2,1,0:T(8,128)(2,1)S(1)} collective-permute-done((bf16[2,64,2048]{2,1,0:T(8,128)(2,1)S(1)}, bf16[2,64,2048]{2,1,0:T(8,128)(2,1)S(1)}, u32[]{:S(2)}, u32[]{:S(2)}) %collective-permute-start.20) | collective-permute-done | bytes 524320 | tf_op jit(solution)/shard_map/ppermute | solution.py:426
  193.2 11.9 %all-gather.15.cloned.1.call-start = ((), (), s32[]{:S(2)}) async-start(), calls=%async_computation.9 | async-start | bytes 5242880 | tf_op jit(solution)/shard_map/all_gather | solution.py:510
  234.6 42.6 %shard_map.339 = (bf16[2560,256]{1,0:T(8,128)(2,1)S(1)}, f32[256,2560]{1,0:T(8,128)}, f32[8,2560]{1,0:T(8,128)S(1)}) custom-call(s32[9]{0:T(128)S(1)} %stack.212.refs_0_, s32[2560,1]{1,0:T(8,128)} %broadcast_in_dim.171.refs_1_.refs_3_, s32[1,2560]{1,0:T(1,128)S(1)} %broadcast_in_dim.78.refs_2_.refs_4_, s32[1,2560]{1,0:T(1,128)S(1)} %broadcast_in_dim.79.refs_3_.refs_5_, ...), custom_call_target="tpu_custom_call" | custom-call | flops 13421772800 | bytes 7864320 | tf_op jit(solution)/shard_map/pallas_call | solution.py:128
  324.4 36.1 %collective-permute-done.32 = bf16[256,2048]{1,0:T(8,128)(2,1)} collective-permute-done((bf16[256,2048]{1,0:T(8,128)(2,1)}, bf16[256,2048]{1,0:T(8,128)(2,1)}, u32[]{:S(2)}, u32[]{:S(2)}) %collective-permute-start.32) | collective-permute-done | bytes 1048608 | tf_op jit(solution)/shard_map/ppermute | solution.py:426
  377.7 20.0 %multiply_convert_fusion = (bf16[1280,2048]{1,0:T(8,128)(2,1)S(1)}, f32[1280,2048]{1,0:T(8,128)}) fusion(f32[2048]{0:T(1024)S(1)} %bitcast.295, bf16[2048,2048]{1,0:T(8,128)(2,1)} %bitcast.59.right_ref, bf16[320,2048]{1,0:T(8,128)(2,1)} %collective-permute-done.29, bf16[320,2048]{1,0:T(8,128)(2,1)S(1)} %collective-permute-done.28, ...), kind=kOutput, calls=%fused_computation.8 | convolution fusion | flops 10774118400 | bytes 29368320 | tf_op jit(solution)/shard_map/dot_general | solution.py:22
  400.1 15.3 %convolution_convert_fusion = bf16[2048,2048]{1,0:T(8,128)(2,1)} fusion(bf16[1280,2048]{1,0:T(8,128)(2,1)S(1)} %get-tuple-element.168.left_ref, bf16[320,2048]{1,0:T(8,128)(2,1)} %collective-permute-done.31, bf16[320,2048]{1,0:T(8,128)(2,1)} %collective-permute-done.21, bf16[320,2048]{1,0:T(8,128)(2,1)} %collective-permute-done.30, ...), kind=kOutput, calls=%fused_computation.11 | convolution fusion | flops 10762584064 | bytes 18874368 | tf_op jit(solution)/shard_map/dot_general | solution.py:22
  420.4 19.7 %convert_reduce_fusion = (f32[2048]{0:T(1024)S(1)}, bf16[1280,2048]{1,0:T(8,128)(2,1)S(1)}) fusion(f32[1280,2048]{1,0:T(8,128)} %get-tuple-element.403, f32[2048]{0:T(1024)S(1)} %bitcast.296, bf16[1280,2048]{1,0:T(8,128)(2,1)} %pad_maximum_fusion, bf16[2048,2048]{1,0:T(8,128)(2,1)} %bitcast.246), kind=kOutput, calls=%fused_computation.7 | convolution fusion | flops 10771494912 | bytes 29376512 | tf_op jit(solution)/shard_map/dot_general | solution.py:22
  440.1 10.2 %convolution_convert_fusion.1 = bf16[640,2048]{1,0:T(8,128)(2,1)S(1)} fusion(bf16[2048,2048]{1,0:T(8,128)(2,1)} %bitcast.59.right_ref, bf16[1280,2048]{1,0:T(8,128)(2,1)S(1)} %get-tuple-element.181.right_ref), kind=kOutput, calls=%fused_computation.60 | convolution fusion | flops 5370019840 | bytes 13631488 | tf_op jit(solution)/shard_map/dot_general | solution.py:22
  454.7 8.3 shard_map.341
  463.0 15.2 %shard_map.340 = bf16[1280,2048]{1,0:T(8,128)(2,1)S(1)} custom-call(bf16[1280,2048]{1,0:T(8,128)(2,1)} %copy-done.28, bf16[2048,2048]{1,0:T(8,128)(2,1)} %bitcast.247), custom_call_target="tpu_custom_call" | custom-call | flops 1048576 | bytes 65536 | tf_op jit(solution)/shard_map/pallas_call | solution.py:284
  502.9 6.9 collective-permute-start.39
  516.3 7.0 shard_map.343
  528.0 16.0 %shard_map.342 = bf16[2048,2048]{1,0:T(8,128)(2,1)} custom-call(bf16[1280,2048]{1,0:T(8,128)(2,1)} %pad_maximum_fusion.1.left_ref, bf16[1280,2048]{1,0:T(8,128)(2,1)} %copy-done.23), custom_call_target="tpu_custom_call" | custom-call | flops 1048576 | bytes 65536 | tf_op jit(solution)/shard_map/pallas_call | solution.py:306
  547.7 62.8 %shard_map.344 = (bf16[2560,768]{1,0:T(8,128)(2,1)}, bf16[2560,768]{1,0:T(8,128)(2,1)}) custom-call(s32[9]{0:T(128)} %copy-done.3, f32[256,2560]{1,0:T(8,128)} %get-tuple-element.175.refs_1_, f32[8,2560]{1,0:T(8,128)} %copy-done.8, s32[2560,1]{1,0:T(8,128)} %broadcast_in_dim.171.refs_1_.refs_3_, s32[1,2560]{1,0:T(1,128)} %copy-done.2, s32[1,2560]{1,0:T(1,128)} %copy-done.1, ...), custom_call_target="tpu_custom_call" | custom-call | flops 18454937600 | bytes 13107200 | tf_op jit(solution)/shard_map/pallas_call | solution.py:259
  649.2 15.2 %shard_map.345 = bf16[2048,768]{1,0:T(8,128)(2,1)} custom-call(bf16[640,2048]{1,0:T(8,128)(2,1)} %fusion.29.refs_0_, bf16[640,2048]{1,0:T(8,128)(2,1)} %get-tuple-element.203.refs_1_, bf16[640,2048]{1,0:T(8,128)(2,1)} %get-tuple-element.204.refs_2_, bf16[640,2048]{1,0:T(8,128)(2,1)} %get-tuple-element.205.refs_3_, bf16[2560,768]{1,0:T(8,128)(2,1)} %get-tuple-element.209.refs_4_), custom_call_target="tpu_custom_call" | custom-call | flops 2013265920 | bytes 65536 | tf_op jit(solution)/shard_map/pallas_call | solution.py:332
  664.4 19.6 %collective-permute-done.48 = bf16[256,2048]{1,0:T(8,128)(2,1)} collective-permute-done((bf16[256,2048]{1,0:T(8,128)(2,1)}, bf16[256,2048]{1,0:T(8,128)(2,1)}, u32[]{:S(2)}, u32[]{:S(2)}) %collective-permute-start.48) | collective-permute-done | bytes 1048608 | tf_op jit(solution)/shard_map/ppermute | solution.py:426
  708.3 7.9 collective-permute-done.53
  722.8 19.6 %collective-permute-done.50 = bf16[320,2048]{1,0:T(8,128)(2,1)} collective-permute-done((bf16[320,2048]{1,0:T(8,128)(2,1)}, bf16[320,2048]{1,0:T(8,128)(2,1)}, u32[]{:S(2)}, u32[]{:S(2)}) %collective-permute-start.50) | collective-permute-done | bytes 1310752 | tf_op jit(solution)/shard_map/ppermute | solution.py:426
  775.6 20.1 %collective-permute-done.58 = bf16[2,64,768]{2,1,0:T(8,128)(2,1)S(1)} collective-permute-done((bf16[2,64,768]{2,1,0:T(8,128)(2,1)S(1)}, bf16[2,64,768]{2,1,0:T(8,128)(2,1)S(1)}, u32[]{:S(2)}, u32[]{:S(2)}) %collective-permute-start.58) | collective-permute-done | bytes 196640 | tf_op jit(solution)/shard_map/ppermute | solution.py:426
  (510 shorter events, 384.5 us)
Async XLA Ops:
  7.2 64.4 %all-gather.7.cloned.1.call-start = ((), (), s32[]{:S(2)}) async-start(), calls=%async_computation.5 | async-start | bytes 5242880 | tf_op jit(solution)/shard_map/all_gather | solution.py:510
  7.9 125.3 %all-gather.9.cloned.1.call-start = ((), (), s32[]{:S(2)}) async-start(), calls=%async_computation.6 | async-start | bytes 3932160 | tf_op jit(solution)/shard_map/all_gather | solution.py:510
  72.6 120.6 %all-gather.11.cloned.1.call-start = ((), (), s32[]{:S(2)}) async-start(), calls=%async_computation.7 | async-start | bytes 5242880 | tf_op jit(solution)/shard_map/all_gather | solution.py:510
  133.2 164.2 %all-gather.13.cloned.1.call-start = ((), (), s32[]{:S(2)}) async-start(), calls=%async_computation.8 | async-start | bytes 5242880 | tf_op jit(solution)/shard_map/all_gather | solution.py:510
  193.2 167.8 %all-gather.15.cloned.1.call-start = ((), (), s32[]{:S(2)}) async-start(), calls=%async_computation.9 | async-start | bytes 5242880 | tf_op jit(solution)/shard_map/all_gather | solution.py:510
  223.4 54.5 %collective-permute-start.21 = (bf16[320,2048]{1,0:T(8,128)(2,1)}, bf16[320,2048]{1,0:T(8,128)(2,1)}, u32[]{:S(2)}, u32[]{:S(2)}) collective-permute-start(bf16[320,2048]{1,0:T(8,128)(2,1)} %get-tuple-element.143), channel_id=1, source_target_pairs={{0,2},{1,3},{2,0},{3,1},{4,6},{5,7},{6,4},{7,5},{8,10},{9,11},{10,... | collective-permute-start | bytes 3932168 | tf_op jit(solution)/shard_map/ppermute | solution.py:426
  225.9 52.0 %collective-permute-start.22 = (bf16[256,2048]{1,0:T(8,128)(2,1)}, bf16[256,2048]{1,0:T(8,128)(2,1)}, u32[]{:S(2)}, u32[]{:S(2)}) collective-permute-start(bf16[256,2048]{1,0:T(8,128)(2,1)} %bitcast.122), channel_id=1, source_target_pairs={{0,4},{1,5},{2,6},{3,7},{4,0},{5,1},{6,2},{7,3},{8,12},{9,13},{10,... | collective-permute-start | bytes 3145736 | tf_op jit(solution)/shard_map/ppermute | solution.py:426
  277.9 137.6 %all-gather.17.cloned.1.call-start = ((), (), s32[]{:S(2)}) async-start(), calls=%async_computation.10 | async-start | bytes 5242880 | tf_op jit(solution)/shard_map/all_gather | solution.py:510
  307.2 53.3 %collective-permute-start.32 = (bf16[256,2048]{1,0:T(8,128)(2,1)}, bf16[256,2048]{1,0:T(8,128)(2,1)}, u32[]{:S(2)}, u32[]{:S(2)}) collective-permute-start(bf16[256,2048]{1,0:T(8,128)(2,1)} %param.36), channel_id=1, source_target_pairs={{0,4},{1,5},{2,6},{3,7},{4,0},{5,1},{6,2},{7,3},{8,12},{9,13},{10,... | collective-permute-start | bytes 3145736 | tf_op jit(solution)/shard_map/ppermute | solution.py:426
  319.8 52.5 %collective-permute-start.28 = (bf16[320,2048]{1,0:T(8,128)(2,1)S(1)}, bf16[320,2048]{1,0:T(8,128)(2,1)S(1)}, u32[]{:S(2)}, u32[]{:S(2)}) collective-permute-start(bf16[320,2048]{1,0:T(8,128)(2,1)S(1)} %add_convert_fusion.7), channel_id=1, source_target_pairs={{0,2},{1,3},{2,0},{3,1},{4,6},{5,7},{6,4},{7,5},{8,10},{9,11},{10,... | collective-permute-start | bytes 3932168 | tf_op jit(solution)/shard_map/ppermute | solution.py:426
  323.9 48.5 %collective-permute-start.30 = (bf16[320,2048]{1,0:T(8,128)(2,1)}, bf16[320,2048]{1,0:T(8,128)(2,1)}, u32[]{:S(2)}, u32[]{:S(2)}) collective-permute-start(bf16[320,2048]{1,0:T(8,128)(2,1)} %get-tuple-element.143), channel_id=1, source_target_pairs={{0,1},{1,0},{2,3},{3,2},{4,5},{5,4},{6,7},{7,6},{8,9},{9,8},{10,11... | collective-permute-start | bytes 3932168 | tf_op jit(solution)/shard_map/ppermute | solution.py:426
  323.9 48.5 %collective-permute-start.31 = (bf16[320,2048]{1,0:T(8,128)(2,1)}, bf16[320,2048]{1,0:T(8,128)(2,1)}, u32[]{:S(2)}, u32[]{:S(2)}) collective-permute-start(bf16[320,2048]{1,0:T(8,128)(2,1)} %collective-permute-done.21), channel_id=1, source_target_pairs={{0,1},{1,0},{2,3},{3,2},{4,5},{5,4},{6,7},{7,6},{8,9},{9,8},{10,11... | collective-permute-start | bytes 3932168 | tf_op jit(solution)/shard_map/ppermute | solution.py:426
  360.5 184.3 %reduce-scatter.5.cloned.1.call-start = ((), (), s32[]{:S(2)}) async-start(), calls=%async_computation.11 | async-start | bytes 10485760 | tf_op jit(solution)/shard_map/reduce_scatter | solution.py:513
  415.5 217.1 %reduce-scatter.7.cloned.1.call-start = ((), (), s32[]{:S(2)}) async-start(), calls=%async_computation.12 | async-start | bytes 10485760 | tf_op jit(solution)/shard_map/reduce_scatter | solution.py:513
  544.0 142.0 %reduce-scatter.9.cloned.1.call-start = ((), (), s32[]{:S(2)}) async-start(), calls=%async_computation.13 | async-start | bytes 5242880 | tf_op jit(solution)/shard_map/reduce_scatter | solution.py:513
  544.7 219.8 %reduce-scatter.11.cloned.1.call-start = ((), (), s32[]{:S(2)}) async-start(), calls=%async_computation.14 | async-start | bytes 3932160 | tf_op jit(solution)/shard_map/reduce_scatter | solution.py:513
  547.1 63.4 %collective-permute-start.41 = (bf16[256,2048]{1,0:T(8,128)(2,1)}, bf16[256,2048]{1,0:T(8,128)(2,1)}, u32[]{:S(2)}, u32[]{:S(2)}) collective-permute-start(bf16[256,2048]{1,0:T(8,128)(2,1)} %dynamic-slice_bitcast_fusion.1), channel_id=1, source_target_pairs={{0,4},{1,5},{2,6},{3,7},{4,0},{5,1},{6,2},{7,3},{8,12},{9,13},{10,... | collective-permute-start | bytes 3145736 | tf_op jit(solution)/shard_map/ppermute | solution.py:426
  547.1 66.5 %collective-permute-start.42 = (bf16[320,2048]{1,0:T(8,128)(2,1)}, bf16[320,2048]{1,0:T(8,128)(2,1)}, u32[]{:S(2)}, u32[]{:S(2)}) collective-permute-start(bf16[320,2048]{1,0:T(8,128)(2,1)} %add_convert_fusion.5), channel_id=1, source_target_pairs={{0,2},{1,3},{2,0},{3,1},{4,6},{5,7},{6,4},{7,5},{8,10},{9,11},{10,... | collective-permute-start | bytes 3932168 | tf_op jit(solution)/shard_map/ppermute | solution.py:426
  624.1 61.9 %collective-permute-start.49 = (bf16[320,2048]{1,0:T(8,128)(2,1)}, bf16[320,2048]{1,0:T(8,128)(2,1)}, u32[]{:S(2)}, u32[]{:S(2)}) collective-permute-start(bf16[320,2048]{1,0:T(8,128)(2,1)} %convolution_convert_fusion.2), channel_id=1, source_target_pairs={{0,1},{1,0},{2,3},{3,2},{4,5},{5,4},{6,7},{7,6},{8,9},{9,8},{10,11... | collective-permute-start | bytes 3932168 | tf_op jit(solution)/shard_map/ppermute | solution.py:426
  627.4 58.5 %collective-permute-start.43 = (bf16[320,2048]{1,0:T(8,128)(2,1)}, bf16[320,2048]{1,0:T(8,128)(2,1)}, u32[]{:S(2)}, u32[]{:S(2)}) collective-permute-start(bf16[320,2048]{1,0:T(8,128)(2,1)} %convolution_convert_fusion.5), channel_id=1, source_target_pairs={{0,1},{1,0},{2,3},{3,2},{4,5},{5,4},{6,7},{7,6},{8,9},{9,8},{10,11... | collective-permute-start | bytes 3932168 | tf_op jit(solution)/shard_map/ppermute | solution.py:426
  634.9 49.1 %collective-permute-start.48 = (bf16[256,2048]{1,0:T(8,128)(2,1)}, bf16[256,2048]{1,0:T(8,128)(2,1)}, u32[]{:S(2)}, u32[]{:S(2)}) collective-permute-start(bf16[256,2048]{1,0:T(8,128)(2,1)} %dynamic-slice_bitcast_fusion), channel_id=1, source_target_pairs={{0,4},{1,5},{2,6},{3,7},{4,0},{5,1},{6,2},{7,3},{8,12},{9,13},{10,... | collective-permute-start | bytes 3145736 | tf_op jit(solution)/shard_map/ppermute | solution.py:426
  642.7 46.1 %collective-permute-start.46 = (bf16[320,2048]{1,0:T(8,128)(2,1)}, bf16[320,2048]{1,0:T(8,128)(2,1)}, u32[]{:S(2)}, u32[]{:S(2)}) collective-permute-start(bf16[320,2048]{1,0:T(8,128)(2,1)} %get-tuple-element.208), channel_id=1, source_target_pairs={{0,2},{1,3},{8,10},{9,11},{16,18},{17,19},{24,26},{25,27}} | collective-permute-start | bytes 3932168 | tf_op jit(solution)/shard_map/ppermute | solution.py:426
  753.4 61.7 %collective-permute-start.55 = (bf16[320,2048]{1,0:T(8,128)(2,1)}, bf16[320,2048]{1,0:T(8,128)(2,1)}, u32[]{:S(2)}, u32[]{:S(2)}) collective-permute-start(bf16[320,2048]{1,0:T(8,128)(2,1)} %add_convert_fusion.1), channel_id=1, source_target_pairs={{0,2},{1,3},{2,4},{3,5},{4,6},{5,7},{8,10},{9,11},{10,12},{11,13},... | collective-permute-start | bytes 3932168 | tf_op jit(solution)/shard_map/ppermute | solution.py:426
  756.5 58.6 %collective-permute-start.56 = (bf16[320,2048]{1,0:T(8,128)(2,1)}, bf16[320,2048]{1,0:T(8,128)(2,1)}, u32[]{:S(2)}, u32[]{:S(2)}) collective-permute-start(bf16[320,2048]{1,0:T(8,128)(2,1)} %add_convert_fusion), channel_id=1, source_target_pairs={{2,0},{3,1},{4,2},{5,3},{6,4},{7,5},{10,8},{11,9},{12,10},{13,11},... | collective-permute-start | bytes 3932168 | tf_op jit(solution)/shard_map/ppermute | solution.py:426
  (125 other events, 2266.4 us)
Sparse Core Ops, SparseCore 0:
  9.9 55.3 all-gather.6
  72.7 42.6 all-gather.8
  133.3 57.1 all-gather.10
  193.4 56.3 all-gather.12
  278.1 54.6 all-gather.14
  360.6 53.8 all-gather.16
  417.6 88.2 reduce-scatter.4
  544.1 84.5 reduce-scatter.6
  631.6 52.6 reduce-scatter.8
  689.0 43.8 reduce-scatter.10

commit v5 on v4

--- a/solution.py
+++ b/solution.py
@@ -106,7 +106,10 @@
             tuple(jnp.full((1, BLOCK), NEGATIVE, F32) for h in range(heads)),
             tuple(jnp.zeros((1, BLOCK), F32) for h in range(heads)),
         )
-        tops, totals = lax.fori_loop(0, i + 1, key_block, start)
+        start = lax.fori_loop(
+            0, (i + 1) // 2, lambda j, inner: key_block(2 * j + 1, key_block(2 * j, inner)), start
+        )
+        tops, totals = lax.fori_loop((i + 1) // 2 * 2, i + 1, key_block, start)
         for h in range(heads):
             acc_s[span[h], :] = acc_s[span[h], :] / totals[h]
             lse_ref[h : h + 1, qs] = tops[h] + jnp.log(totals[h])
@@ -190,6 +193,8 @@
         do = do_s[qs, :]
         qh = [jnp.where(lane == h, q, jnp.zeros_like(q)) for h in range(heads)]
         doh = [jnp.where(lane == h, do, jnp.zeros_like(do)) for h in range(heads)]
+        qh_all = jnp.concatenate(qh, axis=0)
+        doh_all = jnp.concatenate(doh, axis=0)
         low = low_ref[:, qs]
         high = high_ref[:, qs]
         prod = do.astype(F32).T * ot_ref[:, qs]
@@ -207,10 +212,10 @@
             bias = jnp.where(block_mask(place_ref[ks, :], low, high), 0.0, NEGATIVE)
             s = [contract(k, qh[h], 1, 1) for h in range(heads)]
             dp = [contract(v, doh[h], 1, 1) for h in range(heads)]
-            p = [jnp.exp(s[h] + bias - lse[h]) for h in range(heads)]
+            p = [jnp.exp(s[h] + (bias - lse[h])) for h in range(heads)]
             ds = [(p[h] * (dp[h] - delta[h])).astype(BF16) for h in range(heads)]
-            dv = sum(contract(p[h].astype(BF16), doh[h], 1, 0) for h in range(heads))
-            dk = sum(contract(ds[h], qh[h], 1, 0) for h in range(heads))
+            dv = contract(jnp.concatenate([p[h].astype(BF16) for h in range(heads)], axis=1), doh_all, 1, 0)
+            dk = contract(jnp.concatenate(ds, axis=1), qh_all, 1, 0)
             for h in range(heads):
                 hs = slice(h * head_dim, (h + 1) * head_dim)
                 dqt_s[hs, :] += contract(kt_s[hs, ks], ds[h], 1, 0)
@@ -218,7 +223,10 @@
             dv_s[ks, :] += dv
             return inner
 
-        lax.fori_loop(0, i + 1, key_block, 0)
+        lax.fori_loop(
+            0, (i + 1) // 2, lambda j, inner: key_block(2 * j + 1, key_block(2 * j, inner)), 0
+        )
+        lax.fori_loop((i + 1) // 2 * 2, i + 1, key_block, 0)
         dq_s[qs, :] = (dqt_s[...] * scale).T.astype(BF16)
         return carry
 

time: 849 us -> 845 us (level)
  transfers between devices with their start and end apart: 74 -> 74, of which waited for: 26 -> 28; matrix products, arithmetic and copies ran while one was open for 35% -> 35% of each run, Pallas kernels for 20% -> 19%
where the time goes in v5:
time: 845 us; the launch traced here: 841 us
  waiting for transfers between devices  240 us (28%)
  Pallas kernels  159 us (19%)
  matrix products  126 us (15%)
  starting transfers between devices  111 us (13%)
  local copies, waits for them, and re-layouts  95.9 us (11%)
  other arithmetic  92.1 us (11%)
  between operations  16.6 us (2%)
    ppermute x63, waiting for transfers between devices, permute(): return lax.ppermute(array, pairs[0], pairs[1])  234 us
    dot_general x19, matrix products, contract(): lax.dot_general(left, right, (((left_dim,), (right_dim,)), ((), ())), pre...  126 us
    ppermute x63, starting transfers between devices, permute(): return lax.ppermute(array, pairs[0], pairs[1])  91.5 us
    pallas_call x1, Pallas kernels, attention_backward(): pl.pallas_call(functools.partial(backward_kernel, devices, pre, tok, head...  58.4 us
    pallas_call x1, Pallas kernels, attention_forward(): pl.pallas_call(functools.partial(forward_kernel, devices, pre, tok, heads...  39.5 us
    pallas_call x2, Pallas kernels, matmul_low(): pl.pallas_call(functools.partial(matmul_kernel, flipped), grid=(columns /...  23.5 us
    pallas_call x2, Pallas kernels, matmul_transposed(): pl.pallas_call(transposed_kernel, grid=(rows // step,), out_shape=jax.Sha...  22.9 us
  transfers between devices with their start and end apart: 74, of which 28 were waited for; matrix products, arithmetic and copies ran while one was open for 35% of the time, Pallas kernels for 19%

profile of v5, /device:TPU:0, one launch (start us, length us, event | category | flops | bytes accessed | tf_op | source)
XLA Modules:
  0.0 840.9 jit_solution(1740476802644542829)
XLA Ops:
  60.1 11.4 %collective-permute-done.9 = bf16[144,768]{1,0:T(8,128)(2,1)S(1)} collective-permute-done((bf16[144,768]{1,0:T(8,128)(2,1)S(1)}, bf16[144,768]{1,0:T(8,128)(2,1)S(1)}, u32[]{:S(2)}, u32[]{:S(2)}) %collective-permute-start.9) | collective-permute-done | bytes 221216 | tf_op jit(solution)/shard_map/ppermute | solution.py:434
  78.4 10.4 %collective-permute-done.13 = bf16[64,2048]{1,0:T(8,128)(2,1)S(1)} collective-permute-done((bf16[64,2048]{1,0:T(8,128)(2,1)}, bf16[64,2048]{1,0:T(8,128)(2,1)S(1)}, u32[]{:S(2)}, u32[]{:S(2)}) %collective-permute-start.13) | collective-permute-done | bytes 262176 | tf_op jit(solution)/shard_map/ppermute | solution.py:434
  105.3 22.2 %collective-permute-done.14 = bf16[320,2048]{1,0:T(8,128)(2,1)} collective-permute-done((bf16[320,2048]{1,0:T(8,128)(2,1)}, bf16[320,2048]{1,0:T(8,128)(2,1)}, u32[]{:S(2)}, u32[]{:S(2)}) %collective-permute-start.14) | collective-permute-done | bytes 1310752 | tf_op jit(solution)/shard_map/ppermute | solution.py:434
  135.4 24.2 %collective-permute-done.17 = bf16[320,2048]{1,0:T(8,128)(2,1)} collective-permute-done((bf16[320,2048]{1,0:T(8,128)(2,1)}, bf16[320,2048]{1,0:T(8,128)(2,1)}, u32[]{:S(2)}, u32[]{:S(2)}) %collective-permute-start.17) | collective-permute-done | bytes 1310752 | tf_op jit(solution)/shard_map/ppermute | solution.py:434
  170.9 7.0 fusion.17
  178.2 13.9 %collective-permute-done.20 = bf16[2,64,2048]{2,1,0:T(8,128)(2,1)S(1)} collective-permute-done((bf16[2,64,2048]{2,1,0:T(8,128)(2,1)S(1)}, bf16[2,64,2048]{2,1,0:T(8,128)(2,1)S(1)}, u32[]{:S(2)}, u32[]{:S(2)}) %collective-permute-start.20) | collective-permute-done | bytes 524320 | tf_op jit(solution)/shard_map/ppermute | solution.py:434
  193.2 12.6 %all-gather.15.cloned.1.call-start = ((), (), s32[]{:S(2)}) async-start(), calls=%async_computation.9 | async-start | bytes 5242880 | tf_op jit(solution)/shard_map/all_gather | solution.py:518
  235.3 39.5 %shard_map.339 = (bf16[2560,256]{1,0:T(8,128)(2,1)S(1)}, f32[256,2560]{1,0:T(8,128)}, f32[8,2560]{1,0:T(8,128)S(1)}) custom-call(s32[9]{0:T(128)S(1)} %stack.212.refs_0_, s32[2560,1]{1,0:T(8,128)} %broadcast_in_dim.171.refs_1_.refs_3_, s32[1,2560]{1,0:T(1,128)S(1)} %broadcast_in_dim.78.refs_2_.refs_4_, s32[1,2560]{1,0:T(1,128)S(1)} %broadcast_in_dim.79.refs_3_.refs_5_, ...), custom_call_target="tpu_custom_call" | custom-call | flops 13421772800 | bytes 7864320 | tf_op jit(solution)/shard_map/pallas_call | solution.py:131
  325.0 36.1 %collective-permute-done.32 = bf16[256,2048]{1,0:T(8,128)(2,1)} collective-permute-done((bf16[256,2048]{1,0:T(8,128)(2,1)}, bf16[256,2048]{1,0:T(8,128)(2,1)}, u32[]{:S(2)}, u32[]{:S(2)}) %collective-permute-start.32) | collective-permute-done | bytes 1048608 | tf_op jit(solution)/shard_map/ppermute | solution.py:434
  378.4 20.0 %multiply_convert_fusion = (bf16[1280,2048]{1,0:T(8,128)(2,1)S(1)}, f32[1280,2048]{1,0:T(8,128)}) fusion(f32[2048]{0:T(1024)S(1)} %bitcast.295, bf16[2048,2048]{1,0:T(8,128)(2,1)} %bitcast.59.right_ref, bf16[320,2048]{1,0:T(8,128)(2,1)} %collective-permute-done.29, bf16[320,2048]{1,0:T(8,128)(2,1)S(1)} %collective-permute-done.28, ...), kind=kOutput, calls=%fused_computation.8 | convolution fusion | flops 10774118400 | bytes 29368320 | tf_op jit(solution)/shard_map/dot_general | solution.py:22
  400.8 15.3 %convolution_convert_fusion = bf16[2048,2048]{1,0:T(8,128)(2,1)} fusion(bf16[1280,2048]{1,0:T(8,128)(2,1)S(1)} %get-tuple-element.168.left_ref, bf16[320,2048]{1,0:T(8,128)(2,1)} %collective-permute-done.31, bf16[320,2048]{1,0:T(8,128)(2,1)} %collective-permute-done.21, bf16[320,2048]{1,0:T(8,128)(2,1)} %collective-permute-done.30, ...), kind=kOutput, calls=%fused_computation.11 | convolution fusion | flops 10762584064 | bytes 18874368 | tf_op jit(solution)/shard_map/dot_general | solution.py:22
  421.0 19.7 %convert_reduce_fusion = (f32[2048]{0:T(1024)S(1)}, bf16[1280,2048]{1,0:T(8,128)(2,1)S(1)}) fusion(f32[1280,2048]{1,0:T(8,128)} %get-tuple-element.403, f32[2048]{0:T(1024)S(1)} %bitcast.296, bf16[1280,2048]{1,0:T(8,128)(2,1)} %pad_maximum_fusion, bf16[2048,2048]{1,0:T(8,128)(2,1)} %bitcast.246), kind=kOutput, calls=%fused_computation.7 | convolution fusion | flops 10771494912 | bytes 29376512 | tf_op jit(solution)/shard_map/dot_general | solution.py:22
  440.7 10.2 %convolution_convert_fusion.1 = bf16[640,2048]{1,0:T(8,128)(2,1)S(1)} fusion(bf16[2048,2048]{1,0:T(8,128)(2,1)} %bitcast.59.right_ref, bf16[1280,2048]{1,0:T(8,128)(2,1)S(1)} %get-tuple-element.181.right_ref), kind=kOutput, calls=%fused_computation.60 | convolution fusion | flops 5370019840 | bytes 13631488 | tf_op jit(solution)/shard_map/dot_general | solution.py:22
  455.3 8.3 shard_map.341
  463.6 15.2 %shard_map.340 = bf16[1280,2048]{1,0:T(8,128)(2,1)S(1)} custom-call(bf16[1280,2048]{1,0:T(8,128)(2,1)} %copy-done.28, bf16[2048,2048]{1,0:T(8,128)(2,1)} %bitcast.247), custom_call_target="tpu_custom_call" | custom-call | flops 1048576 | bytes 65536 | tf_op jit(solution)/shard_map/pallas_call | solution.py:292
  503.5 6.9 collective-permute-start.39
  516.9 7.0 shard_map.343
  528.6 16.0 %shard_map.342 = bf16[2048,2048]{1,0:T(8,128)(2,1)} custom-call(bf16[1280,2048]{1,0:T(8,128)(2,1)} %pad_maximum_fusion.1.left_ref, bf16[1280,2048]{1,0:T(8,128)(2,1)} %copy-done.23), custom_call_target="tpu_custom_call" | custom-call | flops 1048576 | bytes 65536 | tf_op jit(solution)/shard_map/pallas_call | solution.py:314
  548.3 58.4 %shard_map.344 = (bf16[2560,768]{1,0:T(8,128)(2,1)}, bf16[2560,768]{1,0:T(8,128)(2,1)}) custom-call(s32[9]{0:T(128)} %copy-done.3, f32[256,2560]{1,0:T(8,128)} %get-tuple-element.175.refs_1_, f32[8,2560]{1,0:T(8,128)} %copy-done.8, s32[2560,1]{1,0:T(8,128)} %broadcast_in_dim.171.refs_1_.refs_3_, s32[1,2560]{1,0:T(1,128)} %copy-done.2, s32[1,2560]{1,0:T(1,128)} %copy-done.1, ...), custom_call_target="tpu_custom_call" | custom-call | flops 18454937600 | bytes 13107200 | tf_op jit(solution)/shard_map/pallas_call | solution.py:267
  644.9 15.0 %shard_map.345 = bf16[2048,768]{1,0:T(8,128)(2,1)} custom-call(bf16[640,2048]{1,0:T(8,128)(2,1)} %fusion.29.refs_0_, bf16[640,2048]{1,0:T(8,128)(2,1)} %get-tuple-element.203.refs_1_, bf16[640,2048]{1,0:T(8,128)(2,1)} %get-tuple-element.204.refs_2_, bf16[640,2048]{1,0:T(8,128)(2,1)} %get-tuple-element.205.refs_3_, bf16[2560,768]{1,0:T(8,128)(2,1)} %get-tuple-element.209.refs_4_), custom_call_target="tpu_custom_call" | custom-call | flops 2013265920 | bytes 65536 | tf_op jit(solution)/shard_map/pallas_call | solution.py:340
  659.9 20.3 %collective-permute-done.48 = bf16[256,2048]{1,0:T(8,128)(2,1)} collective-permute-done((bf16[256,2048]{1,0:T(8,128)(2,1)}, bf16[256,2048]{1,0:T(8,128)(2,1)}, u32[]{:S(2)}, u32[]{:S(2)}) %collective-permute-start.48) | collective-permute-done | bytes 1048608 | tf_op jit(solution)/shard_map/ppermute | solution.py:434
  704.2 8.0 collective-permute-done.53
  718.9 19.5 %collective-permute-done.50 = bf16[320,2048]{1,0:T(8,128)(2,1)} collective-permute-done((bf16[320,2048]{1,0:T(8,128)(2,1)}, bf16[320,2048]{1,0:T(8,128)(2,1)}, u32[]{:S(2)}, u32[]{:S(2)}) %collective-permute-start.50) | collective-permute-done | bytes 1310752 | tf_op jit(solution)/shard_map/ppermute | solution.py:434
  771.6 20.1 %collective-permute-done.58 = bf16[2,64,768]{2,1,0:T(8,128)(2,1)S(1)} collective-permute-done((bf16[2,64,768]{2,1,0:T(8,128)(2,1)S(1)}, bf16[2,64,768]{2,1,0:T(8,128)(2,1)S(1)}, u32[]{:S(2)}, u32[]{:S(2)}) %collective-permute-start.58) | collective-permute-done | bytes 196640 | tf_op jit(solution)/shard_map/ppermute | solution.py:434
  (510 shorter events, 387.1 us)
Async XLA Ops:
  7.2 64.4 %all-gather.7.cloned.1.call-start = ((), (), s32[]{:S(2)}) async-start(), calls=%async_computation.5 | async-start | bytes 5242880 | tf_op jit(solution)/shard_map/all_gather | solution.py:518
  7.9 125.3 %all-gather.9.cloned.1.call-start = ((), (), s32[]{:S(2)}) async-start(), calls=%async_computation.6 | async-start | bytes 3932160 | tf_op jit(solution)/shard_map/all_gather | solution.py:518
  72.6 120.6 %all-gather.11.cloned.1.call-start = ((), (), s32[]{:S(2)}) async-start(), calls=%async_computation.7 | async-start | bytes 5242880 | tf_op jit(solution)/shard_map/all_gather | solution.py:518
  133.2 164.9 %all-gather.13.cloned.1.call-start = ((), (), s32[]{:S(2)}) async-start(), calls=%async_computation.8 | async-start | bytes 5242880 | tf_op jit(solution)/shard_map/all_gather | solution.py:518
  193.2 168.4 %all-gather.15.cloned.1.call-start = ((), (), s32[]{:S(2)}) async-start(), calls=%async_computation.9 | async-start | bytes 5242880 | tf_op jit(solution)/shard_map/all_gather | solution.py:518
  224.1 52.8 %collective-permute-start.21 = (bf16[320,2048]{1,0:T(8,128)(2,1)}, bf16[320,2048]{1,0:T(8,128)(2,1)}, u32[]{:S(2)}, u32[]{:S(2)}) collective-permute-start(bf16[320,2048]{1,0:T(8,128)(2,1)} %get-tuple-element.143), channel_id=1, source_target_pairs={{0,2},{1,3},{2,0},{3,1},{4,6},{5,7},{6,4},{7,5},{8,10},{9,11},{10,... | collective-permute-start | bytes 3932168 | tf_op jit(solution)/shard_map/ppermute | solution.py:434
  226.5 48.9 %collective-permute-start.22 = (bf16[256,2048]{1,0:T(8,128)(2,1)}, bf16[256,2048]{1,0:T(8,128)(2,1)}, u32[]{:S(2)}, u32[]{:S(2)}) collective-permute-start(bf16[256,2048]{1,0:T(8,128)(2,1)} %bitcast.122), channel_id=1, source_target_pairs={{0,4},{1,5},{2,6},{3,7},{4,0},{5,1},{6,2},{7,3},{8,12},{9,13},{10,... | collective-permute-start | bytes 3145736 | tf_op jit(solution)/shard_map/ppermute | solution.py:434
  277.0 139.2 %all-gather.17.cloned.1.call-start = ((), (), s32[]{:S(2)}) async-start(), calls=%async_computation.10 | async-start | bytes 5242880 | tf_op jit(solution)/shard_map/all_gather | solution.py:518
  307.8 53.3 %collective-permute-start.32 = (bf16[256,2048]{1,0:T(8,128)(2,1)}, bf16[256,2048]{1,0:T(8,128)(2,1)}, u32[]{:S(2)}, u32[]{:S(2)}) collective-permute-start(bf16[256,2048]{1,0:T(8,128)(2,1)} %param.36), channel_id=1, source_target_pairs={{0,4},{1,5},{2,6},{3,7},{4,0},{5,1},{6,2},{7,3},{8,12},{9,13},{10,... | collective-permute-start | bytes 3145736 | tf_op jit(solution)/shard_map/ppermute | solution.py:434
  320.5 52.5 %collective-permute-start.28 = (bf16[320,2048]{1,0:T(8,128)(2,1)S(1)}, bf16[320,2048]{1,0:T(8,128)(2,1)S(1)}, u32[]{:S(2)}, u32[]{:S(2)}) collective-permute-start(bf16[320,2048]{1,0:T(8,128)(2,1)S(1)} %add_convert_fusion.7), channel_id=1, source_target_pairs={{0,2},{1,3},{2,0},{3,1},{4,6},{5,7},{6,4},{7,5},{8,10},{9,11},{10,... | collective-permute-start | bytes 3932168 | tf_op jit(solution)/shard_map/ppermute | solution.py:434
  324.5 48.5 %collective-permute-start.30 = (bf16[320,2048]{1,0:T(8,128)(2,1)}, bf16[320,2048]{1,0:T(8,128)(2,1)}, u32[]{:S(2)}, u32[]{:S(2)}) collective-permute-start(bf16[320,2048]{1,0:T(8,128)(2,1)} %get-tuple-element.143), channel_id=1, source_target_pairs={{0,1},{1,0},{2,3},{3,2},{4,5},{5,4},{6,7},{7,6},{8,9},{9,8},{10,11... | collective-permute-start | bytes 3932168 | tf_op jit(solution)/shard_map/ppermute | solution.py:434
  324.5 48.5 %collective-permute-start.31 = (bf16[320,2048]{1,0:T(8,128)(2,1)}, bf16[320,2048]{1,0:T(8,128)(2,1)}, u32[]{:S(2)}, u32[]{:S(2)}) collective-permute-start(bf16[320,2048]{1,0:T(8,128)(2,1)} %collective-permute-done.21), channel_id=1, source_target_pairs={{0,1},{1,0},{2,3},{3,2},{4,5},{5,4},{6,7},{7,6},{8,9},{9,8},{10,11... | collective-permute-start | bytes 3932168 | tf_op jit(solution)/shard_map/ppermute | solution.py:434
  361.1 184.3 %reduce-scatter.5.cloned.1.call-start = ((), (), s32[]{:S(2)}) async-start(), calls=%async_computation.11 | async-start | bytes 10485760 | tf_op jit(solution)/shard_map/reduce_scatter | solution.py:521
  416.1 213.2 %reduce-scatter.7.cloned.1.call-start = ((), (), s32[]{:S(2)}) async-start(), calls=%async_computation.12 | async-start | bytes 10485760 | tf_op jit(solution)/shard_map/reduce_scatter | solution.py:521
  544.6 140.4 %reduce-scatter.9.cloned.1.call-start = ((), (), s32[]{:S(2)}) async-start(), calls=%async_computation.13 | async-start | bytes 5242880 | tf_op jit(solution)/shard_map/reduce_scatter | solution.py:521
  545.4 215.5 %reduce-scatter.11.cloned.1.call-start = ((), (), s32[]{:S(2)}) async-start(), calls=%async_computation.14 | async-start | bytes 3932160 | tf_op jit(solution)/shard_map/reduce_scatter | solution.py:521
  547.8 59.0 %collective-permute-start.41 = (bf16[256,2048]{1,0:T(8,128)(2,1)}, bf16[256,2048]{1,0:T(8,128)(2,1)}, u32[]{:S(2)}, u32[]{:S(2)}) collective-permute-start(bf16[256,2048]{1,0:T(8,128)(2,1)} %dynamic-slice_bitcast_fusion.1), channel_id=1, source_target_pairs={{0,4},{1,5},{2,6},{3,7},{4,0},{5,1},{6,2},{7,3},{8,12},{9,13},{10,... | collective-permute-start | bytes 3145736 | tf_op jit(solution)/shard_map/ppermute | solution.py:434
  547.8 62.1 %collective-permute-start.42 = (bf16[320,2048]{1,0:T(8,128)(2,1)}, bf16[320,2048]{1,0:T(8,128)(2,1)}, u32[]{:S(2)}, u32[]{:S(2)}) collective-permute-start(bf16[320,2048]{1,0:T(8,128)(2,1)} %add_convert_fusion.5), channel_id=1, source_target_pairs={{0,2},{1,3},{2,0},{3,1},{4,6},{5,7},{6,4},{7,5},{8,10},{9,11},{10,... | collective-permute-start | bytes 3932168 | tf_op jit(solution)/shard_map/ppermute | solution.py:434
  620.3 64.7 %collective-permute-start.49 = (bf16[320,2048]{1,0:T(8,128)(2,1)}, bf16[320,2048]{1,0:T(8,128)(2,1)}, u32[]{:S(2)}, u32[]{:S(2)}) collective-permute-start(bf16[320,2048]{1,0:T(8,128)(2,1)} %convolution_convert_fusion.2), channel_id=1, source_target_pairs={{0,1},{1,0},{2,3},{3,2},{4,5},{5,4},{6,7},{7,6},{8,9},{9,8},{10,11... | collective-permute-start | bytes 3932168 | tf_op jit(solution)/shard_map/ppermute | solution.py:434
  623.7 61.4 %collective-permute-start.43 = (bf16[320,2048]{1,0:T(8,128)(2,1)}, bf16[320,2048]{1,0:T(8,128)(2,1)}, u32[]{:S(2)}, u32[]{:S(2)}) collective-permute-start(bf16[320,2048]{1,0:T(8,128)(2,1)} %convolution_convert_fusion.5), channel_id=1, source_target_pairs={{0,1},{1,0},{2,3},{3,2},{4,5},{5,4},{6,7},{7,6},{8,9},{9,8},{10,11... | collective-permute-start | bytes 3932168 | tf_op jit(solution)/shard_map/ppermute | solution.py:434
  631.6 48.5 %collective-permute-start.48 = (bf16[256,2048]{1,0:T(8,128)(2,1)}, bf16[256,2048]{1,0:T(8,128)(2,1)}, u32[]{:S(2)}, u32[]{:S(2)}) collective-permute-start(bf16[256,2048]{1,0:T(8,128)(2,1)} %dynamic-slice_bitcast_fusion), channel_id=1, source_target_pairs={{0,4},{1,5},{2,6},{3,7},{4,0},{5,1},{6,2},{7,3},{8,12},{9,13},{10,... | collective-permute-start | bytes 3145736 | tf_op jit(solution)/shard_map/ppermute | solution.py:434
  638.7 46.4 %collective-permute-start.46 = (bf16[320,2048]{1,0:T(8,128)(2,1)}, bf16[320,2048]{1,0:T(8,128)(2,1)}, u32[]{:S(2)}, u32[]{:S(2)}) collective-permute-start(bf16[320,2048]{1,0:T(8,128)(2,1)} %get-tuple-element.208), channel_id=1, source_target_pairs={{0,2},{1,3},{8,10},{9,11},{16,18},{17,19},{24,26},{25,27}} | collective-permute-start | bytes 3932168 | tf_op jit(solution)/shard_map/ppermute | solution.py:434
  750.2 61.0 %collective-permute-start.55 = (bf16[320,2048]{1,0:T(8,128)(2,1)}, bf16[320,2048]{1,0:T(8,128)(2,1)}, u32[]{:S(2)}, u32[]{:S(2)}) collective-permute-start(bf16[320,2048]{1,0:T(8,128)(2,1)} %add_convert_fusion.1), channel_id=1, source_target_pairs={{0,2},{1,3},{2,4},{3,5},{4,6},{5,7},{8,10},{9,11},{10,12},{11,13},... | collective-permute-start | bytes 3932168 | tf_op jit(solution)/shard_map/ppermute | solution.py:434
  752.8 58.3 %collective-permute-start.56 = (bf16[320,2048]{1,0:T(8,128)(2,1)}, bf16[320,2048]{1,0:T(8,128)(2,1)}, u32[]{:S(2)}, u32[]{:S(2)}) collective-permute-start(bf16[320,2048]{1,0:T(8,128)(2,1)} %add_convert_fusion), channel_id=1, source_target_pairs={{2,0},{3,1},{4,2},{5,3},{6,4},{7,5},{10,8},{11,9},{12,10},{13,11},... | collective-permute-start | bytes 3932168 | tf_op jit(solution)/shard_map/ppermute | solution.py:434
  (125 other events, 2257.1 us)
Sparse Core Ops, SparseCore 0:
  9.9 55.3 all-gather.6
  72.7 42.6 all-gather.8
  133.3 57.1 all-gather.10
  193.4 56.3 all-gather.12
  277.1 56.3 all-gather.14
  361.2 53.8 all-gather.16
  418.2 88.2 reduce-scatter.4
  544.7 84.5 reduce-scatter.6
  632.3 52.6 reduce-scatter.8
  688.1 43.9 reduce-scatter.10

commit v6 on v5

--- a/solution.py
+++ b/solution.py
@@ -107,9 +107,9 @@
             tuple(jnp.zeros((1, BLOCK), F32) for h in range(heads)),
         )
         start = lax.fori_loop(
-            0, (i + 1) // 2, lambda j, inner: key_block(2 * j + 1, key_block(2 * j, inner)), start
-        )
-        tops, totals = lax.fori_loop((i + 1) // 2 * 2, i + 1, key_block, start)
+            0, (i + 1) // 4, lambda j, inner: key_block(4 * j + 3, key_block(4 * j + 2, key_block(4 * j + 1, key_block(4 * j, inner)))), start
+        )
+        tops, totals = lax.fori_loop((i + 1) // 4 * 4, i + 1, key_block, start)
         for h in range(heads):
             acc_s[span[h], :] = acc_s[span[h], :] / totals[h]
             lse_ref[h : h + 1, qs] = tops[h] + jnp.log(totals[h])
@@ -224,9 +224,9 @@
             return inner
 
         lax.fori_loop(
-            0, (i + 1) // 2, lambda j, inner: key_block(2 * j + 1, key_block(2 * j, inner)), 0
-        )
-        lax.fori_loop((i + 1) // 2 * 2, i + 1, key_block, 0)
+            0, (i + 1) // 4, lambda j, inner: key_block(4 * j + 3, key_block(4 * j + 2, key_block(4 * j + 1, key_block(4 * j, inner)))), 0
+        )
+        lax.fori_loop((i + 1) // 4 * 4, i + 1, key_block, 0)
         dq_s[qs, :] = (dqt_s[...] * scale).T.astype(BF16)
         return carry
 

time: 845 us -> 839 us (level)
  starting transfers between devices: 111 us -> 97.6 us
    all_gather x6, starting transfers between devices: 12.7 us -> 0.85 us  [batch_gather(): return lax.all_gather(array, 'batch', axis=0, tiled=True)]
  transfers between devices with their start and end apart: 74 -> 74, of which waited for: 28 -> 29; matrix products, arithmetic and copies ran while one was open for 35% -> 35% of each run, Pallas kernels for 19% -> 19%
where the time goes in v6:
time: 839 us; the launch traced here: 829 us
  waiting for transfers between devices  242 us (29%)
  Pallas kernels  158 us (19%)
  matrix products  126 us (15%)
  starting transfers between devices  97.6 us (12%)
  local copies, waits for them, and re-layouts  96.3 us (11%)
  other arithmetic  92.3 us (11%)
  between operations  16.8 us (2%)
    ppermute x63, waiting for transfers between devices, permute(): return lax.ppermute(array, pairs[0], pairs[1])  235 us
    dot_general x19, matrix products, contract(): lax.dot_general(left, right, (((left_dim,), (right_dim,)), ((), ())), pre...  126 us
    ppermute x63, starting transfers between devices, permute(): return lax.ppermute(array, pairs[0], pairs[1])  91 us
    pallas_call x1, Pallas kernels, attention_backward(): pl.pallas_call(functools.partial(backward_kernel, devices, pre, tok, head...  57.7 us
    pallas_call x1, Pallas kernels, attention_forward(): pl.pallas_call(functools.partial(forward_kernel, devices, pre, tok, heads...  38.8 us
    pallas_call x2, Pallas kernels, matmul_low(): pl.pallas_call(functools.partial(matmul_kernel, flipped), grid=(columns /...  23.5 us
    pallas_call x2, Pallas kernels, matmul_transposed(): pl.pallas_call(transposed_kernel, grid=(rows // step,), out_shape=jax.Sha...  22.9 us
  transfers between devices with their start and end apart: 74, of which 29 were waited for; matrix products, arithmetic and copies ran while one was open for 35% of the time, Pallas kernels for 19%

profile of v6, /device:TPU:0, one launch (start us, length us, event | category | flops | bytes accessed | tf_op | source)
XLA Modules:
  0.0 828.9 jit_solution(6143684317101764478)
XLA Ops:
  60.1 11.4 %collective-permute-done.9 = bf16[144,768]{1,0:T(8,128)(2,1)S(1)} collective-permute-done((bf16[144,768]{1,0:T(8,128)(2,1)S(1)}, bf16[144,768]{1,0:T(8,128)(2,1)S(1)}, u32[]{:S(2)}, u32[]{:S(2)}) %collective-permute-start.9) | collective-permute-done | bytes 221216 | tf_op jit(solution)/shard_map/ppermute | solution.py:434
  78.4 10.4 %collective-permute-done.13 = bf16[64,2048]{1,0:T(8,128)(2,1)S(1)} collective-permute-done((bf16[64,2048]{1,0:T(8,128)(2,1)}, bf16[64,2048]{1,0:T(8,128)(2,1)S(1)}, u32[]{:S(2)}, u32[]{:S(2)}) %collective-permute-start.13) | collective-permute-done | bytes 262176 | tf_op jit(solution)/shard_map/ppermute | solution.py:434
  105.3 22.2 %collective-permute-done.14 = bf16[320,2048]{1,0:T(8,128)(2,1)} collective-permute-done((bf16[320,2048]{1,0:T(8,128)(2,1)}, bf16[320,2048]{1,0:T(8,128)(2,1)}, u32[]{:S(2)}, u32[]{:S(2)}) %collective-permute-start.14) | collective-permute-done | bytes 1310752 | tf_op jit(solution)/shard_map/ppermute | solution.py:434
  135.4 24.2 %collective-permute-done.17 = bf16[320,2048]{1,0:T(8,128)(2,1)} collective-permute-done((bf16[320,2048]{1,0:T(8,128)(2,1)}, bf16[320,2048]{1,0:T(8,128)(2,1)}, u32[]{:S(2)}, u32[]{:S(2)}) %collective-permute-start.17) | collective-permute-done | bytes 1310752 | tf_op jit(solution)/shard_map/ppermute | solution.py:434
  170.9 7.0 fusion.17
  178.2 13.9 %collective-permute-done.20 = bf16[2,64,2048]{2,1,0:T(8,128)(2,1)S(1)} collective-permute-done((bf16[2,64,2048]{2,1,0:T(8,128)(2,1)S(1)}, bf16[2,64,2048]{2,1,0:T(8,128)(2,1)S(1)}, u32[]{:S(2)}, u32[]{:S(2)}) %collective-permute-start.20) | collective-permute-done | bytes 524320 | tf_op jit(solution)/shard_map/ppermute | solution.py:434
  223.0 38.8 %shard_map.339 = (bf16[2560,256]{1,0:T(8,128)(2,1)S(1)}, f32[256,2560]{1,0:T(8,128)}, f32[8,2560]{1,0:T(8,128)S(1)}) custom-call(s32[9]{0:T(128)S(1)} %stack.212.refs_0_, s32[2560,1]{1,0:T(8,128)} %broadcast_in_dim.171.refs_1_.refs_3_, s32[1,2560]{1,0:T(1,128)S(1)} %broadcast_in_dim.78.refs_2_.refs_4_, s32[1,2560]{1,0:T(1,128)S(1)} %broadcast_in_dim.79.refs_3_.refs_5_, ...), custom_call_target="tpu_custom_call" | custom-call | flops 13421772800 | bytes 7864320 | tf_op jit(solution)/shard_map/pallas_call | solution.py:131
  313.2 36.1 %collective-permute-done.32 = bf16[256,2048]{1,0:T(8,128)(2,1)} collective-permute-done((bf16[256,2048]{1,0:T(8,128)(2,1)}, bf16[256,2048]{1,0:T(8,128)(2,1)}, u32[]{:S(2)}, u32[]{:S(2)}) %collective-permute-start.32) | collective-permute-done | bytes 1048608 | tf_op jit(solution)/shard_map/ppermute | solution.py:434
  366.6 20.0 %multiply_convert_fusion = (bf16[1280,2048]{1,0:T(8,128)(2,1)S(1)}, f32[1280,2048]{1,0:T(8,128)}) fusion(f32[2048]{0:T(1024)S(1)} %bitcast.295, bf16[2048,2048]{1,0:T(8,128)(2,1)} %bitcast.59.right_ref, bf16[320,2048]{1,0:T(8,128)(2,1)} %collective-permute-done.29, bf16[320,2048]{1,0:T(8,128)(2,1)S(1)} %collective-permute-done.28, ...), kind=kOutput, calls=%fused_computation.8 | convolution fusion | flops 10774118400 | bytes 29368320 | tf_op jit(solution)/shard_map/dot_general | solution.py:22
  389.0 15.3 %convolution_convert_fusion = bf16[2048,2048]{1,0:T(8,128)(2,1)} fusion(bf16[1280,2048]{1,0:T(8,128)(2,1)S(1)} %get-tuple-element.168.left_ref, bf16[320,2048]{1,0:T(8,128)(2,1)} %collective-permute-done.31, bf16[320,2048]{1,0:T(8,128)(2,1)} %collective-permute-done.21, bf16[320,2048]{1,0:T(8,128)(2,1)} %collective-permute-done.30, ...), kind=kOutput, calls=%fused_computation.11 | convolution fusion | flops 10762584064 | bytes 18874368 | tf_op jit(solution)/shard_map/dot_general | solution.py:22
  409.2 19.8 %convert_reduce_fusion = (f32[2048]{0:T(1024)S(1)}, bf16[1280,2048]{1,0:T(8,128)(2,1)S(1)}) fusion(f32[1280,2048]{1,0:T(8,128)} %get-tuple-element.403, f32[2048]{0:T(1024)S(1)} %bitcast.296, bf16[1280,2048]{1,0:T(8,128)(2,1)} %pad_maximum_fusion, bf16[2048,2048]{1,0:T(8,128)(2,1)} %bitcast.246), kind=kOutput, calls=%fused_computation.7 | convolution fusion | flops 10771494912 | bytes 29376512 | tf_op jit(solution)/shard_map/dot_general | solution.py:22
  429.0 10.2 %convolution_convert_fusion.1 = bf16[640,2048]{1,0:T(8,128)(2,1)S(1)} fusion(bf16[2048,2048]{1,0:T(8,128)(2,1)} %bitcast.59.right_ref, bf16[1280,2048]{1,0:T(8,128)(2,1)S(1)} %get-tuple-element.181.right_ref), kind=kOutput, calls=%fused_computation.60 | convolution fusion | flops 5370019840 | bytes 13631488 | tf_op jit(solution)/shard_map/dot_general | solution.py:22
  443.6 8.3 shard_map.341
  451.9 15.2 %shard_map.340 = bf16[1280,2048]{1,0:T(8,128)(2,1)S(1)} custom-call(bf16[1280,2048]{1,0:T(8,128)(2,1)} %copy-done.28, bf16[2048,2048]{1,0:T(8,128)(2,1)} %bitcast.247), custom_call_target="tpu_custom_call" | custom-call | flops 1048576 | bytes 65536 | tf_op jit(solution)/shard_map/pallas_call | solution.py:292
  492.0 6.8 collective-permute-start.39
  505.2 7.0 shard_map.343
  516.9 16.0 %shard_map.342 = bf16[2048,2048]{1,0:T(8,128)(2,1)} custom-call(bf16[1280,2048]{1,0:T(8,128)(2,1)} %pad_maximum_fusion.1.left_ref, bf16[1280,2048]{1,0:T(8,128)(2,1)} %copy-done.23), custom_call_target="tpu_custom_call" | custom-call | flops 1048576 | bytes 65536 | tf_op jit(solution)/shard_map/pallas_call | solution.py:314
  536.6 57.7 %shard_map.344 = (bf16[2560,768]{1,0:T(8,128)(2,1)}, bf16[2560,768]{1,0:T(8,128)(2,1)}) custom-call(s32[9]{0:T(128)} %copy-done.3, f32[256,2560]{1,0:T(8,128)} %get-tuple-element.175.refs_1_, f32[8,2560]{1,0:T(8,128)} %copy-done.8, s32[2560,1]{1,0:T(8,128)} %broadcast_in_dim.171.refs_1_.refs_3_, s32[1,2560]{1,0:T(1,128)} %copy-done.2, s32[1,2560]{1,0:T(1,128)} %copy-done.1, ...), custom_call_target="tpu_custom_call" | custom-call | flops 18454937600 | bytes 13107200 | tf_op jit(solution)/shard_map/pallas_call | solution.py:267
  633.3 15.0 %shard_map.345 = bf16[2048,768]{1,0:T(8,128)(2,1)} custom-call(bf16[640,2048]{1,0:T(8,128)(2,1)} %fusion.29.refs_0_, bf16[640,2048]{1,0:T(8,128)(2,1)} %get-tuple-element.203.refs_1_, bf16[640,2048]{1,0:T(8,128)(2,1)} %get-tuple-element.204.refs_2_, bf16[640,2048]{1,0:T(8,128)(2,1)} %get-tuple-element.205.refs_3_, bf16[2560,768]{1,0:T(8,128)(2,1)} %get-tuple-element.209.refs_4_), custom_call_target="tpu_custom_call" | custom-call | flops 2013265920 | bytes 65536 | tf_op jit(solution)/shard_map/pallas_call | solution.py:340
  648.3 20.3 %collective-permute-done.48 = bf16[256,2048]{1,0:T(8,128)(2,1)} collective-permute-done((bf16[256,2048]{1,0:T(8,128)(2,1)}, bf16[256,2048]{1,0:T(8,128)(2,1)}, u32[]{:S(2)}, u32[]{:S(2)}) %collective-permute-start.48) | collective-permute-done | bytes 1048608 | tf_op jit(solution)/shard_map/ppermute | solution.py:434
  692.5 8.0 collective-permute-done.53
  707.2 19.4 %collective-permute-done.50 = bf16[320,2048]{1,0:T(8,128)(2,1)} collective-permute-done((bf16[320,2048]{1,0:T(8,128)(2,1)}, bf16[320,2048]{1,0:T(8,128)(2,1)}, u32[]{:S(2)}, u32[]{:S(2)}) %collective-permute-start.50) | collective-permute-done | bytes 1310752 | tf_op jit(solution)/shard_map/ppermute | solution.py:434
  759.9 20.1 %collective-permute-done.58 = bf16[2,64,768]{2,1,0:T(8,128)(2,1)S(1)} collective-permute-done((bf16[2,64,768]{2,1,0:T(8,128)(2,1)S(1)}, bf16[2,64,768]{2,1,0:T(8,128)(2,1)S(1)}, u32[]{:S(2)}, u32[]{:S(2)}) %collective-permute-start.58) | collective-permute-done | bytes 196640 | tf_op jit(solution)/shard_map/ppermute | solution.py:434
  799.5 6.7 fusion.51
  (510 shorter events, 382.2 us)
Async XLA Ops:
  7.2 64.4 %all-gather.7.cloned.1.call-start = ((), (), s32[]{:S(2)}) async-start(), calls=%async_computation.5 | async-start | bytes 5242880 | tf_op jit(solution)/shard_map/all_gather | solution.py:518
  7.9 125.3 %all-gather.9.cloned.1.call-start = ((), (), s32[]{:S(2)}) async-start(), calls=%async_computation.6 | async-start | bytes 3932160 | tf_op jit(solution)/shard_map/all_gather | solution.py:518
  72.6 120.6 %all-gather.11.cloned.1.call-start = ((), (), s32[]{:S(2)}) async-start(), calls=%async_computation.7 | async-start | bytes 5242880 | tf_op jit(solution)/shard_map/all_gather | solution.py:518
  133.2 153.2 %all-gather.13.cloned.1.call-start = ((), (), s32[]{:S(2)}) async-start(), calls=%async_computation.8 | async-start | bytes 5242880 | tf_op jit(solution)/shard_map/all_gather | solution.py:518
  193.2 156.4 %all-gather.15.cloned.1.call-start = ((), (), s32[]{:S(2)}) async-start(), calls=%async_computation.9 | async-start | bytes 5242880 | tf_op jit(solution)/shard_map/all_gather | solution.py:518
  211.9 52.8 %collective-permute-start.21 = (bf16[320,2048]{1,0:T(8,128)(2,1)}, bf16[320,2048]{1,0:T(8,128)(2,1)}, u32[]{:S(2)}, u32[]{:S(2)}) collective-permute-start(bf16[320,2048]{1,0:T(8,128)(2,1)} %get-tuple-element.143), channel_id=1, source_target_pairs={{0,2},{1,3},{2,0},{3,1},{4,6},{5,7},{6,4},{7,5},{8,10},{9,11},{10,... | collective-permute-start | bytes 3932168 | tf_op jit(solution)/shard_map/ppermute | solution.py:434
  214.2 48.6 %collective-permute-start.22 = (bf16[256,2048]{1,0:T(8,128)(2,1)}, bf16[256,2048]{1,0:T(8,128)(2,1)}, u32[]{:S(2)}, u32[]{:S(2)}) collective-permute-start(bf16[256,2048]{1,0:T(8,128)(2,1)} %bitcast.122), channel_id=1, source_target_pairs={{0,4},{1,5},{2,6},{3,7},{4,0},{5,1},{6,2},{7,3},{8,12},{9,13},{10,... | collective-permute-start | bytes 3145736 | tf_op jit(solution)/shard_map/ppermute | solution.py:434
  264.7 139.7 %all-gather.17.cloned.1.call-start = ((), (), s32[]{:S(2)}) async-start(), calls=%async_computation.10 | async-start | bytes 5242880 | tf_op jit(solution)/shard_map/all_gather | solution.py:518
  296.0 53.3 %collective-permute-start.32 = (bf16[256,2048]{1,0:T(8,128)(2,1)}, bf16[256,2048]{1,0:T(8,128)(2,1)}, u32[]{:S(2)}, u32[]{:S(2)}) collective-permute-start(bf16[256,2048]{1,0:T(8,128)(2,1)} %param.36), channel_id=1, source_target_pairs={{0,4},{1,5},{2,6},{3,7},{4,0},{5,1},{6,2},{7,3},{8,12},{9,13},{10,... | collective-permute-start | bytes 3145736 | tf_op jit(solution)/shard_map/ppermute | solution.py:434
  308.7 52.5 %collective-permute-start.28 = (bf16[320,2048]{1,0:T(8,128)(2,1)S(1)}, bf16[320,2048]{1,0:T(8,128)(2,1)S(1)}, u32[]{:S(2)}, u32[]{:S(2)}) collective-permute-start(bf16[320,2048]{1,0:T(8,128)(2,1)S(1)} %add_convert_fusion.7), channel_id=1, source_target_pairs={{0,2},{1,3},{2,0},{3,1},{4,6},{5,7},{6,4},{7,5},{8,10},{9,11},{10,... | collective-permute-start | bytes 3932168 | tf_op jit(solution)/shard_map/ppermute | solution.py:434
  312.7 48.5 %collective-permute-start.30 = (bf16[320,2048]{1,0:T(8,128)(2,1)}, bf16[320,2048]{1,0:T(8,128)(2,1)}, u32[]{:S(2)}, u32[]{:S(2)}) collective-permute-start(bf16[320,2048]{1,0:T(8,128)(2,1)} %get-tuple-element.143), channel_id=1, source_target_pairs={{0,1},{1,0},{2,3},{3,2},{4,5},{5,4},{6,7},{7,6},{8,9},{9,8},{10,11... | collective-permute-start | bytes 3932168 | tf_op jit(solution)/shard_map/ppermute | solution.py:434
  312.7 48.5 %collective-permute-start.31 = (bf16[320,2048]{1,0:T(8,128)(2,1)}, bf16[320,2048]{1,0:T(8,128)(2,1)}, u32[]{:S(2)}, u32[]{:S(2)}) collective-permute-start(bf16[320,2048]{1,0:T(8,128)(2,1)} %collective-permute-done.21), channel_id=1, source_target_pairs={{0,1},{1,0},{2,3},{3,2},{4,5},{5,4},{6,7},{7,6},{8,9},{9,8},{10,11... | collective-permute-start | bytes 3932168 | tf_op jit(solution)/shard_map/ppermute | solution.py:434
  349.3 184.4 %reduce-scatter.5.cloned.1.call-start = ((), (), s32[]{:S(2)}) async-start(), calls=%async_computation.11 | async-start | bytes 10485760 | tf_op jit(solution)/shard_map/reduce_scatter | solution.py:521
  404.4 213.4 %reduce-scatter.7.cloned.1.call-start = ((), (), s32[]{:S(2)}) async-start(), calls=%async_computation.12 | async-start | bytes 10485760 | tf_op jit(solution)/shard_map/reduce_scatter | solution.py:521
  532.9 140.6 %reduce-scatter.9.cloned.1.call-start = ((), (), s32[]{:S(2)}) async-start(), calls=%async_computation.13 | async-start | bytes 5242880 | tf_op jit(solution)/shard_map/reduce_scatter | solution.py:521
  533.7 215.7 %reduce-scatter.11.cloned.1.call-start = ((), (), s32[]{:S(2)}) async-start(), calls=%async_computation.14 | async-start | bytes 3932160 | tf_op jit(solution)/shard_map/reduce_scatter | solution.py:521
  536.1 58.3 %collective-permute-start.41 = (bf16[256,2048]{1,0:T(8,128)(2,1)}, bf16[256,2048]{1,0:T(8,128)(2,1)}, u32[]{:S(2)}, u32[]{:S(2)}) collective-permute-start(bf16[256,2048]{1,0:T(8,128)(2,1)} %dynamic-slice_bitcast_fusion.1), channel_id=1, source_target_pairs={{0,4},{1,5},{2,6},{3,7},{4,0},{5,1},{6,2},{7,3},{8,12},{9,13},{10,... | collective-permute-start | bytes 3145736 | tf_op jit(solution)/shard_map/ppermute | solution.py:434
  536.1 61.4 %collective-permute-start.42 = (bf16[320,2048]{1,0:T(8,128)(2,1)}, bf16[320,2048]{1,0:T(8,128)(2,1)}, u32[]{:S(2)}, u32[]{:S(2)}) collective-permute-start(bf16[320,2048]{1,0:T(8,128)(2,1)} %add_convert_fusion.5), channel_id=1, source_target_pairs={{0,2},{1,3},{2,0},{3,1},{4,6},{5,7},{6,4},{7,5},{8,10},{9,11},{10,... | collective-permute-start | bytes 3932168 | tf_op jit(solution)/shard_map/ppermute | solution.py:434
  607.9 65.6 %collective-permute-start.49 = (bf16[320,2048]{1,0:T(8,128)(2,1)}, bf16[320,2048]{1,0:T(8,128)(2,1)}, u32[]{:S(2)}, u32[]{:S(2)}) collective-permute-start(bf16[320,2048]{1,0:T(8,128)(2,1)} %convolution_convert_fusion.2), channel_id=1, source_target_pairs={{0,1},{1,0},{2,3},{3,2},{4,5},{5,4},{6,7},{7,6},{8,9},{9,8},{10,11... | collective-permute-start | bytes 3932168 | tf_op jit(solution)/shard_map/ppermute | solution.py:434
  611.3 62.2 %collective-permute-start.43 = (bf16[320,2048]{1,0:T(8,128)(2,1)}, bf16[320,2048]{1,0:T(8,128)(2,1)}, u32[]{:S(2)}, u32[]{:S(2)}) collective-permute-start(bf16[320,2048]{1,0:T(8,128)(2,1)} %convolution_convert_fusion.5), channel_id=1, source_target_pairs={{0,1},{1,0},{2,3},{3,2},{4,5},{5,4},{6,7},{7,6},{8,9},{9,8},{10,11... | collective-permute-start | bytes 3932168 | tf_op jit(solution)/shard_map/ppermute | solution.py:434
  620.1 48.5 %collective-permute-start.48 = (bf16[256,2048]{1,0:T(8,128)(2,1)}, bf16[256,2048]{1,0:T(8,128)(2,1)}, u32[]{:S(2)}, u32[]{:S(2)}) collective-permute-start(bf16[256,2048]{1,0:T(8,128)(2,1)} %dynamic-slice_bitcast_fusion), channel_id=1, source_target_pairs={{0,4},{1,5},{2,6},{3,7},{4,0},{5,1},{6,2},{7,3},{8,12},{9,13},{10,... | collective-permute-start | bytes 3145736 | tf_op jit(solution)/shard_map/ppermute | solution.py:434
  627.1 46.4 %collective-permute-start.46 = (bf16[320,2048]{1,0:T(8,128)(2,1)}, bf16[320,2048]{1,0:T(8,128)(2,1)}, u32[]{:S(2)}, u32[]{:S(2)}) collective-permute-start(bf16[320,2048]{1,0:T(8,128)(2,1)} %get-tuple-element.208), channel_id=1, source_target_pairs={{0,2},{1,3},{8,10},{9,11},{16,18},{17,19},{24,26},{25,27}} | collective-permute-start | bytes 3932168 | tf_op jit(solution)/shard_map/ppermute | solution.py:434
  738.6 60.9 %collective-permute-start.55 = (bf16[320,2048]{1,0:T(8,128)(2,1)}, bf16[320,2048]{1,0:T(8,128)(2,1)}, u32[]{:S(2)}, u32[]{:S(2)}) collective-permute-start(bf16[320,2048]{1,0:T(8,128)(2,1)} %add_convert_fusion.1), channel_id=1, source_target_pairs={{0,2},{1,3},{2,4},{3,5},{4,6},{5,7},{8,10},{9,11},{10,12},{11,13},... | collective-permute-start | bytes 3932168 | tf_op jit(solution)/shard_map/ppermute | solution.py:434
  741.3 58.2 %collective-permute-start.56 = (bf16[320,2048]{1,0:T(8,128)(2,1)}, bf16[320,2048]{1,0:T(8,128)(2,1)}, u32[]{:S(2)}, u32[]{:S(2)}) collective-permute-start(bf16[320,2048]{1,0:T(8,128)(2,1)} %add_convert_fusion), channel_id=1, source_target_pairs={{2,0},{3,1},{4,2},{5,3},{6,4},{7,5},{10,8},{11,9},{12,10},{13,11},... | collective-permute-start | bytes 3932168 | tf_op jit(solution)/shard_map/ppermute | solution.py:434
  (125 other events, 2205.7 us)
Sparse Core Ops, SparseCore 0:
  9.9 55.3 all-gather.6
  72.7 42.6 all-gather.8
  133.3 57.1 all-gather.10
  193.4 56.3 all-gather.12
  264.9 56.2 all-gather.14
  349.4 53.9 all-gather.16
  406.5 88.2 reduce-scatter.4
  533.0 84.6 reduce-scatter.6
  620.8 52.6 reduce-scatter.8
  676.6 43.8 reduce-scatter.10
